TPU v7x, 256 devices: a whole 4x4x8 slice. The times are simulated.
256 devices in a mesh: row: 8 (over y_lo, x), col: 32 (over y_hi, z, core).
Axes of the slice: x: 4, y: 4 (y_hi: 2, y_lo: 2; y = y_hi * 2 + y_lo), z: 8, core: 2. Of those that a mesh axis runs over, the one named last changes fastest.
Arguments:
- features: bfloat16 [64, 65536], P(None, ('col', 'row')), may hold values from -4.5 to 4.5
- groups: int32 [65536], P(('col', 'row')), may hold values from 0 to 7
- targets: float32 [32, 65536], P(None, ('col', 'row')), may hold values from -7.5 to 7.5
- start: float32 [32, 65536], P(None, ('col', 'row')), may hold values from -3 to 3
Outputs:
- solution: float32 [32, 65536], P(None, ('col', 'row'))
- residual: float32 [32, 65536], P(None, ('col', 'row'))
- direction: float32 [32, 65536], P(None, ('col', 'row'))
All inputs are finite; a program needn't handle non-finite values.
Results may differ from a plain program's by a relative error of at most 0.0032.
Values may be sent and summed in bfloat16 or wider, within the bound.
No kernel may reach another device: no remote copies, remote signals or barrier semaphores. Data moves between devices by JAX's collectives and lax.ppermute only.
A program may use at most 64 MiB of HBM per device.

v0:
```python
import math

import jax
import jax.numpy as jnp
from jax import lax
from jax.sharding import PartitionSpec as P

RHO = 0.2
NOISE = 1.0
AMP_NUM = 16.0


def from_behind(value, axis, steps):
    count = lax.axis_size(axis)
    pairs = [(source, (source + steps) % count) for source in range(count)]
    return lax.ppermute(value, axis, pairs)


def squares_of(values):
    wide = values.astype(jnp.float32)
    return jnp.sum(wide * wide, axis=0)


def kernel_tile(home_features, home_squares, home_groups, piece_features, piece_groups, amplitude):
    piece_squares = squares_of(piece_features)
    cross = lax.dot_general(
        home_features, piece_features, (((0,), (0,)), ((), ())), preferred_element_type=jnp.float32
    )
    distance = home_squares[:, None] + piece_squares[None, :] - 2.0 * cross
    same = (home_groups[:, None] == piece_groups[None, :]).astype(jnp.float32)
    width = home_features.shape[0]
    return (amplitude * jnp.exp(-distance / width) * (RHO + (1.0 - RHO) * same)).astype(
        jnp.bfloat16
    )


def rows_product(piece_vector, tile):
    return lax.dot_general(
        piece_vector, tile, (((1,), (1,)), ((), ())), preferred_element_type=jnp.float32
    )


def columns_product(home_vector, tile):
    return jnp.dot(home_vector, tile, preferred_element_type=jnp.float32)


def per_device(features, groups, targets, start):
    points = features.shape[1]
    halfway = lax.axis_size("col") // 2
    amplitude = AMP_NUM / math.sqrt(points * lax.axis_size("row") * lax.axis_size("col"))
    home_features, home_groups = (
        lax.all_gather(features, "row", axis=1, tiled=True),
        lax.all_gather(groups, "row", axis=0, tiled=True),
    )
    home_squares = squares_of(home_features)

    def tile_with(piece_features, piece_groups):
        return kernel_tile(
            home_features, home_squares, home_groups, piece_features, piece_groups, amplitude
        )

    def apply_operator(vector):
        rounded = vector.astype(jnp.bfloat16)
        home_vector = lax.all_gather(rounded, "row", axis=1, tiled=True)
        partial_value = rows_product(rounded, tile_with(features, groups))
        empty = jnp.zeros(vector.shape, jnp.float32)

        def visit(step, carried):
            piece_features, piece_groups, piece_vector, collected, partial_value = carried
            piece_features, piece_groups, piece_vector = from_behind(
                (piece_features, piece_groups, piece_vector), "col", 1
            )
            collected = from_behind(collected, "col", 1)
            tile = tile_with(piece_features, piece_groups)
            collected = collected + columns_product(home_vector, tile)
            partial_value = partial_value + rows_product(piece_vector, tile)
            return (piece_features, piece_groups, piece_vector, collected, partial_value)

        piece_features, piece_groups, piece_vector, collected, partial_value = lax.fori_loop(
            1, halfway, visit, (features, groups, rounded, empty, partial_value)
        )
        returned = from_behind(collected, "col", 1 - halfway)
        piece_features, piece_groups, piece_vector = from_behind(
            (piece_features, piece_groups, piece_vector), "col", 1
        )
        partial_value = partial_value + rows_product(
            piece_vector, tile_with(piece_features, piece_groups)
        )
        return (
            NOISE * vector
            + lax.psum_scatter(partial_value, "row", scatter_dimension=1, tiled=True)
            + returned
        )

    residual0 = targets - apply_operator(start)
    norm_old = lax.psum(jnp.sum(residual0 * residual0, axis=1), ("row", "col"))
    image = apply_operator(residual0)
    curvature = lax.psum(jnp.sum(residual0 * image, axis=1), ("row", "col"))
    alpha = norm_old / curvature
    solution = start + alpha[:, None] * residual0
    residual = residual0 - alpha[:, None] * image
    norm_new = lax.psum(jnp.sum(residual * residual, axis=1), ("row", "col"))
    direction = residual + (norm_new / norm_old)[:, None] * residual0
    return (solution, residual, direction)


def solution(mesh):
    in_specs = (
        P(None, ("col", "row")),
        P(("col", "row")),
        P(None, ("col", "row")),
        P(None, ("col", "row")),
    )
    out_specs = (P(None, ("col", "row")), P(None, ("col", "row")), P(None, ("col", "row")))
    return jax.shard_map(
        per_device, mesh=mesh, in_specs=in_specs, out_specs=out_specs, check_vma=False
    )
```

profile of v0, /device:TPU:1, one launch (start us, length us, event | category | flops | bytes accessed | tf_op | source)
XLA Modules:
  0.0 640.3 jit_solution(12578731523250859715)
XLA Ops:
  8.6 23.3 %all_gather.12 = bf16[64,2048]{1,0:T(8,128)(2,1)S(1)} all-gather(bf16[64,256]{1,0:T(8,128)(2,1)S(1)} %copy.45), channel_id=1, replica_groups=mesh['row'=8,'col'=32] {'row'}, dimensions={1}, use_global_device_ids=true | all-gather | bytes 294912 | tf_op jit(solution)/shard_map/all_gather | solution.py:52
  32.1 14.9 %all-gather = s32[8,1,256]{2,1,0:T(1,128)S(1)} all-gather(s32[1,1,256]{2,1,0:T(1,128)S(1)} %bitcast.88), channel_id=1, replica_groups=mesh['row'=8,'col'=32] {'row'}, dimensions={0}, use_global_device_ids=true | all-gather | bytes 9216 | tf_op jit(solution)/shard_map/all_gather | solution.py:53
  47.8 22.0 %all_gather.14 = bf16[32,2048]{1,0:T(8,128)(2,1)S(1)} all-gather(bf16[32,256]{1,0:T(8,128)(2,1)S(1)} %convert_element_type.47), channel_id=1, replica_groups=mesh['row'=8,'col'=32] {'row'}, dimensions={1}, use_global_device_ids=true | all-gather | bytes 147456 | tf_op jit(solution)/shard_map/all_gather | solution.py:64
  71.5 150.0 %while.38 = (s32[]{:T(128)}, bf16[64,256]{1,0:T(8,128)(2,1)S(1)}, s32[256]{0:T(256)S(1)}, bf16[32,256]{1,0:T(8,128)(2,1)S(1)}, f32[32,256]{1,0:T(8,128)S(1)}, /*...) while((s32[]{:T(128)}, bf16[64,256]{1,0:T(8,128)(2,1)S(1)}, ...), condition=%wide.region_4.0_spmd.clone, body=%wide.region_2.0_spmd.clone.sunk | while | flops 140115712 | bytes 4728095 | solution.py:79
  71.5 18.2 %collective-permute-start = (bf16[64,256]{1,0:T(8,128)(2,1)S(1)}, bf16[64,256]{1,0:T(8,128)(2,1)S(1)}, u32[]{:S(2)}, u32[]{:S(2)}) collective-permute-start(bf16[64,256]{1,0:T(8,128)(2,1)S(1)} %get-tuple-element.375), channel_id=1, source_target_pairs={{0,1},{1,2},{2,3},{3,4},{4,5},{5,6},{6,7},{7,8},{8,9},{9,10},{10,1... | collective-permute-start | bytes 98312 | tf_op jit(solution)/shard_map/while/body/eval_jaxpr/ppermute | solution.py:16
  94.5 2.4 collective-permute-start
  97.0 2.1 collective-permute-start.2
  101.9 2.4 collective-permute-start
  105.1 2.3 collective-permute-start.2
  112.7 2.3 collective-permute-start.2
  115.1 3.0 collective-permute-done.1
  121.9 5.5 collective-permute-done.1
  129.8 6.7 %collective-permute-done.1 = s32[256]{0:T(256)S(1)} collective-permute-done((s32[256]{0:T(256)S(1)}, s32[256]{0:T(256)S(1)}, u32[]{:S(2)}, u32[]{:S(2)}) %collective-permute-start.1) | collective-permute-done | bytes 1056 | tf_op jit(solution)/shard_map/while/body/eval_jaxpr/ppermute | solution.py:16
  139.0 6.7 %collective-permute-done.1 = s32[256]{0:T(256)S(1)} collective-permute-done((s32[256]{0:T(256)S(1)}, s32[256]{0:T(256)S(1)}, u32[]{:S(2)}, u32[]{:S(2)}) %collective-permute-start.1) | collective-permute-done | bytes 1056 | tf_op jit(solution)/shard_map/while/body/eval_jaxpr/ppermute | solution.py:16
  148.2 6.7 %collective-permute-done.1 = s32[256]{0:T(256)S(1)} collective-permute-done((s32[256]{0:T(256)S(1)}, s32[256]{0:T(256)S(1)}, u32[]{:S(2)}, u32[]{:S(2)}) %collective-permute-start.1) | collective-permute-done | bytes 1056 | tf_op jit(solution)/shard_map/while/body/eval_jaxpr/ppermute | solution.py:16
  157.4 6.7 %collective-permute-done.1 = s32[256]{0:T(256)S(1)} collective-permute-done((s32[256]{0:T(256)S(1)}, s32[256]{0:T(256)S(1)}, u32[]{:S(2)}, u32[]{:S(2)}) %collective-permute-start.1) | collective-permute-done | bytes 1056 | tf_op jit(solution)/shard_map/while/body/eval_jaxpr/ppermute | solution.py:16
  166.6 6.7 %collective-permute-done.1 = s32[256]{0:T(256)S(1)} collective-permute-done((s32[256]{0:T(256)S(1)}, s32[256]{0:T(256)S(1)}, u32[]{:S(2)}, u32[]{:S(2)}) %collective-permute-start.1) | collective-permute-done | bytes 1056 | tf_op jit(solution)/shard_map/while/body/eval_jaxpr/ppermute | solution.py:16
  175.8 6.7 %collective-permute-done.1 = s32[256]{0:T(256)S(1)} collective-permute-done((s32[256]{0:T(256)S(1)}, s32[256]{0:T(256)S(1)}, u32[]{:S(2)}, u32[]{:S(2)}) %collective-permute-start.1) | collective-permute-done | bytes 1056 | tf_op jit(solution)/shard_map/while/body/eval_jaxpr/ppermute | solution.py:16
  185.0 6.7 %collective-permute-done.1 = s32[256]{0:T(256)S(1)} collective-permute-done((s32[256]{0:T(256)S(1)}, s32[256]{0:T(256)S(1)}, u32[]{:S(2)}, u32[]{:S(2)}) %collective-permute-start.1) | collective-permute-done | bytes 1056 | tf_op jit(solution)/shard_map/while/body/eval_jaxpr/ppermute | solution.py:16
  194.3 6.7 %collective-permute-done.1 = s32[256]{0:T(256)S(1)} collective-permute-done((s32[256]{0:T(256)S(1)}, s32[256]{0:T(256)S(1)}, u32[]{:S(2)}, u32[]{:S(2)}) %collective-permute-start.1) | collective-permute-done | bytes 1056 | tf_op jit(solution)/shard_map/while/body/eval_jaxpr/ppermute | solution.py:16
  203.5 6.7 %collective-permute-done.1 = s32[256]{0:T(256)S(1)} collective-permute-done((s32[256]{0:T(256)S(1)}, s32[256]{0:T(256)S(1)}, u32[]{:S(2)}, u32[]{:S(2)}) %collective-permute-start.1) | collective-permute-done | bytes 1056 | tf_op jit(solution)/shard_map/while/body/eval_jaxpr/ppermute | solution.py:16
  212.7 6.7 %collective-permute-done.1 = s32[256]{0:T(256)S(1)} collective-permute-done((s32[256]{0:T(256)S(1)}, s32[256]{0:T(256)S(1)}, u32[]{:S(2)}, u32[]{:S(2)}) %collective-permute-start.1) | collective-permute-done | bytes 1056 | tf_op jit(solution)/shard_map/while/body/eval_jaxpr/ppermute | solution.py:16
  221.8 6.8 %collective-permute-done.9 = bf16[64,256]{1,0:T(8,128)(2,1)S(1)} collective-permute-done((bf16[64,256]{1,0:T(8,128)(2,1)S(1)}, bf16[64,256]{1,0:T(8,128)(2,1)S(1)}, u32[]{:S(2)}, u32[]{:S(2)}) %collective-permute-start.9) | collective-permute-done | bytes 32800 | tf_op jit(solution)/shard_map/ppermute | solution.py:16
  230.7 10.4 %collective-permute-done.11 = f32[32,256]{1,0:T(8,128)S(1)} collective-permute-done((f32[32,256]{1,0:T(8,128)S(1)}, f32[32,256]{1,0:T(8,128)S(1)}, u32[]{:S(2)}, u32[]{:S(2)}) %collective-permute-start.11) | collective-permute-done | bytes 32800 | tf_op jit(solution)/shard_map/ppermute | solution.py:16
  241.2 23.4 %reduce-scatter.3.cloned.1.call-done = f32[32,256]{1,0:T(8,128)} async-done(((f32[32,2048]{1,0:T(8,128)}), f32[32,256]{1,0:T(8,128)}) %reduce-scatter.3.cloned.1.call-update) | async-done | bytes 32784 | tf_op jit(solution)/shard_map/reduce_scatter | solution.py:91
  265.7 22.0 %all_gather.15 = bf16[32,2048]{1,0:T(8,128)(2,1)S(1)} all-gather(bf16[32,256]{1,0:T(8,128)(2,1)S(1)} %get-tuple-element.401), channel_id=1, replica_groups=mesh['row'=8,'col'=32] {'row'}, dimensions={1}, use_global_device_ids=true | all-gather | bytes 147456 | tf_op jit(solution)/shard_map/all_gather | solution.py:64
  287.7 145.5 %while.39 = (s32[]{:T(128)}, bf16[64,256]{1,0:T(8,128)(2,1)S(1)}, s32[256]{0:T(256)S(1)}, bf16[32,256]{1,0:T(8,128)(2,1)S(1)}, f32[32,256]{1,0:T(8,128)S(1)}, /*...) while((s32[]{:T(128)}, bf16[64,256]{1,0:T(8,128)(2,1)S(1)}, ...), condition=%wide.region_11.12_spmd.clone, body=%wide.region_9.11_spmd.clone.sunk | while | flops 140115712 | bytes 4728095 | solution.py:79
  287.7 13.7 %collective-permute-start.4 = (bf16[64,256]{1,0:T(8,128)(2,1)S(1)}, bf16[64,256]{1,0:T(8,128)(2,1)S(1)}, u32[]{:S(2)}, u32[]{:S(2)}) collective-permute-start(bf16[64,256]{1,0:T(8,128)(2,1)S(1)} %get-tuple-element.411), channel_id=1, source_target_pairs={{0,1},{1,2},{2,3},{3,4},{4,5},{5,6},{6,7},{7,8},{8,9},{9,10},{10,1... | collective-permute-start | bytes 98312 | tf_op jit(solution)/shard_map/while/body/eval_jaxpr/ppermute | solution.py:16
  305.9 2.4 collective-permute-start.4
  315.8 2.3 collective-permute-start.6
  318.2 2.5 collective-permute-done.5
  325.4 4.5 collective-permute-done.5
  332.4 6.7 %collective-permute-done.5 = s32[256]{0:T(256)S(1)} collective-permute-done((s32[256]{0:T(256)S(1)}, s32[256]{0:T(256)S(1)}, u32[]{:S(2)}, u32[]{:S(2)}) %collective-permute-start.5) | collective-permute-done | bytes 1056 | tf_op jit(solution)/shard_map/while/body/eval_jaxpr/ppermute | solution.py:16
  341.6 6.7 %collective-permute-done.5 = s32[256]{0:T(256)S(1)} collective-permute-done((s32[256]{0:T(256)S(1)}, s32[256]{0:T(256)S(1)}, u32[]{:S(2)}, u32[]{:S(2)}) %collective-permute-start.5) | collective-permute-done | bytes 1056 | tf_op jit(solution)/shard_map/while/body/eval_jaxpr/ppermute | solution.py:16
  350.8 6.7 %collective-permute-done.5 = s32[256]{0:T(256)S(1)} collective-permute-done((s32[256]{0:T(256)S(1)}, s32[256]{0:T(256)S(1)}, u32[]{:S(2)}, u32[]{:S(2)}) %collective-permute-start.5) | collective-permute-done | bytes 1056 | tf_op jit(solution)/shard_map/while/body/eval_jaxpr/ppermute | solution.py:16
  360.0 6.7 %collective-permute-done.5 = s32[256]{0:T(256)S(1)} collective-permute-done((s32[256]{0:T(256)S(1)}, s32[256]{0:T(256)S(1)}, u32[]{:S(2)}, u32[]{:S(2)}) %collective-permute-start.5) | collective-permute-done | bytes 1056 | tf_op jit(solution)/shard_map/while/body/eval_jaxpr/ppermute | solution.py:16
  369.2 6.7 %collective-permute-done.5 = s32[256]{0:T(256)S(1)} collective-permute-done((s32[256]{0:T(256)S(1)}, s32[256]{0:T(256)S(1)}, u32[]{:S(2)}, u32[]{:S(2)}) %collective-permute-start.5) | collective-permute-done | bytes 1056 | tf_op jit(solution)/shard_map/while/body/eval_jaxpr/ppermute | solution.py:16
  378.4 6.7 %collective-permute-done.5 = s32[256]{0:T(256)S(1)} collective-permute-done((s32[256]{0:T(256)S(1)}, s32[256]{0:T(256)S(1)}, u32[]{:S(2)}, u32[]{:S(2)}) %collective-permute-start.5) | collective-permute-done | bytes 1056 | tf_op jit(solution)/shard_map/while/body/eval_jaxpr/ppermute | solution.py:16
  387.6 6.7 %collective-permute-done.5 = s32[256]{0:T(256)S(1)} collective-permute-done((s32[256]{0:T(256)S(1)}, s32[256]{0:T(256)S(1)}, u32[]{:S(2)}, u32[]{:S(2)}) %collective-permute-start.5) | collective-permute-done | bytes 1056 | tf_op jit(solution)/shard_map/while/body/eval_jaxpr/ppermute | solution.py:16
  396.8 6.7 %collective-permute-done.5 = s32[256]{0:T(256)S(1)} collective-permute-done((s32[256]{0:T(256)S(1)}, s32[256]{0:T(256)S(1)}, u32[]{:S(2)}, u32[]{:S(2)}) %collective-permute-start.5) | collective-permute-done | bytes 1056 | tf_op jit(solution)/shard_map/while/body/eval_jaxpr/ppermute | solution.py:16
  406.0 6.7 %collective-permute-done.5 = s32[256]{0:T(256)S(1)} collective-permute-done((s32[256]{0:T(256)S(1)}, s32[256]{0:T(256)S(1)}, u32[]{:S(2)}, u32[]{:S(2)}) %collective-permute-start.5) | collective-permute-done | bytes 1056 | tf_op jit(solution)/shard_map/while/body/eval_jaxpr/ppermute | solution.py:16
  415.2 6.7 %collective-permute-done.5 = s32[256]{0:T(256)S(1)} collective-permute-done((s32[256]{0:T(256)S(1)}, s32[256]{0:T(256)S(1)}, u32[]{:S(2)}, u32[]{:S(2)}) %collective-permute-start.5) | collective-permute-done | bytes 1056 | tf_op jit(solution)/shard_map/while/body/eval_jaxpr/ppermute | solution.py:16
  424.4 6.7 %collective-permute-done.5 = s32[256]{0:T(256)S(1)} collective-permute-done((s32[256]{0:T(256)S(1)}, s32[256]{0:T(256)S(1)}, u32[]{:S(2)}, u32[]{:S(2)}) %collective-permute-start.5) | collective-permute-done | bytes 1056 | tf_op jit(solution)/shard_map/while/body/eval_jaxpr/ppermute | solution.py:16
  433.5 6.8 %collective-permute-done.13 = bf16[64,256]{1,0:T(8,128)(2,1)S(1)} collective-permute-done((bf16[64,256]{1,0:T(8,128)(2,1)S(1)}, bf16[64,256]{1,0:T(8,128)(2,1)S(1)}, u32[]{:S(2)}, u32[]{:S(2)}) %collective-permute-start.13) | collective-permute-done | bytes 32800 | tf_op jit(solution)/shard_map/ppermute | solution.py:16
  442.4 10.3 %collective-permute-done.15 = f32[32,256]{1,0:T(8,128)S(1)} collective-permute-done((f32[32,256]{1,0:T(8,128)S(1)}, f32[32,256]{1,0:T(8,128)S(1)}, u32[]{:S(2)}, u32[]{:S(2)}) %collective-permute-start.15) | collective-permute-done | bytes 32800 | tf_op jit(solution)/shard_map/ppermute | solution.py:16
  452.7 23.4 %reduce-scatter.5.cloned.1.call-done = f32[32,256]{1,0:T(8,128)} async-done(((f32[32,2048]{1,0:T(8,128)}), f32[32,256]{1,0:T(8,128)}) %reduce-scatter.5.cloned.1.call-update) | async-done | bytes 32784 | tf_op jit(solution)/shard_map/reduce_scatter | solution.py:91
  477.0 80.9 %all-reduce = (f32[32]{0:T(128)S(1)}, f32[32]{0:T(128)S(1)}) all-reduce(f32[32]{0:T(128)S(1)} %get-tuple-element.192, f32[32]{0:T(128)S(1)} %get-tuple-element.191), channel_id=1, replica_groups=mesh['row'=8,'col'=32] {'row','col'}, use_global_device_ids=true, to_apply=%region_8.0 | all-reduce | flops 64 | bytes 512 | tf_op jit(solution)/shard_map/psum | solution.py:96
  559.5 73.3 %psum.23 = f32[32]{0:T(128)S(1)} all-reduce(f32[32]{0:T(128)S(1)} %get-tuple-element.235), channel_id=1, replica_groups=mesh['row'=8,'col'=32] {'row','col'}, use_global_device_ids=true, to_apply=%region_17.0 | all-reduce | flops 32 | bytes 256 | tf_op jit(solution)/shard_map/psum | solution.py:102
  (490 shorter events, 102.3 us)
Async XLA Ops:
  7.2 257.4 %reduce-scatter.3.cloned.1.call-start = ((), (), s32[]{:S(2)}) async-start(), calls=%async_computation.2 | async-start | bytes 294912 | tf_op jit(solution)/shard_map/reduce_scatter | solution.py:91
  71.5 21.1 %collective-permute-start = (bf16[64,256]{1,0:T(8,128)(2,1)S(1)}, bf16[64,256]{1,0:T(8,128)(2,1)S(1)}, u32[]{:S(2)}, u32[]{:S(2)}) collective-permute-start(bf16[64,256]{1,0:T(8,128)(2,1)S(1)} %get-tuple-element.375), channel_id=1, source_target_pairs={{0,1},{1,2},{2,3},{3,4},{4,5},{5,6},{6,7},{7,8},{8,9},{9,10},{10,1... | collective-permute-start | bytes 98312 | tf_op jit(solution)/shard_map/while/body/eval_jaxpr/ppermute | solution.py:16
  111.0 7.2 %collective-permute-start = (bf16[64,256]{1,0:T(8,128)(2,1)S(1)}, bf16[64,256]{1,0:T(8,128)(2,1)S(1)}, u32[]{:S(2)}, u32[]{:S(2)}) collective-permute-start(bf16[64,256]{1,0:T(8,128)(2,1)S(1)} %get-tuple-element.375), channel_id=1, source_target_pairs={{0,1},{1,2},{2,3},{3,4},{4,5},{5,6},{6,7},{7,8},{8,9},{9,10},{10,1... | collective-permute-start | bytes 98312 | tf_op jit(solution)/shard_map/while/body/eval_jaxpr/ppermute | solution.py:16
  120.2 7.2 %collective-permute-start = (bf16[64,256]{1,0:T(8,128)(2,1)S(1)}, bf16[64,256]{1,0:T(8,128)(2,1)S(1)}, u32[]{:S(2)}, u32[]{:S(2)}) collective-permute-start(bf16[64,256]{1,0:T(8,128)(2,1)S(1)} %get-tuple-element.375), channel_id=1, source_target_pairs={{0,1},{1,2},{2,3},{3,4},{4,5},{5,6},{6,7},{7,8},{8,9},{9,10},{10,1... | collective-permute-start | bytes 98312 | tf_op jit(solution)/shard_map/while/body/eval_jaxpr/ppermute | solution.py:16
  121.8 7.4 %collective-permute-start.3 = (f32[32,256]{1,0:T(8,128)S(1)}, f32[32,256]{1,0:T(8,128)S(1)}, u32[]{:S(2)}, u32[]{:S(2)}) collective-permute-start(f32[32,256]{1,0:T(8,128)S(1)} %broadcast_select_fusion.4), channel_id=1, source_target_pairs={{0,1},{1,2},{2,3},{3,4},{4,5},{5,6},{6,7},{7,8},{8,9},{9,10},{10,1... | collective-permute-start | bytes 98312 | tf_op jit(solution)/shard_map/while/body/eval_jaxpr/ppermute | solution.py:16
  129.4 7.2 %collective-permute-start = (bf16[64,256]{1,0:T(8,128)(2,1)S(1)}, bf16[64,256]{1,0:T(8,128)(2,1)S(1)}, u32[]{:S(2)}, u32[]{:S(2)}) collective-permute-start(bf16[64,256]{1,0:T(8,128)(2,1)S(1)} %get-tuple-element.375), channel_id=1, source_target_pairs={{0,1},{1,2},{2,3},{3,4},{4,5},{5,6},{6,7},{7,8},{8,9},{9,10},{10,1... | collective-permute-start | bytes 98312 | tf_op jit(solution)/shard_map/while/body/eval_jaxpr/ppermute | solution.py:16
  129.7 8.6 %collective-permute-start.3 = (f32[32,256]{1,0:T(8,128)S(1)}, f32[32,256]{1,0:T(8,128)S(1)}, u32[]{:S(2)}, u32[]{:S(2)}) collective-permute-start(f32[32,256]{1,0:T(8,128)S(1)} %broadcast_select_fusion.4), channel_id=1, source_target_pairs={{0,1},{1,2},{2,3},{3,4},{4,5},{5,6},{6,7},{7,8},{8,9},{9,10},{10,1... | collective-permute-start | bytes 98312 | tf_op jit(solution)/shard_map/while/body/eval_jaxpr/ppermute | solution.py:16
  138.6 7.2 %collective-permute-start = (bf16[64,256]{1,0:T(8,128)(2,1)S(1)}, bf16[64,256]{1,0:T(8,128)(2,1)S(1)}, u32[]{:S(2)}, u32[]{:S(2)}) collective-permute-start(bf16[64,256]{1,0:T(8,128)(2,1)S(1)} %get-tuple-element.375), channel_id=1, source_target_pairs={{0,1},{1,2},{2,3},{3,4},{4,5},{5,6},{6,7},{7,8},{8,9},{9,10},{10,1... | collective-permute-start | bytes 98312 | tf_op jit(solution)/shard_map/while/body/eval_jaxpr/ppermute | solution.py:16
  138.9 8.6 %collective-permute-start.3 = (f32[32,256]{1,0:T(8,128)S(1)}, f32[32,256]{1,0:T(8,128)S(1)}, u32[]{:S(2)}, u32[]{:S(2)}) collective-permute-start(f32[32,256]{1,0:T(8,128)S(1)} %broadcast_select_fusion.4), channel_id=1, source_target_pairs={{0,1},{1,2},{2,3},{3,4},{4,5},{5,6},{6,7},{7,8},{8,9},{9,10},{10,1... | collective-permute-start | bytes 98312 | tf_op jit(solution)/shard_map/while/body/eval_jaxpr/ppermute | solution.py:16
  147.8 7.2 %collective-permute-start = (bf16[64,256]{1,0:T(8,128)(2,1)S(1)}, bf16[64,256]{1,0:T(8,128)(2,1)S(1)}, u32[]{:S(2)}, u32[]{:S(2)}) collective-permute-start(bf16[64,256]{1,0:T(8,128)(2,1)S(1)} %get-tuple-element.375), channel_id=1, source_target_pairs={{0,1},{1,2},{2,3},{3,4},{4,5},{5,6},{6,7},{7,8},{8,9},{9,10},{10,1... | collective-permute-start | bytes 98312 | tf_op jit(solution)/shard_map/while/body/eval_jaxpr/ppermute | solution.py:16
  148.1 8.6 %collective-permute-start.3 = (f32[32,256]{1,0:T(8,128)S(1)}, f32[32,256]{1,0:T(8,128)S(1)}, u32[]{:S(2)}, u32[]{:S(2)}) collective-permute-start(f32[32,256]{1,0:T(8,128)S(1)} %broadcast_select_fusion.4), channel_id=1, source_target_pairs={{0,1},{1,2},{2,3},{3,4},{4,5},{5,6},{6,7},{7,8},{8,9},{9,10},{10,1... | collective-permute-start | bytes 98312 | tf_op jit(solution)/shard_map/while/body/eval_jaxpr/ppermute | solution.py:16
  157.1 7.2 %collective-permute-start = (bf16[64,256]{1,0:T(8,128)(2,1)S(1)}, bf16[64,256]{1,0:T(8,128)(2,1)S(1)}, u32[]{:S(2)}, u32[]{:S(2)}) collective-permute-start(bf16[64,256]{1,0:T(8,128)(2,1)S(1)} %get-tuple-element.375), channel_id=1, source_target_pairs={{0,1},{1,2},{2,3},{3,4},{4,5},{5,6},{6,7},{7,8},{8,9},{9,10},{10,1... | collective-permute-start | bytes 98312 | tf_op jit(solution)/shard_map/while/body/eval_jaxpr/ppermute | solution.py:16
  157.3 8.6 %collective-permute-start.3 = (f32[32,256]{1,0:T(8,128)S(1)}, f32[32,256]{1,0:T(8,128)S(1)}, u32[]{:S(2)}, u32[]{:S(2)}) collective-permute-start(f32[32,256]{1,0:T(8,128)S(1)} %broadcast_select_fusion.4), channel_id=1, source_target_pairs={{0,1},{1,2},{2,3},{3,4},{4,5},{5,6},{6,7},{7,8},{8,9},{9,10},{10,1... | collective-permute-start | bytes 98312 | tf_op jit(solution)/shard_map/while/body/eval_jaxpr/ppermute | solution.py:16
  166.3 7.2 %collective-permute-start = (bf16[64,256]{1,0:T(8,128)(2,1)S(1)}, bf16[64,256]{1,0:T(8,128)(2,1)S(1)}, u32[]{:S(2)}, u32[]{:S(2)}) collective-permute-start(bf16[64,256]{1,0:T(8,128)(2,1)S(1)} %get-tuple-element.375), channel_id=1, source_target_pairs={{0,1},{1,2},{2,3},{3,4},{4,5},{5,6},{6,7},{7,8},{8,9},{9,10},{10,1... | collective-permute-start | bytes 98312 | tf_op jit(solution)/shard_map/while/body/eval_jaxpr/ppermute | solution.py:16
  166.5 8.6 %collective-permute-start.3 = (f32[32,256]{1,0:T(8,128)S(1)}, f32[32,256]{1,0:T(8,128)S(1)}, u32[]{:S(2)}, u32[]{:S(2)}) collective-permute-start(f32[32,256]{1,0:T(8,128)S(1)} %broadcast_select_fusion.4), channel_id=1, source_target_pairs={{0,1},{1,2},{2,3},{3,4},{4,5},{5,6},{6,7},{7,8},{8,9},{9,10},{10,1... | collective-permute-start | bytes 98312 | tf_op jit(solution)/shard_map/while/body/eval_jaxpr/ppermute | solution.py:16
  175.5 7.2 %collective-permute-start = (bf16[64,256]{1,0:T(8,128)(2,1)S(1)}, bf16[64,256]{1,0:T(8,128)(2,1)S(1)}, u32[]{:S(2)}, u32[]{:S(2)}) collective-permute-start(bf16[64,256]{1,0:T(8,128)(2,1)S(1)} %get-tuple-element.375), channel_id=1, source_target_pairs={{0,1},{1,2},{2,3},{3,4},{4,5},{5,6},{6,7},{7,8},{8,9},{9,10},{10,1... | collective-permute-start | bytes 98312 | tf_op jit(solution)/shard_map/while/body/eval_jaxpr/ppermute | solution.py:16
  175.8 8.6 %collective-permute-start.3 = (f32[32,256]{1,0:T(8,128)S(1)}, f32[32,256]{1,0:T(8,128)S(1)}, u32[]{:S(2)}, u32[]{:S(2)}) collective-permute-start(f32[32,256]{1,0:T(8,128)S(1)} %broadcast_select_fusion.4), channel_id=1, source_target_pairs={{0,1},{1,2},{2,3},{3,4},{4,5},{5,6},{6,7},{7,8},{8,9},{9,10},{10,1... | collective-permute-start | bytes 98312 | tf_op jit(solution)/shard_map/while/body/eval_jaxpr/ppermute | solution.py:16
  184.7 7.2 %collective-permute-start = (bf16[64,256]{1,0:T(8,128)(2,1)S(1)}, bf16[64,256]{1,0:T(8,128)(2,1)S(1)}, u32[]{:S(2)}, u32[]{:S(2)}) collective-permute-start(bf16[64,256]{1,0:T(8,128)(2,1)S(1)} %get-tuple-element.375), channel_id=1, source_target_pairs={{0,1},{1,2},{2,3},{3,4},{4,5},{5,6},{6,7},{7,8},{8,9},{9,10},{10,1... | collective-permute-start | bytes 98312 | tf_op jit(solution)/shard_map/while/body/eval_jaxpr/ppermute | solution.py:16
  185.0 8.6 %collective-permute-start.3 = (f32[32,256]{1,0:T(8,128)S(1)}, f32[32,256]{1,0:T(8,128)S(1)}, u32[]{:S(2)}, u32[]{:S(2)}) collective-permute-start(f32[32,256]{1,0:T(8,128)S(1)} %broadcast_select_fusion.4), channel_id=1, source_target_pairs={{0,1},{1,2},{2,3},{3,4},{4,5},{5,6},{6,7},{7,8},{8,9},{9,10},{10,1... | collective-permute-start | bytes 98312 | tf_op jit(solution)/shard_map/while/body/eval_jaxpr/ppermute | solution.py:16
  193.9 7.2 %collective-permute-start = (bf16[64,256]{1,0:T(8,128)(2,1)S(1)}, bf16[64,256]{1,0:T(8,128)(2,1)S(1)}, u32[]{:S(2)}, u32[]{:S(2)}) collective-permute-start(bf16[64,256]{1,0:T(8,128)(2,1)S(1)} %get-tuple-element.375), channel_id=1, source_target_pairs={{0,1},{1,2},{2,3},{3,4},{4,5},{5,6},{6,7},{7,8},{8,9},{9,10},{10,1... | collective-permute-start | bytes 98312 | tf_op jit(solution)/shard_map/while/body/eval_jaxpr/ppermute | solution.py:16
  194.2 8.6 %collective-permute-start.3 = (f32[32,256]{1,0:T(8,128)S(1)}, f32[32,256]{1,0:T(8,128)S(1)}, u32[]{:S(2)}, u32[]{:S(2)}) collective-permute-start(f32[32,256]{1,0:T(8,128)S(1)} %broadcast_select_fusion.4), channel_id=1, source_target_pairs={{0,1},{1,2},{2,3},{3,4},{4,5},{5,6},{6,7},{7,8},{8,9},{9,10},{10,1... | collective-permute-start | bytes 98312 | tf_op jit(solution)/shard_map/while/body/eval_jaxpr/ppermute | solution.py:16
  203.1 7.2 %collective-permute-start = (bf16[64,256]{1,0:T(8,128)(2,1)S(1)}, bf16[64,256]{1,0:T(8,128)(2,1)S(1)}, u32[]{:S(2)}, u32[]{:S(2)}) collective-permute-start(bf16[64,256]{1,0:T(8,128)(2,1)S(1)} %get-tuple-element.375), channel_id=1, source_target_pairs={{0,1},{1,2},{2,3},{3,4},{4,5},{5,6},{6,7},{7,8},{8,9},{9,10},{10,1... | collective-permute-start | bytes 98312 | tf_op jit(solution)/shard_map/while/body/eval_jaxpr/ppermute | solution.py:16
  203.4 8.6 %collective-permute-start.3 = (f32[32,256]{1,0:T(8,128)S(1)}, f32[32,256]{1,0:T(8,128)S(1)}, u32[]{:S(2)}, u32[]{:S(2)}) collective-permute-start(f32[32,256]{1,0:T(8,128)S(1)} %broadcast_select_fusion.4), channel_id=1, source_target_pairs={{0,1},{1,2},{2,3},{3,4},{4,5},{5,6},{6,7},{7,8},{8,9},{9,10},{10,1... | collective-permute-start | bytes 98312 | tf_op jit(solution)/shard_map/while/body/eval_jaxpr/ppermute | solution.py:16
  212.3 7.2 %collective-permute-start = (bf16[64,256]{1,0:T(8,128)(2,1)S(1)}, bf16[64,256]{1,0:T(8,128)(2,1)S(1)}, u32[]{:S(2)}, u32[]{:S(2)}) collective-permute-start(bf16[64,256]{1,0:T(8,128)(2,1)S(1)} %get-tuple-element.375), channel_id=1, source_target_pairs={{0,1},{1,2},{2,3},{3,4},{4,5},{5,6},{6,7},{7,8},{8,9},{9,10},{10,1... | collective-permute-start | bytes 98312 | tf_op jit(solution)/shard_map/while/body/eval_jaxpr/ppermute | solution.py:16
  212.6 8.6 %collective-permute-start.3 = (f32[32,256]{1,0:T(8,128)S(1)}, f32[32,256]{1,0:T(8,128)S(1)}, u32[]{:S(2)}, u32[]{:S(2)}) collective-permute-start(f32[32,256]{1,0:T(8,128)S(1)} %broadcast_select_fusion.4), channel_id=1, source_target_pairs={{0,1},{1,2},{2,3},{3,4},{4,5},{5,6},{6,7},{7,8},{8,9},{9,10},{10,1... | collective-permute-start | bytes 98312 | tf_op jit(solution)/shard_map/while/body/eval_jaxpr/ppermute | solution.py:16
  230.6 245.5 %reduce-scatter.5.cloned.1.call-start = ((), (), s32[]{:S(2)}) async-start(), calls=%async_computation.3 | async-start | bytes 294912 | tf_op jit(solution)/shard_map/reduce_scatter | solution.py:91
  230.6 10.5 %collective-permute-start.11 = (f32[32,256]{1,0:T(8,128)S(1)}, f32[32,256]{1,0:T(8,128)S(1)}, u32[]{:S(2)}, u32[]{:S(2)}) collective-permute-start(f32[32,256]{1,0:T(8,128)S(1)} %get-tuple-element.119), channel_id=1, source_target_pairs={{0,17},{1,18},{2,19},{3,20},{4,21},{5,22},{6,23},{7,24},{8,25},{9,... | collective-permute-start | bytes 98312 | tf_op jit(solution)/shard_map/ppermute | solution.py:16
  287.7 16.2 %collective-permute-start.4 = (bf16[64,256]{1,0:T(8,128)(2,1)S(1)}, bf16[64,256]{1,0:T(8,128)(2,1)S(1)}, u32[]{:S(2)}, u32[]{:S(2)}) collective-permute-start(bf16[64,256]{1,0:T(8,128)(2,1)S(1)} %get-tuple-element.411), channel_id=1, source_target_pairs={{0,1},{1,2},{2,3},{3,4},{4,5},{5,6},{6,7},{7,8},{8,9},{9,10},{10,1... | collective-permute-start | bytes 98312 | tf_op jit(solution)/shard_map/while/body/eval_jaxpr/ppermute | solution.py:16
  332.0 7.2 %collective-permute-start.4 = (bf16[64,256]{1,0:T(8,128)(2,1)S(1)}, bf16[64,256]{1,0:T(8,128)(2,1)S(1)}, u32[]{:S(2)}, u32[]{:S(2)}) collective-permute-start(bf16[64,256]{1,0:T(8,128)(2,1)S(1)} %get-tuple-element.411), channel_id=1, source_target_pairs={{0,1},{1,2},{2,3},{3,4},{4,5},{5,6},{6,7},{7,8},{8,9},{9,10},{10,1... | collective-permute-start | bytes 98312 | tf_op jit(solution)/shard_map/while/body/eval_jaxpr/ppermute | solution.py:16
  332.3 8.6 %collective-permute-start.7 = (f32[32,256]{1,0:T(8,128)S(1)}, f32[32,256]{1,0:T(8,128)S(1)}, u32[]{:S(2)}, u32[]{:S(2)}) collective-permute-start(f32[32,256]{1,0:T(8,128)S(1)} %broadcast_select_fusion.5), channel_id=1, source_target_pairs={{0,1},{1,2},{2,3},{3,4},{4,5},{5,6},{6,7},{7,8},{8,9},{9,10},{10,1... | collective-permute-start | bytes 98312 | tf_op jit(solution)/shard_map/while/body/eval_jaxpr/ppermute | solution.py:16
  341.2 7.2 %collective-permute-start.4 = (bf16[64,256]{1,0:T(8,128)(2,1)S(1)}, bf16[64,256]{1,0:T(8,128)(2,1)S(1)}, u32[]{:S(2)}, u32[]{:S(2)}) collective-permute-start(bf16[64,256]{1,0:T(8,128)(2,1)S(1)} %get-tuple-element.411), channel_id=1, source_target_pairs={{0,1},{1,2},{2,3},{3,4},{4,5},{5,6},{6,7},{7,8},{8,9},{9,10},{10,1... | collective-permute-start | bytes 98312 | tf_op jit(solution)/shard_map/while/body/eval_jaxpr/ppermute | solution.py:16
  341.5 8.6 %collective-permute-start.7 = (f32[32,256]{1,0:T(8,128)S(1)}, f32[32,256]{1,0:T(8,128)S(1)}, u32[]{:S(2)}, u32[]{:S(2)}) collective-permute-start(f32[32,256]{1,0:T(8,128)S(1)} %broadcast_select_fusion.5), channel_id=1, source_target_pairs={{0,1},{1,2},{2,3},{3,4},{4,5},{5,6},{6,7},{7,8},{8,9},{9,10},{10,1... | collective-permute-start | bytes 98312 | tf_op jit(solution)/shard_map/while/body/eval_jaxpr/ppermute | solution.py:16
  350.4 7.2 %collective-permute-start.4 = (bf16[64,256]{1,0:T(8,128)(2,1)S(1)}, bf16[64,256]{1,0:T(8,128)(2,1)S(1)}, u32[]{:S(2)}, u32[]{:S(2)}) collective-permute-start(bf16[64,256]{1,0:T(8,128)(2,1)S(1)} %get-tuple-element.411), channel_id=1, source_target_pairs={{0,1},{1,2},{2,3},{3,4},{4,5},{5,6},{6,7},{7,8},{8,9},{9,10},{10,1... | collective-permute-start | bytes 98312 | tf_op jit(solution)/shard_map/while/body/eval_jaxpr/ppermute | solution.py:16
  350.7 8.6 %collective-permute-start.7 = (f32[32,256]{1,0:T(8,128)S(1)}, f32[32,256]{1,0:T(8,128)S(1)}, u32[]{:S(2)}, u32[]{:S(2)}) collective-permute-start(f32[32,256]{1,0:T(8,128)S(1)} %broadcast_select_fusion.5), channel_id=1, source_target_pairs={{0,1},{1,2},{2,3},{3,4},{4,5},{5,6},{6,7},{7,8},{8,9},{9,10},{10,1... | collective-permute-start | bytes 98312 | tf_op jit(solution)/shard_map/while/body/eval_jaxpr/ppermute | solution.py:16
  359.6 7.2 %collective-permute-start.4 = (bf16[64,256]{1,0:T(8,128)(2,1)S(1)}, bf16[64,256]{1,0:T(8,128)(2,1)S(1)}, u32[]{:S(2)}, u32[]{:S(2)}) collective-permute-start(bf16[64,256]{1,0:T(8,128)(2,1)S(1)} %get-tuple-element.411), channel_id=1, source_target_pairs={{0,1},{1,2},{2,3},{3,4},{4,5},{5,6},{6,7},{7,8},{8,9},{9,10},{10,1... | collective-permute-start | bytes 98312 | tf_op jit(solution)/shard_map/while/body/eval_jaxpr/ppermute | solution.py:16
  359.9 8.6 %collective-permute-start.7 = (f32[32,256]{1,0:T(8,128)S(1)}, f32[32,256]{1,0:T(8,128)S(1)}, u32[]{:S(2)}, u32[]{:S(2)}) collective-permute-start(f32[32,256]{1,0:T(8,128)S(1)} %broadcast_select_fusion.5), channel_id=1, source_target_pairs={{0,1},{1,2},{2,3},{3,4},{4,5},{5,6},{6,7},{7,8},{8,9},{9,10},{10,1... | collective-permute-start | bytes 98312 | tf_op jit(solution)/shard_map/while/body/eval_jaxpr/ppermute | solution.py:16
  368.8 7.2 %collective-permute-start.4 = (bf16[64,256]{1,0:T(8,128)(2,1)S(1)}, bf16[64,256]{1,0:T(8,128)(2,1)S(1)}, u32[]{:S(2)}, u32[]{:S(2)}) collective-permute-start(bf16[64,256]{1,0:T(8,128)(2,1)S(1)} %get-tuple-element.411), channel_id=1, source_target_pairs={{0,1},{1,2},{2,3},{3,4},{4,5},{5,6},{6,7},{7,8},{8,9},{9,10},{10,1... | collective-permute-start | bytes 98312 | tf_op jit(solution)/shard_map/while/body/eval_jaxpr/ppermute | solution.py:16
  369.1 8.6 %collective-permute-start.7 = (f32[32,256]{1,0:T(8,128)S(1)}, f32[32,256]{1,0:T(8,128)S(1)}, u32[]{:S(2)}, u32[]{:S(2)}) collective-permute-start(f32[32,256]{1,0:T(8,128)S(1)} %broadcast_select_fusion.5), channel_id=1, source_target_pairs={{0,1},{1,2},{2,3},{3,4},{4,5},{5,6},{6,7},{7,8},{8,9},{9,10},{10,1... | collective-permute-start | bytes 98312 | tf_op jit(solution)/shard_map/while/body/eval_jaxpr/ppermute | solution.py:16
  378.0 7.2 %collective-permute-start.4 = (bf16[64,256]{1,0:T(8,128)(2,1)S(1)}, bf16[64,256]{1,0:T(8,128)(2,1)S(1)}, u32[]{:S(2)}, u32[]{:S(2)}) collective-permute-start(bf16[64,256]{1,0:T(8,128)(2,1)S(1)} %get-tuple-element.411), channel_id=1, source_target_pairs={{0,1},{1,2},{2,3},{3,4},{4,5},{5,6},{6,7},{7,8},{8,9},{9,10},{10,1... | collective-permute-start | bytes 98312 | tf_op jit(solution)/shard_map/while/body/eval_jaxpr/ppermute | solution.py:16
  378.3 8.6 %collective-permute-start.7 = (f32[32,256]{1,0:T(8,128)S(1)}, f32[32,256]{1,0:T(8,128)S(1)}, u32[]{:S(2)}, u32[]{:S(2)}) collective-permute-start(f32[32,256]{1,0:T(8,128)S(1)} %broadcast_select_fusion.5), channel_id=1, source_target_pairs={{0,1},{1,2},{2,3},{3,4},{4,5},{5,6},{6,7},{7,8},{8,9},{9,10},{10,1... | collective-permute-start | bytes 98312 | tf_op jit(solution)/shard_map/while/body/eval_jaxpr/ppermute | solution.py:16
  387.2 7.2 %collective-permute-start.4 = (bf16[64,256]{1,0:T(8,128)(2,1)S(1)}, bf16[64,256]{1,0:T(8,128)(2,1)S(1)}, u32[]{:S(2)}, u32[]{:S(2)}) collective-permute-start(bf16[64,256]{1,0:T(8,128)(2,1)S(1)} %get-tuple-element.411), channel_id=1, source_target_pairs={{0,1},{1,2},{2,3},{3,4},{4,5},{5,6},{6,7},{7,8},{8,9},{9,10},{10,1... | collective-permute-start | bytes 98312 | tf_op jit(solution)/shard_map/while/body/eval_jaxpr/ppermute | solution.py:16
  387.5 8.6 %collective-permute-start.7 = (f32[32,256]{1,0:T(8,128)S(1)}, f32[32,256]{1,0:T(8,128)S(1)}, u32[]{:S(2)}, u32[]{:S(2)}) collective-permute-start(f32[32,256]{1,0:T(8,128)S(1)} %broadcast_select_fusion.5), channel_id=1, source_target_pairs={{0,1},{1,2},{2,3},{3,4},{4,5},{5,6},{6,7},{7,8},{8,9},{9,10},{10,1... | collective-permute-start | bytes 98312 | tf_op jit(solution)/shard_map/while/body/eval_jaxpr/ppermute | solution.py:16
  396.4 7.2 %collective-permute-start.4 = (bf16[64,256]{1,0:T(8,128)(2,1)S(1)}, bf16[64,256]{1,0:T(8,128)(2,1)S(1)}, u32[]{:S(2)}, u32[]{:S(2)}) collective-permute-start(bf16[64,256]{1,0:T(8,128)(2,1)S(1)} %get-tuple-element.411), channel_id=1, source_target_pairs={{0,1},{1,2},{2,3},{3,4},{4,5},{5,6},{6,7},{7,8},{8,9},{9,10},{10,1... | collective-permute-start | bytes 98312 | tf_op jit(solution)/shard_map/while/body/eval_jaxpr/ppermute | solution.py:16
  396.7 8.6 %collective-permute-start.7 = (f32[32,256]{1,0:T(8,128)S(1)}, f32[32,256]{1,0:T(8,128)S(1)}, u32[]{:S(2)}, u32[]{:S(2)}) collective-permute-start(f32[32,256]{1,0:T(8,128)S(1)} %broadcast_select_fusion.5), channel_id=1, source_target_pairs={{0,1},{1,2},{2,3},{3,4},{4,5},{5,6},{6,7},{7,8},{8,9},{9,10},{10,1... | collective-permute-start | bytes 98312 | tf_op jit(solution)/shard_map/while/body/eval_jaxpr/ppermute | solution.py:16
  405.9 8.6 %collective-permute-start.7 = (f32[32,256]{1,0:T(8,128)S(1)}, f32[32,256]{1,0:T(8,128)S(1)}, u32[]{:S(2)}, u32[]{:S(2)}) collective-permute-start(f32[32,256]{1,0:T(8,128)S(1)} %broadcast_select_fusion.5), channel_id=1, source_target_pairs={{0,1},{1,2},{2,3},{3,4},{4,5},{5,6},{6,7},{7,8},{8,9},{9,10},{10,1... | collective-permute-start | bytes 98312 | tf_op jit(solution)/shard_map/while/body/eval_jaxpr/ppermute | solution.py:16
  415.1 8.6 %collective-permute-start.7 = (f32[32,256]{1,0:T(8,128)S(1)}, f32[32,256]{1,0:T(8,128)S(1)}, u32[]{:S(2)}, u32[]{:S(2)}) collective-permute-start(f32[32,256]{1,0:T(8,128)S(1)} %broadcast_select_fusion.5), channel_id=1, source_target_pairs={{0,1},{1,2},{2,3},{3,4},{4,5},{5,6},{6,7},{7,8},{8,9},{9,10},{10,1... | collective-permute-start | bytes 98312 | tf_op jit(solution)/shard_map/while/body/eval_jaxpr/ppermute | solution.py:16
  424.3 8.6 %collective-permute-start.7 = (f32[32,256]{1,0:T(8,128)S(1)}, f32[32,256]{1,0:T(8,128)S(1)}, u32[]{:S(2)}, u32[]{:S(2)}) collective-permute-start(f32[32,256]{1,0:T(8,128)S(1)} %broadcast_select_fusion.5), channel_id=1, source_target_pairs={{0,1},{1,2},{2,3},{3,4},{4,5},{5,6},{6,7},{7,8},{8,9},{9,10},{10,1... | collective-permute-start | bytes 98312 | tf_op jit(solution)/shard_map/while/body/eval_jaxpr/ppermute | solution.py:16
  442.3 10.3 %collective-permute-start.15 = (f32[32,256]{1,0:T(8,128)S(1)}, f32[32,256]{1,0:T(8,128)S(1)}, u32[]{:S(2)}, u32[]{:S(2)}) collective-permute-start(f32[32,256]{1,0:T(8,128)S(1)} %get-tuple-element.124), channel_id=1, source_target_pairs={{0,17},{1,18},{2,19},{3,20},{4,21},{5,22},{6,23},{7,24},{8,25},{9,... | collective-permute-start | bytes 98312 | tf_op jit(solution)/shard_map/ppermute | solution.py:16
  (85 other events, 646.1 us)
Sparse Core Ops, SparseCore 0:
  230.7 33.8 reduce-scatter.2
  442.5 33.5 reduce-scatter.4
where the time goes:
time: 641 us; the launch traced here: 640 us
  waiting for transfers between devices  245 us (38%)
  blocking collectives  237 us (37%)
  starting transfers between devices  71.8 us (11%)
  matrix products  63 us (10%)
  between operations  14.2 us (2%)
    ppermute x128, waiting for transfers between devices, from_behind(): return lax.ppermute(value, axis, pairs)  198 us
    psum x1, blocking collectives, per_device(): norm_old = lax.psum(jnp.sum(residual0 * residual0, axis=1), ('row', 'col'))  80.9 us
    psum x1, blocking collectives, per_device(): norm_new = lax.psum(jnp.sum(residual * residual, axis=1), ('row', 'col'))  73.3 us
    ppermute x128, starting transfers between devices, from_behind(): return lax.ppermute(value, axis, pairs)  71.7 us
    reduce_scatter x2, waiting for transfers between devices, apply_operator(): lax.psum_scatter(partial_value, 'row', scatter_dimension=1, tiled=True)  46.8 us
    all_gather x2, blocking collectives, apply_operator(): home_vector = lax.all_gather(rounded, 'row', axis=1, tiled=True)  44.1 us
    dot_general x31, matrix products, kernel_tile(): lax.dot_general(home_features, piece_features, (((0,), (0,)), ((), ())),...  37.4 us
    all_gather x1, blocking collectives, per_device(): lax.all_gather(features, 'row', axis=1, tiled=True)  23.3 us
  transfers between devices with their start and end apart: 130, of which 64 were waited for; matrix products, arithmetic and copies ran while one was open for 8% of the time, Pallas kernels for 0%

commit v1 on v0

v1 whole, which is shorter than its diff:
```python
import functools
import math

import jax
import jax.numpy as jnp
from jax import lax
from jax.experimental import pallas as pl
from jax.experimental.pallas import tpu as pltpu
from jax.sharding import Mesh, PartitionSpec as P

RHO = 0.2
AMP_NUM = 16.0

AXES = ("yl", "x", "yh", "z", "core")
PLANE = ("yl", "x", "yh")
LINE = ("z",)

BF16 = jnp.bfloat16
F32 = jnp.float32

HEAD = 80
DEPTH = 128
WIDE = 512


def scale_of(width):
    return 2.0 * math.log2(math.e) / width


def pieces_of(value):
    first = value.astype(BF16).astype(F32)
    rest = value - first
    second = rest.astype(BF16).astype(F32)
    return first, second, rest - second


def constant_pieces(value):
    import numpy as np
    import ml_dtypes

    out = []
    rest = value
    for _ in range(3):
        piece = float(np.float32(rest).astype(ml_dtypes.bfloat16))
        out.append(piece)
        rest = rest - piece
    return out


def pack_body(features_ref, groups_ref, start_ref, plane_ref, line_ref, *, shift):
    features = features_ref[...]
    wide = features.astype(F32)
    half = shift - 0.5 * jnp.sum(wide * wide, axis=0, keepdims=True)
    first, second, third = pieces_of(half)
    group = groups_ref[...].astype(F32)
    count = features.shape[1]
    row = lax.broadcasted_iota(jnp.int32, (16, count), 0)
    tail = jnp.where(row == 0, first, 0.0)
    tail = jnp.where(row == 1, second, tail)
    tail = jnp.where(row == 2, third, tail)
    tail = jnp.where(row == 3, group, tail).astype(BF16)
    vector = start_ref[...].astype(BF16)
    for n in range(plane_ref.shape[0]):
        plane_ref[n, 0:64, :] = features
        plane_ref[n, 64:80, :] = tail
    for n in range(line_ref.shape[0]):
        line_ref[n, 0:64, :] = features
        line_ref[n, 64:80, :] = tail
        line_ref[n, 80:112, :] = vector


def tail_rows(packed, left, gains):
    count = packed.shape[1]
    head = packed.astype(F32)
    first, second, third, group = (head[n : n + 1, :] for n in range(4))
    row = lax.broadcasted_iota(jnp.int32, (64, count), 0)
    level = (row & 7).astype(F32)
    hot = jnp.where(level == group, 1.0, 0.0)
    if not left:
        hot = hot * jnp.where(row < 16, gains[0], jnp.where(row < 24, gains[1], gains[2]))
    out = jnp.where((row >= 8) & (row < 32), hot, 0.0)
    base = 0 if left else 3
    out = jnp.where((row >= 3 - base) & (row < 6 - base), 1.0, out)
    out = jnp.where(row == base, first, out)
    out = jnp.where(row == base + 1, second, out)
    out = jnp.where(row == base + 2, third, out)
    return out.astype(BF16)


def build_body(scale, gains, added, line_ref, plane_ref, *refs):
    if added:
        carried_ref, tile_ref, out_ref, left_ref, vector_ref, right_ref = refs
    else:
        tile_ref, out_ref, left_ref, vector_ref, right_ref = refs
    blocks, _, size = line_ref.shape

    @pl.when(pl.program_id(0) == 0)
    def _():
        for n in range(blocks):
            rows = line_ref[n, 0:64, :]
            tail = tail_rows(line_ref[n, 64:80, :], True, gains)
            left_ref[n * size : (n + 1) * size, :] = jnp.concatenate([rows, tail], axis=0).T
            vector_ref[:, n * size : (n + 1) * size] = line_ref[n, 80:112, :]

    for n in range(plane_ref.shape[0]):
        right_ref[0:64, n * size : (n + 1) * size] = plane_ref[n, 0:64, :]
        right_ref[64:128, n * size : (n + 1) * size] = tail_rows(
            plane_ref[n, 64:80, :], False, gains
        )
    right = right_ref[...]
    for n in range(blocks):
        power = jnp.dot(
            left_ref[n * size : (n + 1) * size, :], right, preferred_element_type=F32
        )
        tile_ref[n * size : (n + 1) * size, :] = jnp.exp2(power * scale).astype(BF16)
    product = jnp.dot(vector_ref[...], tile_ref[...], preferred_element_type=F32)
    for n in range(plane_ref.shape[0]):
        value = product[:, n * size : (n + 1) * size]
        if added:
            value = value + carried_ref[n]
        out_ref[n] = value.astype(out_ref.dtype)


def build(line, plane, carried, scale, gains, out_dtype):
    blocks, rows, size = line.shape
    columns = plane.shape[0]
    per = WIDE // size
    vectors = rows - HEAD
    points = blocks * size
    in_specs = [
        pl.BlockSpec(line.shape, lambda j: (0, 0, 0)),
        pl.BlockSpec((per, HEAD, size), lambda j: (j, 0, 0)),
    ]
    operands = [line, plane]
    if carried is not None:
        in_specs.append(pl.BlockSpec((per, vectors, size), lambda j: (j, 0, 0)))
        operands.append(carried)
    return pl.pallas_call(
        functools.partial(build_body, scale, gains, carried is not None),
        grid=(columns // per,),
        in_specs=in_specs,
        out_specs=[
            pl.BlockSpec((points, WIDE), lambda j: (0, j)),
            pl.BlockSpec((per, vectors, size), lambda j: (j, 0, 0)),
        ],
        out_shape=[
            jax.ShapeDtypeStruct((points, columns * size), BF16),
            jax.ShapeDtypeStruct((columns, vectors, size), out_dtype),
        ],
        scratch_shapes=[
            pltpu.VMEM((points, DEPTH), BF16),
            pltpu.VMEM((vectors, points), BF16),
            pltpu.VMEM((DEPTH, WIDE), BF16),
        ],
        compiler_params=pltpu.CompilerParams(vmem_limit_bytes=40 << 20),
        cost_estimate=pl.CostEstimate(
            flops=2 * points * columns * size * 512,
            bytes_accessed=2 * points * columns * size,
            transcendentals=points * columns * size,
        ),
        name="build",
    )(*operands)


def apply_body(added, vector_ref, tile_ref, *refs):
    if added:
        carried_ref, out_ref, flat_ref = refs
    else:
        out_ref, flat_ref = refs
    blocks, _, size = vector_ref.shape

    @pl.when(pl.program_id(0) == 0)
    def _():
        for n in range(blocks):
            flat_ref[:, n * size : (n + 1) * size] = vector_ref[n]

    product = jnp.dot(flat_ref[...], tile_ref[...], preferred_element_type=F32)
    for n in range(out_ref.shape[0]):
        value = product[:, n * size : (n + 1) * size]
        if added:
            value = value + carried_ref[n]
        out_ref[n] = value.astype(out_ref.dtype)


def apply(vector, tile, carried, out_dtype):
    blocks, vectors, size = vector.shape
    points, total = tile.shape
    per = WIDE // size
    in_specs = [
        pl.BlockSpec(vector.shape, lambda j: (0, 0, 0)),
        pl.BlockSpec((points, WIDE), lambda j: (0, j)),
    ]
    operands = [vector, tile]
    if carried is not None:
        in_specs.append(pl.BlockSpec((per, vectors, size), lambda j: (j, 0, 0)))
        operands.append(carried)
    return pl.pallas_call(
        functools.partial(apply_body, carried is not None),
        grid=(total // WIDE,),
        in_specs=in_specs,
        out_specs=pl.BlockSpec((per, vectors, size), lambda j: (j, 0, 0)),
        out_shape=jax.ShapeDtypeStruct((total // size, vectors, size), out_dtype),
        scratch_shapes=[pltpu.VMEM((vectors, points), BF16)],
        compiler_params=pltpu.CompilerParams(vmem_limit_bytes=40 << 20),
        cost_estimate=pl.CostEstimate(
            flops=2 * points * total * 256,
            bytes_accessed=2 * points * total,
            transcendentals=0,
        ),
        name="apply",
    )(*operands)


def first_body(received_ref, targets_ref, start_ref, residual_ref, line_ref):
    product = jnp.sum(received_ref[...].astype(F32), axis=0)
    residual = targets_ref[...] - (start_ref[...] + product)
    residual_ref[...] = residual
    rounded = residual.astype(BF16)
    for n in range(line_ref.shape[0]):
        line_ref[n] = rounded


def sums_body(received_ref, residual_ref, product_ref, sums_ref):
    product = jnp.sum(received_ref[...].astype(F32), axis=0)
    product_ref[...] = product
    residual = residual_ref[...]
    vectors = residual.shape[0]
    one = jnp.sum(residual * residual, axis=1, keepdims=True)
    two = jnp.sum(residual * product, axis=1, keepdims=True)
    three = jnp.sum(product * product, axis=1, keepdims=True)
    lane = lax.broadcasted_iota(jnp.int32, (vectors, 128), 1)
    table = jnp.where(lane == 0, one, jnp.where(lane == 1, two, jnp.where(lane == 2, three, 0.0)))
    table = jnp.concatenate([table, jnp.zeros((128 - vectors, 128), F32)], axis=0).T[0:8, :]
    for n in range(sums_ref.shape[0]):
        sums_ref[n] = table


def spread_body(received_ref, sums_ref):
    table = jnp.sum(received_ref[...], axis=0)
    for n in range(sums_ref.shape[0]):
        sums_ref[n] = table


def total_body(received_ref, sums_ref):
    sums_ref[...] = jnp.sum(received_ref[...], axis=0)


def last_body(
    mine_ref, other_ref, start_ref, residual_ref, product_ref, solution_ref, new_ref, direction_ref
):
    vectors = start_ref.shape[0]
    table = mine_ref[...] + other_ref[...]
    table = jnp.concatenate([table, jnp.zeros((120, 128), F32)], axis=0).T[0:vectors, :]
    one, two, three = table[:, 0:1], table[:, 1:2], table[:, 2:3]
    alpha = one / (one + two)
    norm_new = alpha * alpha * jnp.maximum(three - two * two / one, 0.0)
    residual = residual_ref[...]
    image = residual + product_ref[...]
    solution_ref[...] = start_ref[...] + alpha * residual
    new = residual - alpha * image
    new_ref[...] = new
    direction_ref[...] = new + (norm_new / one) * residual


def per_device(features, groups, targets, start):
    width, size = features.shape
    vectors = start.shape[0]
    planes = lax.axis_size(PLANE)
    lines = lax.axis_size(LINE)
    cores = lax.axis_size("core")
    scale = scale_of(width)
    amplitude = AMP_NUM / math.sqrt(size * planes * lines * cores)
    gain = -math.log2(RHO) / scale
    gains = constant_pieces(gain)
    shift = 0.5 * (math.log2(amplitude) / scale - gain)
    shape = jax.ShapeDtypeStruct

    def across(value):
        return lax.ppermute(value, "core", [(0, 1), (1, 0)])

    plane, line = pl.pallas_call(
        functools.partial(pack_body, shift=shift),
        out_shape=[shape((planes, HEAD, size), BF16), shape((lines, HEAD + vectors, size), BF16)],
        name="pack",
    )(features, groups.reshape(1, size), start)
    line = lax.all_to_all(line, LINE, 0, 0)
    plane = lax.all_to_all(plane, PLANE, 0, 0)
    far_line = across(line)
    tile, carried = build(line, plane, None, scale, gains, F32)
    far_tile, partial_value = build(far_line, plane, carried, scale, gains, BF16)
    received = lax.all_to_all(partial_value, PLANE, 0, 0)

    residual0, line_vector = pl.pallas_call(
        first_body,
        out_shape=[shape((vectors, size), F32), shape((lines, vectors, size), BF16)],
        name="first",
    )(received, targets, start)
    line_vector = lax.all_to_all(line_vector, LINE, 0, 0)
    far_vector = across(line_vector)
    carried = apply(line_vector, tile, None, F32)
    partial_value = apply(far_vector, far_tile, carried, BF16)
    received = lax.all_to_all(partial_value, PLANE, 0, 0)

    product, sums = pl.pallas_call(
        sums_body,
        out_shape=[shape((vectors, size), F32), shape((planes, 8, 128), F32)],
        name="sums",
    )(received, residual0)
    sums = lax.all_to_all(sums, PLANE, 0, 0)
    sums = pl.pallas_call(
        spread_body, out_shape=shape((lines, 8, 128), F32), name="spread"
    )(sums)
    sums = lax.all_to_all(sums, LINE, 0, 0)
    sums = pl.pallas_call(total_body, out_shape=shape((8, 128), F32), name="total")(sums)
    other = across(sums)
    return tuple(
        pl.pallas_call(
            last_body, out_shape=[shape((vectors, size), F32)] * 3, name="last"
        )(sums, other, start, residual0, product)
    )


def solution(mesh):
    fine = Mesh(mesh.devices.reshape(2, 4, 2, 8, 2), AXES)
    split = ("yh", "z", "core", "yl", "x")
    in_specs = (P(None, split), P(split), P(None, split), P(None, split))
    out_specs = (P(None, split),) * 3
    return jax.shard_map(
        per_device, mesh=fine, in_specs=in_specs, out_specs=out_specs, check_vma=False
    )
```

time: 641 us -> 157 us (0.24)
  waiting for transfers between devices: 245 us -> 8.19 us
  blocking collectives: 237 us -> 81.3 us
  matrix products: 63 us -> 0 us
  starting transfers between devices: 71.8 us -> 17.4 us
  Pallas kernels: 0 us -> 48.2 us
  between operations: 14.2 us -> 0.66 us
    ppermute x128 -> x3, waiting for transfers between devices: 198 us -> 1.04 us  [across(): return lax.ppermute(value, 'core', [(0, 1), (1, 0)])]
    psum x2 -> x0, blocking collectives: 154 us -> none  [the longest x1 80.9 us: per_device(): norm_old = lax.psum(jnp.sum(residual0 * residual0, axis=1), ('row', 'col'))]
    all_gather x4 -> x0, blocking collectives: 82.3 us -> none  [the longest x2 44.1 us: apply_operator(): home_vector = lax.all_gather(rounded, 'row', axis=1, tiled=True)]
    all_to_all x0 -> x6, blocking collectives: none -> 81.3 us  [the longest x1 23.5 us: per_device(): line = lax.all_to_all(line, LINE, 0, 0)]
    dot_general x95 -> x0, matrix products: 63 us -> none  [the longest x31 37.4 us: kernel_tile(): lax.dot_general(home_features, piece_features, (((0,), (0,)), ((), ())),...]
    ppermute x128 -> x3, starting transfers between devices: 71.7 us -> 10.6 us  [across(): return lax.ppermute(value, 'core', [(0, 1), (1, 0)])]
    pallas_call x0 -> x10, Pallas kernels: none -> 48.2 us  [the longest x2 19.6 us: build(): pl.pallas_call(functools.partial(build_body, scale, gains, carried is not...]
    reduce_scatter x2 -> x0, waiting for transfers between devices: 46.8 us -> none  [apply_operator(): lax.psum_scatter(partial_value, 'row', scatter_dimension=1, tiled=True)]
  transfers between devices with their start and end apart: 130 -> 4, of which waited for: 64 -> 2; matrix products, arithmetic and copies ran while one was open for 8% -> 0% of each run, Pallas kernels for 0% -> 12%
where the time goes in v1:
time: 157 us; the launch traced here: 156 us
  blocking collectives  81.3 us (52%)
  Pallas kernels  48.2 us (31%)
  starting transfers between devices  17.4 us (11%)
  waiting for transfers between devices  8.19 us (5%)
    all_to_all x1, blocking collectives, per_device(): line = lax.all_to_all(line, LINE, 0, 0)  23.5 us
    all_to_all x2, blocking collectives, per_device(): received = lax.all_to_all(partial_value, PLANE, 0, 0)  22.6 us
    pallas_call x2, Pallas kernels, build(): pl.pallas_call(functools.partial(build_body, scale, gains, carried is not...  19.6 us
    pallas_call x2, Pallas kernels, apply(): pl.pallas_call(functools.partial(apply_body, carried is not None), grid=(...  18.7 us
    all_to_all x1, blocking collectives, per_device(): line_vector = lax.all_to_all(line_vector, LINE, 0, 0)  13.5 us
    all_to_all x1, blocking collectives, per_device(): sums = lax.all_to_all(sums, PLANE, 0, 0)  10.9 us
    all_to_all x1, blocking collectives, per_device(): sums = lax.all_to_all(sums, LINE, 0, 0)  10.8 us
    ppermute x3, starting transfers between devices, across(): return lax.ppermute(value, 'core', [(0, 1), (1, 0)])  10.6 us
  transfers between devices with their start and end apart: 4, of which 2 were waited for; matrix products, arithmetic and copies ran while one was open for 0% of the time, Pallas kernels for 12%

profile of v1, /device:TPU:1, one launch (start us, length us, event | category | flops | bytes accessed | tf_op | source)
XLA Modules:
  0.0 156.3 jit_solution(9693284997165886915)
XLA Ops:
  0.6 1.9 %pack.1 = (bf16[16,80,256]{2,1,0:T(8,128)(2,1)}, bf16[8,112,256]{2,1,0:T(8,128)(2,1)}) custom-call(bf16[64,256]{1,0:T(8,128)(2,1)} %features_ref.1, s32[1,256]{1,0:T(1,128)} %bitcast.1, f32[32,256]{1,0:T(8,128)} %start_ref.5), custom_call_target="tpu_custom_call" | custom-call | tf_op jit(solution)/shard_map/pack/pallas_call | solution.py:281
  2.5 23.5 %all_to_all.35.line_ref = bf16[8,112,256]{2,1,0:T(8,128)(2,1)S(1)} all-to-all(bf16[8,112,256]{2,1,0:T(8,128)(2,1)} %get-tuple-element.13), channel_id=1, replica_groups=mesh['yl'=2,'x'=4,'yh'=2,'z'=8,'core'=2] {'z'}, dimensions={0} | all-to-all | bytes 917504 | tf_op jit(solution)/shard_map/all_to_all | solution.py:286
  26.0 6.8 %all-to-all-start.1 = ((bf16[16,80,256]{2,1,0:T(8,128)(2,1)}), bf16[16,80,256]{2,1,0:T(8,128)(2,1)S(1)}, u32[]{:S(2)}, u32[]{:S(2)}) async-start(bf16[16,80,256]{2,1,0:T(8,128)(2,1)} %get-tuple-element.14), calls=%async_computation.1 | async-start | bytes 1310720 | tf_op jit(solution)/shard_map/all_to_all | solution.py:287
  32.8 2.9 %collective-permute-start = (bf16[8,112,256]{2,1,0:T(8,128)(2,1)S(1)}, bf16[8,112,256]{2,1,0:T(8,128)(2,1)S(1)}, u32[]{:S(2)}, u32[]{:S(2)}) collective-permute-start(bf16[8,112,256]{2,1,0:T(8,128)(2,1)S(1)} %all_to_all.35.line_ref), channel_id=1, source_target_pairs={{0,1},{1,0},{2,3},{3,2},{4,5},{5,4},{6,7},{7,6},{8,9},{9,8},{10,11... | collective-permute-start | bytes 1376264 | tf_op jit(solution)/shard_map/ppermute | solution.py:279
  35.7 7.2 %all-to-all-done.1.plane_ref = bf16[16,80,256]{2,1,0:T(8,128)(2,1)S(1)} async-done(((bf16[16,80,256]{2,1,0:T(8,128)(2,1)}), bf16[16,80,256]{2,1,0:T(8,128)(2,1)S(1)}, u32[]{:S(2)}, u32[]{:S(2)}) %all-to-all-start.1) | async-done | bytes 655392 | tf_op jit(solution)/shard_map/all_to_all | solution.py:287
  42.8 9.8 %build.2 = (bf16[2048,4096]{1,0:T(8,128)(2,1)}, f32[16,32,256]{2,1,0:T(8,128)S(1)}) custom-call(bf16[8,112,256]{2,1,0:T(8,128)(2,1)S(1)} %all_to_all.35.line_ref, bf16[16,80,256]{2,1,0:T(8,128)(2,1)S(1)} %all-to-all-done.1.plane_ref), custom_call_target="tpu_custom_call" | custom-call | flops 8589934592 | bytes 16777216 | tf_op jit(solution)/shard_map/build/pallas_call | solution.py:138
  52.6 0.0 collective-permute-done.line_ref
  52.6 9.8 %build.3 = (bf16[2048,4096]{1,0:T(8,128)(2,1)}, bf16[16,32,256]{2,1,0:T(8,128)(2,1)S(1)}) custom-call(bf16[8,112,256]{2,1,0:T(8,128)(2,1)S(1)} %collective-permute-done.line_ref, bf16[16,80,256]{2,1,0:T(8,128)(2,1)S(1)} %all-to-all-done.1.plane_ref, f32[16,32,256]{2,1,0:T(8,128)S(1)} %get-tuple-element.15.refs_0_), custom_call_target="tpu_custom_call" | custom-call | flops 8589934592 | bytes 16777216 | tf_op jit(solution)/shard_map/build/pallas_call | solution.py:138
  62.4 10.9 %all_to_all.36.received_ref = bf16[16,32,256]{2,1,0:T(8,128)(2,1)} all-to-all(bf16[16,32,256]{2,1,0:T(8,128)(2,1)S(1)} %get-tuple-element.16), channel_id=1, replica_groups=mesh['yl'=2,'x'=4,'yh'=2,'z'=8,'core'=2] {'yl','x','yh'}, dimensions={0} | all-to-all | bytes 524288 | tf_op jit(solution)/shard_map/all_to_all | solution.py:291
  73.3 1.7 %first.1 = (f32[32,256]{1,0:T(8,128)}, bf16[8,32,256]{2,1,0:T(8,128)(2,1)}) custom-call(bf16[16,32,256]{2,1,0:T(8,128)(2,1)} %all_to_all.36.received_ref, f32[32,256]{1,0:T(8,128)} %targets_ref.1, f32[32,256]{1,0:T(8,128)} %start_ref.5), custom_call_target="tpu_custom_call" | custom-call | tf_op jit(solution)/shard_map/first/pallas_call | solution.py:293
  75.0 13.5 %all_to_all.37.vector_ref = bf16[8,32,256]{2,1,0:T(8,128)(2,1)S(1)} all-to-all(bf16[8,32,256]{2,1,0:T(8,128)(2,1)} %get-tuple-element.17), channel_id=1, replica_groups=mesh['yl'=2,'x'=4,'yh'=2,'z'=8,'core'=2] {'z'}, dimensions={0} | all-to-all | bytes 262144 | tf_op jit(solution)/shard_map/all_to_all | solution.py:298
  88.5 4.2 %collective-permute-start.1 = (bf16[8,32,256]{2,1,0:T(8,128)(2,1)S(1)}, bf16[8,32,256]{2,1,0:T(8,128)(2,1)S(1)}, u32[]{:S(2)}, u32[]{:S(2)}) collective-permute-start(bf16[8,32,256]{2,1,0:T(8,128)(2,1)S(1)} %all_to_all.37.vector_ref), channel_id=1, source_target_pairs={{0,1},{1,0},{2,3},{3,2},{4,5},{5,4},{6,7},{7,6},{8,9},{9,8},{10,11... | collective-permute-start | bytes 393224 | tf_op jit(solution)/shard_map/ppermute | solution.py:279
  92.7 9.3 %apply.2.refs_0_ = f32[16,32,256]{2,1,0:T(8,128)S(1)} custom-call(bf16[8,32,256]{2,1,0:T(8,128)(2,1)S(1)} %all_to_all.37.vector_ref, bf16[2048,4096]{1,0:T(8,128)(2,1)} %get-tuple-element.19.tile_ref), custom_call_target="tpu_custom_call" | custom-call | flops 4294967296 | bytes 16777216 | tf_op jit(solution)/shard_map/apply/pallas_call | solution.py:197
  102.0 0.0 collective-permute-done.1.vector_ref
  102.1 9.3 %apply.3 = bf16[16,32,256]{2,1,0:T(8,128)(2,1)S(1)} custom-call(bf16[8,32,256]{2,1,0:T(8,128)(2,1)S(1)} %collective-permute-done.1.vector_ref, bf16[2048,4096]{1,0:T(8,128)(2,1)} %get-tuple-element.18.tile_ref, f32[16,32,256]{2,1,0:T(8,128)S(1)} %apply.2.refs_0_), custom_call_target="tpu_custom_call" | custom-call | flops 4294967296 | bytes 16777216 | tf_op jit(solution)/shard_map/apply/pallas_call | solution.py:197
  111.4 11.7 %all_to_all.38.received_ref = bf16[16,32,256]{2,1,0:T(8,128)(2,1)} all-to-all(bf16[16,32,256]{2,1,0:T(8,128)(2,1)S(1)} %apply.3), channel_id=1, replica_groups=mesh['yl'=2,'x'=4,'yh'=2,'z'=8,'core'=2] {'yl','x','yh'}, dimensions={0} | all-to-all | bytes 524288 | tf_op jit(solution)/shard_map/all_to_all | solution.py:302
  123.1 1.8 %sums.1 = (f32[32,256]{1,0:T(8,128)}, f32[16,8,128]{2,1,0:T(8,128)}) custom-call(bf16[16,32,256]{2,1,0:T(8,128)(2,1)} %all_to_all.38.received_ref, f32[32,256]{1,0:T(8,128)} %get-tuple-element.20.residual_ref), custom_call_target="tpu_custom_call" | custom-call | tf_op jit(solution)/shard_map/sums/pallas_call | solution.py:304
  124.9 10.9 %all_to_all.39.received_ref = f32[16,8,128]{2,1,0:T(8,128)} all-to-all(f32[16,8,128]{2,1,0:T(8,128)} %get-tuple-element.21), channel_id=1, replica_groups=mesh['yl'=2,'x'=4,'yh'=2,'z'=8,'core'=2] {'yl','x','yh'}, dimensions={0} | all-to-all | bytes 131072 | tf_op jit(solution)/shard_map/all_to_all | solution.py:309
  135.7 1.5 spread.1
  137.2 10.8 %all_to_all.40.received_ref = f32[8,8,128]{2,1,0:T(8,128)} all-to-all(f32[8,8,128]{2,1,0:T(8,128)} %spread.1), channel_id=1, replica_groups=mesh['yl'=2,'x'=4,'yh'=2,'z'=8,'core'=2] {'z'}, dimensions={0} | all-to-all | bytes 65536 | tf_op jit(solution)/shard_map/all_to_all | solution.py:313
  148.0 1.4 total.1.mine_ref
  149.4 3.5 %collective-permute-start.2 = (f32[8,128]{1,0:T(8,128)}, f32[8,128]{1,0:T(8,128)S(1)}, u32[]{:S(2)}, u32[]{:S(2)}) collective-permute-start(f32[8,128]{1,0:T(8,128)} %total.1.mine_ref), channel_id=1, source_target_pairs={{0,1},{1,0},{2,3},{3,2},{4,5},{5,4},{6,7},{7,6},{8,9},{9,8},{10,11... | collective-permute-start | bytes 12296 | tf_op jit(solution)/shard_map/ppermute | solution.py:279
  152.9 1.0 collective-permute-done.2.other_ref
  153.9 0.0 copy-start
  153.9 0.6 copy-done
  154.5 1.8 %last.1 = (f32[32,256]{1,0:T(8,128)}, f32[32,256]{1,0:T(8,128)}, f32[32,256]{1,0:T(8,128)}) custom-call(f32[8,128]{1,0:T(8,128)} %total.1.mine_ref, f32[8,128]{1,0:T(8,128)} %copy-done, f32[32,256]{1,0:T(8,128)} %start_ref.5, f32[32,256]{1,0:T(8,128)} %get-tuple-element.20.residual_ref, f32[32,256]{1,0:T(8,128)} %get-tuple-element.22.product_ref), custom_call_target="tpu_custom_call" | custom-call | tf_op jit(solution)/shard_map/last/pallas_call | solution.py:317
Async XLA Ops:
  26.0 16.8 %all-to-all-start.1 = ((bf16[16,80,256]{2,1,0:T(8,128)(2,1)}), bf16[16,80,256]{2,1,0:T(8,128)(2,1)S(1)}, u32[]{:S(2)}, u32[]{:S(2)}) async-start(bf16[16,80,256]{2,1,0:T(8,128)(2,1)} %get-tuple-element.14), calls=%async_computation.1 | async-start | bytes 1310720 | tf_op jit(solution)/shard_map/all_to_all | solution.py:287
  32.8 19.9 %collective-permute-start = (bf16[8,112,256]{2,1,0:T(8,128)(2,1)S(1)}, bf16[8,112,256]{2,1,0:T(8,128)(2,1)S(1)}, u32[]{:S(2)}, u32[]{:S(2)}) collective-permute-start(bf16[8,112,256]{2,1,0:T(8,128)(2,1)S(1)} %all_to_all.35.line_ref), channel_id=1, source_target_pairs={{0,1},{1,0},{2,3},{3,2},{4,5},{5,4},{6,7},{7,6},{8,9},{9,8},{10,11... | collective-permute-start | bytes 1376264 | tf_op jit(solution)/shard_map/ppermute | solution.py:279
  88.5 13.5 %collective-permute-start.1 = (bf16[8,32,256]{2,1,0:T(8,128)(2,1)S(1)}, bf16[8,32,256]{2,1,0:T(8,128)(2,1)S(1)}, u32[]{:S(2)}, u32[]{:S(2)}) collective-permute-start(bf16[8,32,256]{2,1,0:T(8,128)(2,1)S(1)} %all_to_all.37.vector_ref), channel_id=1, source_target_pairs={{0,1},{1,0},{2,3},{3,2},{4,5},{5,4},{6,7},{7,6},{8,9},{9,8},{10,11... | collective-permute-start | bytes 393224 | tf_op jit(solution)/shard_map/ppermute | solution.py:279
  149.4 4.6 %collective-permute-start.2 = (f32[8,128]{1,0:T(8,128)}, f32[8,128]{1,0:T(8,128)S(1)}, u32[]{:S(2)}, u32[]{:S(2)}) collective-permute-start(f32[8,128]{1,0:T(8,128)} %total.1.mine_ref), channel_id=1, source_target_pairs={{0,1},{1,0},{2,3},{3,2},{4,5},{5,4},{6,7},{7,6},{8,9},{9,8},{10,11... | collective-permute-start | bytes 12296 | tf_op jit(solution)/shard_map/ppermute | solution.py:279
  153.9 0.6 copy-start

commit v2 on v1

v2 whole, which is shorter than its diff:
```python
import functools
import math

import jax
import jax.numpy as jnp
from jax import lax
from jax.experimental import pallas as pl
from jax.experimental.pallas import tpu as pltpu
from jax.sharding import Mesh, PartitionSpec as P

RHO = 0.2
AMP_NUM = 16.0

AXES = ("yl", "x", "yh", "z", "core")
ROW = ("yl", "x")
COL = ("yh", "z", "core")
LINE = ("z",)

BF16 = jnp.bfloat16
F32 = jnp.float32
VMEM = pl.BlockSpec(memory_space=pltpu.VMEM)

HEAD = 80
DEPTH = 128
WIDE = 512


def scale_of(width):
    return 2.0 * math.log2(math.e) / width


def pieces_of(value):
    first = value.astype(BF16).astype(F32)
    rest = value - first
    second = rest.astype(BF16).astype(F32)
    return first, second, rest - second


def constant_pieces(value):
    import numpy as np
    import ml_dtypes

    out = []
    rest = value
    for _ in range(3):
        piece = float(np.float32(rest).astype(ml_dtypes.bfloat16))
        out.append(piece)
        rest = rest - piece
    return out


def pack_body(features_ref, groups_ref, start_ref, plane_ref, line_ref, *, shift):
    features = features_ref[...]
    wide = features.astype(F32)
    half = shift - 0.5 * jnp.sum(wide * wide, axis=0, keepdims=True)
    first, second, third = pieces_of(half)
    group = groups_ref[...].astype(F32)
    count = features.shape[1]
    row = lax.broadcasted_iota(jnp.int32, (16, count), 0)
    tail = jnp.where(row == 0, first, 0.0)
    tail = jnp.where(row == 1, second, tail)
    tail = jnp.where(row == 2, third, tail)
    tail = jnp.where(row == 3, group, tail).astype(BF16)
    vector = start_ref[...].astype(BF16)
    for n in range(plane_ref.shape[0]):
        plane_ref[n, 0:64, :] = features
        plane_ref[n, 64:80, :] = tail
    for n in range(line_ref.shape[0]):
        line_ref[n, 0:64, :] = features
        line_ref[n, 64:80, :] = tail
        line_ref[n, 80:112, :] = vector


def tail_rows(packed, left, gains):
    count = packed.shape[1]
    head = packed.astype(F32)
    first, second, third, group = (head[n : n + 1, :] for n in range(4))
    row = lax.broadcasted_iota(jnp.int32, (64, count), 0)
    level = (row & 7).astype(F32)
    hot = jnp.where(level == group, 1.0, 0.0)
    if not left:
        hot = hot * jnp.where(row < 16, gains[0], jnp.where(row < 24, gains[1], gains[2]))
    out = jnp.where((row >= 8) & (row < 32), hot, 0.0)
    base = 0 if left else 3
    out = jnp.where((row >= 3 - base) & (row < 6 - base), 1.0, out)
    out = jnp.where(row == base, first, out)
    out = jnp.where(row == base + 1, second, out)
    out = jnp.where(row == base + 2, third, out)
    return out.astype(BF16)


def build_body(scale, gains, line_ref, plane_ref, carried_ref, tile_ref, out_ref, *scratch):
    left_ref, vector_ref, right_ref = scratch
    blocks, _, size = line_ref.shape
    per = WIDE // size
    for n in range(blocks):
        rows = line_ref[n, 0:64, :]
        tail = tail_rows(line_ref[n, 64:80, :], True, gains)
        left_ref[n * size : (n + 1) * size, :] = jnp.concatenate([rows, tail], axis=0).T
        vector_ref[:, n * size : (n + 1) * size] = line_ref[n, 80:112, :]

    def step(turn, state):
        columns = pl.ds(pl.multiple_of(turn * WIDE, WIDE), WIDE)
        for n in range(per):
            block = turn * per + n
            right_ref[0:64, n * size : (n + 1) * size] = plane_ref[block, 0:64, :]
            right_ref[64:128, n * size : (n + 1) * size] = tail_rows(
                plane_ref[block, 64:80, :], False, gains
            )
        right = right_ref[...]
        for n in range(blocks):
            power = jnp.dot(
                left_ref[n * size : (n + 1) * size, :], right, preferred_element_type=F32
            )
            tile_ref[n * size : (n + 1) * size, columns] = jnp.exp2(power * scale).astype(BF16)
        product = jnp.dot(
            vector_ref[...], tile_ref[:, columns], preferred_element_type=F32
        )
        for n in range(per):
            block = turn * per + n
            value = carried_ref[block] + product[:, n * size : (n + 1) * size]
            out_ref[block] = value.astype(out_ref.dtype)
        return state

    lax.fori_loop(0, plane_ref.shape[0] // per, step, 0)


def start_body(scale, gains, line_ref, plane_ref, tile_ref, out_ref, *scratch):
    out_ref[...] = jnp.zeros_like(out_ref)
    build_body(scale, gains, line_ref, plane_ref, out_ref, tile_ref, out_ref, *scratch)


def build(line, plane, carried, scale, gains, out_dtype):
    blocks, rows, size = line.shape
    columns = plane.shape[0]
    vectors = rows - HEAD
    points = blocks * size
    body = start_body if carried is None else build_body
    operands = [line, plane] + ([] if carried is None else [carried])
    return pl.pallas_call(
        functools.partial(body, scale, gains),
        in_specs=[VMEM] * len(operands),
        out_specs=[VMEM] * 2,
        out_shape=[
            pltpu.VMEM((points, columns * size), BF16),
            pltpu.VMEM((columns, vectors, size), out_dtype),
        ],
        scratch_shapes=[
            pltpu.VMEM((points, DEPTH), BF16),
            pltpu.VMEM((vectors, points), BF16),
            pltpu.VMEM((DEPTH, WIDE), BF16),
        ],
        compiler_params=pltpu.CompilerParams(vmem_limit_bytes=16 << 20),
        cost_estimate=pl.CostEstimate(
            flops=2 * points * columns * size * 512,
            bytes_accessed=2 * points * columns * size,
            transcendentals=points * columns * size,
        ),
        name="build",
    )(*operands)


def apply_body(vector_ref, tile_ref, *refs):
    out_ref, flat_ref = refs[-2:]
    blocks, _, size = vector_ref.shape
    for n in range(blocks):
        flat_ref[:, n * size : (n + 1) * size] = vector_ref[n]
    product = jnp.dot(flat_ref[...], tile_ref[...], preferred_element_type=F32)
    for n in range(out_ref.shape[0]):
        value = product[:, n * size : (n + 1) * size]
        if len(refs) == 3:
            value = value + refs[0][n]
        out_ref[n] = value.astype(out_ref.dtype)


def apply(vector, tile, carried, out_dtype):
    blocks, vectors, size = vector.shape
    points, total = tile.shape
    operands = [vector, tile] + ([] if carried is None else [carried])
    return pl.pallas_call(
        apply_body,
        in_specs=[VMEM] * len(operands),
        out_specs=VMEM,
        out_shape=pltpu.VMEM((total // size, vectors, size), out_dtype),
        scratch_shapes=[pltpu.VMEM((vectors, points), BF16)],
        compiler_params=pltpu.CompilerParams(vmem_limit_bytes=8 << 20),
        cost_estimate=pl.CostEstimate(
            flops=2 * points * total * 256,
            bytes_accessed=2 * points * total,
            transcendentals=0,
        ),
        name="apply",
    )(*operands)


def first_body(received_ref, targets_ref, start_ref, residual_ref, line_ref):
    product = jnp.sum(received_ref[...].astype(F32), axis=0)
    residual = targets_ref[...] - (start_ref[...] + product)
    residual_ref[...] = residual
    rounded = residual.astype(BF16)
    for n in range(line_ref.shape[0]):
        line_ref[n] = rounded


def sums_body(received_ref, residual_ref, product_ref, sums_ref):
    product = jnp.sum(received_ref[...].astype(F32), axis=0)
    product_ref[...] = product
    residual = residual_ref[...]
    vectors = residual.shape[0]
    one = jnp.sum(residual * residual, axis=1, keepdims=True)
    two = jnp.sum(residual * product, axis=1, keepdims=True)
    three = jnp.sum(product * product, axis=1, keepdims=True)
    lane = lax.broadcasted_iota(jnp.int32, (vectors, 128), 1)
    table = jnp.where(lane == 0, one, jnp.where(lane == 1, two, jnp.where(lane == 2, three, 0.0)))
    table = jnp.concatenate([table, jnp.zeros((128 - vectors, 128), F32)], axis=0).T[0:8, :]
    for n in range(sums_ref.shape[0]):
        sums_ref[n] = table


def spread_body(received_ref, sums_ref):
    table = jnp.sum(received_ref[...], axis=0)
    for n in range(sums_ref.shape[0]):
        sums_ref[n] = table


def last_body(
    received_ref, start_ref, residual_ref, product_ref, solution_ref, new_ref, direction_ref
):
    vectors = start_ref.shape[0]
    table = jnp.sum(received_ref[...], axis=0)
    table = jnp.concatenate([table, jnp.zeros((120, 128), F32)], axis=0).T[0:vectors, :]
    one, two, three = table[:, 0:1], table[:, 1:2], table[:, 2:3]
    alpha = one / (one + two)
    norm_new = alpha * alpha * jnp.maximum(three - two * two / one, 0.0)
    residual = residual_ref[...]
    image = residual + product_ref[...]
    solution_ref[...] = start_ref[...] + alpha * residual
    new = residual - alpha * image
    new_ref[...] = new
    direction_ref[...] = new + (norm_new / one) * residual


def small(body, name, outs, operands):
    return pl.pallas_call(
        body,
        in_specs=[VMEM] * len(operands),
        out_specs=[VMEM] * len(outs),
        out_shape=outs,
        compiler_params=pltpu.CompilerParams(vmem_limit_bytes=4 << 20),
        name=name,
    )(*operands)


def per_device(features, groups, targets, start):
    width, size = features.shape
    vectors = start.shape[0]
    rows = lax.axis_size(ROW)
    lines = lax.axis_size(LINE)
    columns = lax.axis_size(COL)
    scale = scale_of(width)
    amplitude = AMP_NUM / math.sqrt(size * rows * columns)
    gain = -math.log2(RHO) / scale
    gains = constant_pieces(gain)
    shift = 0.5 * (math.log2(amplitude) / scale - gain)

    def across(value, axis):
        return lax.ppermute(value, axis, [(0, 1), (1, 0)])

    plane, line = small(
        functools.partial(pack_body, shift=shift),
        "pack",
        [pltpu.VMEM((rows, HEAD, size), BF16), pltpu.VMEM((lines, HEAD + vectors, size), BF16)],
        [features, groups.reshape(1, size), start],
    )
    line = lax.all_to_all(line, LINE, 0, 0)
    far = across(line, "yh")
    near = across(line, "core")
    plane = lax.all_to_all(plane, ROW, 0, 0)
    tiles = [None] * 4
    tiles[0], carried = build(line, plane, None, scale, gains, F32)
    tiles[1], carried = build(near, plane, carried, scale, gains, F32)
    far, carried = lax.optimization_barrier((far, carried))
    last = across(far, "core")
    tiles[2], carried = build(far, plane, carried, scale, gains, F32)
    tiles[3], partial_value = build(last, plane, carried, scale, gains, BF16)
    received = lax.all_to_all(partial_value, ROW, 0, 0)

    residual0, vector = small(
        first_body,
        "first",
        [pltpu.VMEM((vectors, size), F32), pltpu.VMEM((lines, vectors, size), BF16)],
        [received, targets, start],
    )
    vector = lax.all_to_all(vector, LINE, 0, 0)
    far = across(vector, "yh")
    near = across(vector, "core")
    carried = apply(vector, tiles[0], None, F32)
    carried = apply(near, tiles[1], carried, F32)
    far, carried = lax.optimization_barrier((far, carried))
    last = across(far, "core")
    carried = apply(far, tiles[2], carried, F32)
    partial_value = apply(last, tiles[3], carried, BF16)
    received = lax.all_to_all(partial_value, ROW, 0, 0)

    product, sums = small(
        sums_body,
        "sums",
        [pltpu.VMEM((vectors, size), F32), pltpu.VMEM((rows, 8, 128), F32)],
        [received, residual0],
    )
    sums = lax.all_to_all(sums, ROW, 0, 0)
    (sums,) = small(spread_body, "spread", [pltpu.VMEM((columns, 8, 128), F32)], [sums])
    sums = lax.all_to_all(sums, COL, 0, 0)
    return tuple(
        small(
            last_body,
            "last",
            [jax.ShapeDtypeStruct((vectors, size), F32)] * 3,
            [sums, start, residual0, product],
        )
    )


def solution(mesh):
    fine = Mesh(mesh.devices.reshape(2, 4, 2, 8, 2), AXES)
    split = ("yh", "z", "core", "yl", "x")
    in_specs = (P(None, split), P(split), P(None, split), P(None, split))
    out_specs = (P(None, split),) * 3
    return jax.shard_map(
        per_device, mesh=fine, in_specs=in_specs, out_specs=out_specs, check_vma=False
    )
```

time: 157 us -> 126 us (0.80)
  Pallas kernels: 48.2 us -> 25 us
  blocking collectives: 81.3 us -> 74.5 us
  local copies, waits for them, and re-layouts: 0.59 us -> 2.2 us
    pallas_call x10 -> x13, Pallas kernels: 48.2 us -> 25 us  [the longest x4 16.9 us: build(): pl.pallas_call(functools.partial(body, scale, gains), in_specs=[VMEM] * l...]
    all_to_all x5, blocking collectives: 57.8 us -> 51.2 us  [the longest x2 17 us: per_device(): received = lax.all_to_all(partial_value, ROW, 0, 0)]
    all_to_all x1, waiting for transfers between devices: 7.15 us -> 1.08 us  [per_device(): plane = lax.all_to_all(plane, ROW, 0, 0)]
    ppermute x3 -> x6, waiting for transfers between devices: 1.04 us -> 6.06 us  [across(): return lax.ppermute(value, axis, [(0, 1), (1, 0)])]
    all_to_all x1, starting transfers between devices: 6.76 us -> 5.03 us  [per_device(): plane = lax.all_to_all(plane, ROW, 0, 0)]
    unnamed x2 -> x10, local copies, waits for them, and re-layouts: 0.59 us -> 2.2 us
    ppermute x3 -> x6, starting transfers between devices: 10.6 us -> 11.2 us  [across(): return lax.ppermute(value, axis, [(0, 1), (1, 0)])]
  transfers between devices with their start and end apart: 4 -> 7, of which waited for: 2 -> 3; matrix products, arithmetic and copies ran while one was open for 0% -> 0% of each run, Pallas kernels for 12% -> 14%
where the time goes in v2:
time: 126 us
  blocking collectives  74.5 us (59%)
  Pallas kernels  25 us (20%)
  starting transfers between devices  16.2 us (13%)
  waiting for transfers between devices  7.14 us (6%)
  local copies, waits for them, and re-layouts  2.2 us (2%)
    all_to_all x1, blocking collectives, per_device(): line = lax.all_to_all(line, LINE, 0, 0)  23.3 us
    all_to_all x2, blocking collectives, per_device(): received = lax.all_to_all(partial_value, ROW, 0, 0)  17 us
    pallas_call x4, Pallas kernels, build(): pl.pallas_call(functools.partial(body, scale, gains), in_specs=[VMEM] * l...  16.9 us
    all_to_all x1, blocking collectives, per_device(): sums = lax.all_to_all(sums, COL, 0, 0)  16 us
    ppermute x6, starting transfers between devices, across(): return lax.ppermute(value, axis, [(0, 1), (1, 0)])  11.2 us
    all_to_all x1, blocking collectives, per_device(): vector = lax.all_to_all(vector, LINE, 0, 0)  10.4 us
    all_to_all x1, blocking collectives, per_device(): sums = lax.all_to_all(sums, ROW, 0, 0)  7.77 us
    pallas_call x4, Pallas kernels, apply(): pl.pallas_call(apply_body, in_specs=[VMEM] * len(operands), out_specs=VME...  6.11 us
  transfers between devices with their start and end apart: 7, of which 3 were waited for; matrix products, arithmetic and copies ran while one was open for 0% of the time, Pallas kernels for 14%

profile of v2, /device:TPU:1, one launch (start us, length us, event | category | flops | bytes accessed | tf_op | source)
XLA Modules:
  0.0 125.8 jit_solution(12102410566593440462)
XLA Ops:
  0.6 0.0 copy-start
  0.6 0.7 copy-done
  1.4 0.0 copy-start.2
  1.4 0.8 copy-done.2
  2.1 0.0 copy-start.4
  2.2 0.7 copy-done.4
  2.8 0.8 pack.1
  3.6 23.3 %all_to_all.35.line_ref = bf16[8,112,256]{2,1,0:T(8,128)(2,1)S(1)} all-to-all(bf16[8,112,256]{2,1,0:T(8,128)(2,1)S(1)} %get-tuple-element.21), channel_id=1, replica_groups=mesh['yl'=2,'x'=4,'yh'=2,'z'=8,'core'=2] {'z'}, dimensions={0} | all-to-all | bytes 917504 | tf_op jit(solution)/shard_map/all_to_all | solution.py:275
  26.9 5.0 %all-to-all-start.1 = ((bf16[8,80,256]{2,1,0:T(8,128)(2,1)}), bf16[8,80,256]{2,1,0:T(8,128)(2,1)S(1)}, u32[]{:S(2)}, u32[]{:S(2)}) async-start(bf16[8,80,256]{2,1,0:T(8,128)(2,1)} %get-tuple-element.22), calls=%async_computation.1 | async-start | bytes 655360 | tf_op jit(solution)/shard_map/all_to_all | solution.py:278
  32.0 2.8 %collective-permute-start.1 = (bf16[8,112,256]{2,1,0:T(8,128)(2,1)S(1)}, bf16[8,112,256]{2,1,0:T(8,128)(2,1)S(1)}, u32[]{:S(2)}, u32[]{:S(2)}) collective-permute-start(bf16[8,112,256]{2,1,0:T(8,128)(2,1)S(1)} %all_to_all.35.line_ref), channel_id=1, source_target_pairs={{0,1},{1,0},{2,3},{3,2},{4,5},{5,4},{6,7},{7,6},{8,9},{9,8},{10,11... | collective-permute-start | bytes 1376264 | tf_op jit(solution)/shard_map/ppermute | solution.py:267
  34.8 2.6 %collective-permute-start = (bf16[8,112,256]{2,1,0:T(8,128)(2,1)S(1)}, bf16[8,112,256]{2,1,0:T(8,128)(2,1)S(1)}, u32[]{:S(2)}, u32[]{:S(2)}) collective-permute-start(bf16[8,112,256]{2,1,0:T(8,128)(2,1)S(1)} %all_to_all.35.line_ref), channel_id=1, source_target_pairs={{0,16},{16,0},{1,17},{17,1},{2,18},{18,2},{3,19},{19,3},{4,20},{20... | collective-permute-start | bytes 1376264 | tf_op jit(solution)/shard_map/ppermute | solution.py:267
  37.4 1.1 all-to-all-done.1.plane_ref
  38.5 4.2 %build.4 = (bf16[2048,2048]{1,0:T(8,128)(2,1)S(1)}, f32[8,32,256]{2,1,0:T(8,128)S(1)}) custom-call(bf16[8,112,256]{2,1,0:T(8,128)(2,1)S(1)} %all_to_all.35.line_ref, bf16[8,80,256]{2,1,0:T(8,128)(2,1)S(1)} %all-to-all-done.1.plane_ref), custom_call_target="tpu_custom_call" | custom-call | flops 4294967296 | bytes 8388608 | tf_op jit(solution)/shard_map/build/pallas_call | solution.py:140
  42.7 0.0 collective-permute-done.1.line_ref
  42.7 4.2 %build.5 = (bf16[2048,2048]{1,0:T(8,128)(2,1)S(1)}, f32[8,32,256]{2,1,0:T(8,128)S(1)}) custom-call(bf16[8,112,256]{2,1,0:T(8,128)(2,1)S(1)} %collective-permute-done.1.line_ref, bf16[8,80,256]{2,1,0:T(8,128)(2,1)S(1)} %all-to-all-done.1.plane_ref, f32[8,32,256]{2,1,0:T(8,128)S(1)} %get-tuple-element.23.carried_ref), custom_call_target="tpu_custom_call" | custom-call | flops 4294967296 | bytes 8388608 | tf_op jit(solution)/shard_map/build/pallas_call | solution.py:140
  47.0 4.0 %collective-permute-done.line_ref = bf16[8,112,256]{2,1,0:T(8,128)(2,1)S(1)} collective-permute-done((bf16[8,112,256]{2,1,0:T(8,128)(2,1)S(1)}, bf16[8,112,256]{2,1,0:T(8,128)(2,1)S(1)}, u32[]{:S(2)}, u32[]{:S(2)}) %collective-permute-start) | collective-permute-done | bytes 458784 | tf_op jit(solution)/shard_map/ppermute | solution.py:267
  51.0 0.9 collective-permute-start.2
  51.9 4.2 %build.6 = (bf16[2048,2048]{1,0:T(8,128)(2,1)S(1)}, f32[8,32,256]{2,1,0:T(8,128)S(1)}) custom-call(bf16[8,112,256]{2,1,0:T(8,128)(2,1)S(1)} %collective-permute-done.line_ref, bf16[8,80,256]{2,1,0:T(8,128)(2,1)S(1)} %all-to-all-done.1.plane_ref, f32[8,32,256]{2,1,0:T(8,128)S(1)} %get-tuple-element.26.carried_ref), custom_call_target="tpu_custom_call" | custom-call | flops 4294967296 | bytes 8388608 | tf_op jit(solution)/shard_map/build/pallas_call | solution.py:140
  56.1 0.0 copy-start.1
  56.1 0.0 copy-start.3
  56.1 0.0 collective-permute-done.2.line_ref
  56.1 4.2 %build.7 = (bf16[2048,2048]{1,0:T(8,128)(2,1)S(1)}, bf16[8,32,256]{2,1,0:T(8,128)(2,1)S(1)}) custom-call(bf16[8,112,256]{2,1,0:T(8,128)(2,1)S(1)} %collective-permute-done.2.line_ref, bf16[8,80,256]{2,1,0:T(8,128)(2,1)S(1)} %all-to-all-done.1.plane_ref, f32[8,32,256]{2,1,0:T(8,128)S(1)} %get-tuple-element.27.carried_ref), custom_call_target="tpu_custom_call" | custom-call | flops 4294967296 | bytes 8388608 | tf_op jit(solution)/shard_map/build/pallas_call | solution.py:140
  60.4 9.2 %all_to_all.36.received_ref = bf16[8,32,256]{2,1,0:T(8,128)(2,1)S(1)} all-to-all(bf16[8,32,256]{2,1,0:T(8,128)(2,1)S(1)} %get-tuple-element.28), channel_id=1, replica_groups=mesh['yl'=2,'x'=4,'yh'=2,'z'=8,'core'=2] {'yl','x'}, dimensions={0} | all-to-all | bytes 262144 | tf_op jit(solution)/shard_map/all_to_all | solution.py:286
  69.6 0.0 copy-done.1
  69.6 0.0 copy-done.3
  69.6 10.4 %all_to_all.37.vector_ref = bf16[8,32,256]{2,1,0:T(8,128)(2,1)S(1)} all-to-all(bf16[8,32,256]{2,1,0:T(8,128)(2,1)S(1)} %get-tuple-element.29), channel_id=1, replica_groups=mesh['yl'=2,'x'=4,'yh'=2,'z'=8,'core'=2] {'z'}, dimensions={0} | all-to-all | bytes 262144 | tf_op jit(solution)/shard_map/all_to_all | solution.py:294
  80.0 2.5 %collective-permute-start.4 = (bf16[8,32,256]{2,1,0:T(8,128)(2,1)S(1)}, bf16[8,32,256]{2,1,0:T(8,128)(2,1)S(1)}, u32[]{:S(2)}, u32[]{:S(2)}) collective-permute-start(bf16[8,32,256]{2,1,0:T(8,128)(2,1)S(1)} %all_to_all.37.vector_ref), channel_id=1, source_target_pairs={{0,1},{1,0},{2,3},{3,2},{4,5},{5,4},{6,7},{7,6},{8,9},{9,8},{10,11... | collective-permute-start | bytes 393224 | tf_op jit(solution)/shard_map/ppermute | solution.py:267
  82.5 1.6 %collective-permute-start.3 = (bf16[8,32,256]{2,1,0:T(8,128)(2,1)S(1)}, bf16[8,32,256]{2,1,0:T(8,128)(2,1)S(1)}, u32[]{:S(2)}, u32[]{:S(2)}) collective-permute-start(bf16[8,32,256]{2,1,0:T(8,128)(2,1)S(1)} %all_to_all.37.vector_ref), channel_id=1, source_target_pairs={{0,16},{16,0},{1,17},{17,1},{2,18},{18,2},{3,19},{19,3},{4,20},{20... | collective-permute-start | bytes 393224 | tf_op jit(solution)/shard_map/ppermute | solution.py:267
  84.1 1.5 %apply.4.refs_0_ = f32[8,32,256]{2,1,0:T(8,128)S(1)} custom-call(bf16[8,32,256]{2,1,0:T(8,128)(2,1)S(1)} %all_to_all.37.vector_ref, bf16[2048,2048]{1,0:T(8,128)(2,1)S(1)} %get-tuple-element.31.tile_ref), custom_call_target="tpu_custom_call" | custom-call | flops 2147483648 | bytes 8388608 | tf_op jit(solution)/shard_map/apply/pallas_call | solution.py:180
  85.6 0.0 collective-permute-done.4.vector_ref
  85.6 1.5 %apply.5.refs_0_ = f32[8,32,256]{2,1,0:T(8,128)S(1)} custom-call(bf16[8,32,256]{2,1,0:T(8,128)(2,1)S(1)} %collective-permute-done.4.vector_ref, bf16[2048,2048]{1,0:T(8,128)(2,1)S(1)} %get-tuple-element.30.tile_ref, f32[8,32,256]{2,1,0:T(8,128)S(1)} %apply.4.refs_0_), custom_call_target="tpu_custom_call" | custom-call | flops 2147483648 | bytes 8388608 | tf_op jit(solution)/shard_map/apply/pallas_call | solution.py:180
  87.1 2.0 %collective-permute-done.3.vector_ref = bf16[8,32,256]{2,1,0:T(8,128)(2,1)S(1)} collective-permute-done((bf16[8,32,256]{2,1,0:T(8,128)(2,1)S(1)}, bf16[8,32,256]{2,1,0:T(8,128)(2,1)S(1)}, u32[]{:S(2)}, u32[]{:S(2)}) %collective-permute-start.3) | collective-permute-done | bytes 131104 | tf_op jit(solution)/shard_map/ppermute | solution.py:267
  89.1 0.8 collective-permute-start.5
  89.9 1.5 %apply.6.refs_0_ = f32[8,32,256]{2,1,0:T(8,128)S(1)} custom-call(bf16[8,32,256]{2,1,0:T(8,128)(2,1)S(1)} %collective-permute-done.3.vector_ref, bf16[2048,2048]{1,0:T(8,128)(2,1)S(1)} %get-tuple-element.34.tile_ref, f32[8,32,256]{2,1,0:T(8,128)S(1)} %apply.5.refs_0_), custom_call_target="tpu_custom_call" | custom-call | flops 2147483648 | bytes 8388608 | tf_op jit(solution)/shard_map/apply/pallas_call | solution.py:180
  91.5 0.0 collective-permute-done.5.vector_ref
  91.5 1.5 %apply.7 = bf16[8,32,256]{2,1,0:T(8,128)(2,1)S(1)} custom-call(bf16[8,32,256]{2,1,0:T(8,128)(2,1)S(1)} %collective-permute-done.5.vector_ref, bf16[2048,2048]{1,0:T(8,128)(2,1)S(1)} %get-tuple-element.33.tile_ref, f32[8,32,256]{2,1,0:T(8,128)S(1)} %apply.6.refs_0_), custom_call_target="tpu_custom_call" | custom-call | flops 2147483648 | bytes 8388608 | tf_op jit(solution)/shard_map/apply/pallas_call | solution.py:180
  93.0 7.8 %all_to_all.38.received_ref = bf16[8,32,256]{2,1,0:T(8,128)(2,1)S(1)} all-to-all(bf16[8,32,256]{2,1,0:T(8,128)(2,1)S(1)} %apply.7), channel_id=1, replica_groups=mesh['yl'=2,'x'=4,'yh'=2,'z'=8,'core'=2] {'yl','x'}, dimensions={0} | all-to-all | bytes 262144 | tf_op jit(solution)/shard_map/all_to_all | solution.py:303
  100.8 0.2 sums.1
  101.0 7.8 %all_to_all.39.received_ref = f32[8,8,128]{2,1,0:T(8,128)S(1)} all-to-all(f32[8,8,128]{2,1,0:T(8,128)S(1)} %get-tuple-element.37), channel_id=1, replica_groups=mesh['yl'=2,'x'=4,'yh'=2,'z'=8,'core'=2] {'yl','x'}, dimensions={0} | all-to-all | bytes 65536 | tf_op jit(solution)/shard_map/all_to_all | solution.py:311
  108.8 16.0 %all_to_all.40.received_ref = f32[32,8,128]{2,1,0:T(8,128)S(1)} all-to-all(f32[32,8,128]{2,1,0:T(8,128)S(1)} %spread.1), channel_id=1, replica_groups=mesh['yl'=2,'x'=4,'yh'=2,'z'=8,'core'=2] {'yh','z','core'}, dimensions={0} | all-to-all | bytes 262144 | tf_op jit(solution)/shard_map/all_to_all | solution.py:313
  124.8 1.0 last.1
  (2 shorter events, 0.0 us)
Async XLA Ops:
  0.6 0.8 copy-start
  1.4 0.8 copy-start.2
  2.1 0.7 copy-start.4
  26.9 11.6 %all-to-all-start.1 = ((bf16[8,80,256]{2,1,0:T(8,128)(2,1)}), bf16[8,80,256]{2,1,0:T(8,128)(2,1)S(1)}, u32[]{:S(2)}, u32[]{:S(2)}) async-start(bf16[8,80,256]{2,1,0:T(8,128)(2,1)} %get-tuple-element.22), calls=%async_computation.1 | async-start | bytes 655360 | tf_op jit(solution)/shard_map/all_to_all | solution.py:278
  32.0 10.8 %collective-permute-start.1 = (bf16[8,112,256]{2,1,0:T(8,128)(2,1)S(1)}, bf16[8,112,256]{2,1,0:T(8,128)(2,1)S(1)}, u32[]{:S(2)}, u32[]{:S(2)}) collective-permute-start(bf16[8,112,256]{2,1,0:T(8,128)(2,1)S(1)} %all_to_all.35.line_ref), channel_id=1, source_target_pairs={{0,1},{1,0},{2,3},{3,2},{4,5},{5,4},{6,7},{7,6},{8,9},{9,8},{10,11... | collective-permute-start | bytes 1376264 | tf_op jit(solution)/shard_map/ppermute | solution.py:267
  34.8 16.2 %collective-permute-start = (bf16[8,112,256]{2,1,0:T(8,128)(2,1)S(1)}, bf16[8,112,256]{2,1,0:T(8,128)(2,1)S(1)}, u32[]{:S(2)}, u32[]{:S(2)}) collective-permute-start(bf16[8,112,256]{2,1,0:T(8,128)(2,1)S(1)} %all_to_all.35.line_ref), channel_id=1, source_target_pairs={{0,16},{16,0},{1,17},{17,1},{2,18},{18,2},{3,19},{19,3},{4,20},{20... | collective-permute-start | bytes 1376264 | tf_op jit(solution)/shard_map/ppermute | solution.py:267
  51.0 5.1 %collective-permute-start.2 = (bf16[8,112,256]{2,1,0:T(8,128)(2,1)S(1)}, bf16[8,112,256]{2,1,0:T(8,128)(2,1)S(1)}, u32[]{:S(2)}, u32[]{:S(2)}) collective-permute-start(bf16[8,112,256]{2,1,0:T(8,128)(2,1)S(1)} %collective-permute-done.line_ref), channel_id=1, source_target_pairs={{0,1},{1,0},{2,3},{3,2},{4,5},{5,4},{6,7},{7,6},{8,9},{9,8},{10,11... | collective-permute-start | bytes 1376264 | tf_op jit(solution)/shard_map/ppermute | solution.py:267
  56.1 13.5 %copy-start.1 = (f32[32,256]{1,0:T(8,128)S(1)}, f32[32,256]{1,0:T(8,128)}, u32[]{:S(2)}) copy-start(f32[32,256]{1,0:T(8,128)} %start_ref.5) | copy-start | bytes 98308
  56.1 13.4 %copy-start.3 = (f32[32,256]{1,0:T(8,128)S(1)}, f32[32,256]{1,0:T(8,128)}, u32[]{:S(2)}) copy-start(f32[32,256]{1,0:T(8,128)} %targets_ref.1) | copy-start | bytes 98308
  80.0 5.6 %collective-permute-start.4 = (bf16[8,32,256]{2,1,0:T(8,128)(2,1)S(1)}, bf16[8,32,256]{2,1,0:T(8,128)(2,1)S(1)}, u32[]{:S(2)}, u32[]{:S(2)}) collective-permute-start(bf16[8,32,256]{2,1,0:T(8,128)(2,1)S(1)} %all_to_all.37.vector_ref), channel_id=1, source_target_pairs={{0,1},{1,0},{2,3},{3,2},{4,5},{5,4},{6,7},{7,6},{8,9},{9,8},{10,11... | collective-permute-start | bytes 393224 | tf_op jit(solution)/shard_map/ppermute | solution.py:267
  82.5 6.6 %collective-permute-start.3 = (bf16[8,32,256]{2,1,0:T(8,128)(2,1)S(1)}, bf16[8,32,256]{2,1,0:T(8,128)(2,1)S(1)}, u32[]{:S(2)}, u32[]{:S(2)}) collective-permute-start(bf16[8,32,256]{2,1,0:T(8,128)(2,1)S(1)} %all_to_all.37.vector_ref), channel_id=1, source_target_pairs={{0,16},{16,0},{1,17},{17,1},{2,18},{18,2},{3,19},{19,3},{4,20},{20... | collective-permute-start | bytes 393224 | tf_op jit(solution)/shard_map/ppermute | solution.py:267
  89.1 2.3 %collective-permute-start.5 = (bf16[8,32,256]{2,1,0:T(8,128)(2,1)S(1)}, bf16[8,32,256]{2,1,0:T(8,128)(2,1)S(1)}, u32[]{:S(2)}, u32[]{:S(2)}) collective-permute-start(bf16[8,32,256]{2,1,0:T(8,128)(2,1)S(1)} %collective-permute-done.3.vector_ref), channel_id=1, source_target_pairs={{0,1},{1,0},{2,3},{3,2},{4,5},{5,4},{6,7},{7,6},{8,9},{9,8},{10,11... | collective-permute-start | bytes 393224 | tf_op jit(solution)/shard_map/ppermute | solution.py:267

commit v3 on v2

--- a/solution.py
+++ b/solution.py
@@ -12,17 +12,19 @@
 AMP_NUM = 16.0
 
 AXES = ("yl", "x", "yh", "z", "core")
-ROW = ("yl", "x")
+ROW = ("x", "yl")
 COL = ("yh", "z", "core")
 LINE = ("z",)
 
 BF16 = jnp.bfloat16
 F32 = jnp.float32
 VMEM = pl.BlockSpec(memory_space=pltpu.VMEM)
+SMEM = pl.BlockSpec(memory_space=pltpu.SMEM)
+HBM = pl.BlockSpec(memory_space=pltpu.HBM)
 
 HEAD = 80
 DEPTH = 128
-WIDE = 512
+WIDE = 1024
 
 
 def scale_of(width):
@@ -49,7 +51,20 @@
     return out
 
 
-def pack_body(features_ref, groups_ref, start_ref, plane_ref, line_ref, *, shift):
+def pack_body(
+    features_hbm, groups_hbm, start_hbm, own_ref, line_ref, features_ref, groups_ref, start_ref, sems,
+    *, shift
+):
+    copies = [
+        pltpu.make_async_copy(source, target, sems.at[n])
+        for n, (source, target) in enumerate(
+            ((features_hbm, features_ref), (groups_hbm, groups_ref), (start_hbm, start_ref))
+        )
+    ]
+    for copy in copies:
+        copy.start()
+    for copy in copies:
+        copy.wait()
     features = features_ref[...]
     wide = features.astype(F32)
     half = shift - 0.5 * jnp.sum(wide * wide, axis=0, keepdims=True)
@@ -62,9 +77,8 @@
     tail = jnp.where(row == 2, third, tail)
     tail = jnp.where(row == 3, group, tail).astype(BF16)
     vector = start_ref[...].astype(BF16)
-    for n in range(plane_ref.shape[0]):
-        plane_ref[n, 0:64, :] = features
-        plane_ref[n, 64:80, :] = tail
+    own_ref[0, 0:64, :] = features
+    own_ref[0, 64:80, :] = tail
     for n in range(line_ref.shape[0]):
         line_ref[n, 0:64, :] = features
         line_ref[n, 64:80, :] = tail
@@ -89,25 +103,33 @@
     return out.astype(BF16)
 
 
-def build_body(scale, gains, line_ref, plane_ref, carried_ref, tile_ref, out_ref, *scratch):
-    left_ref, vector_ref, right_ref = scratch
+def right_body(gains, *refs):
+    right_ref = refs[-1]
+    size = refs[0].shape[2]
+    place = 0
+    for ref in refs[:-1]:
+        for n in range(ref.shape[0]):
+            columns = slice(place * size, (place + 1) * size)
+            right_ref[0:64, columns] = ref[n, 0:64, :]
+            right_ref[64:128, columns] = tail_rows(ref[n, 64:80, :], False, gains)
+            place += 1
+
+
+def build_body(scale, me_ref, line_ref, right_ref, *refs, first, last):
+    if not first:
+        carried_ref, refs = refs[0], refs[1:]
+    tile_ref, out_ref, left_ref, vector_ref = refs
     blocks, _, size = line_ref.shape
     per = WIDE // size
     for n in range(blocks):
         rows = line_ref[n, 0:64, :]
-        tail = tail_rows(line_ref[n, 64:80, :], True, gains)
+        tail = tail_rows(line_ref[n, 64:80, :], True, None)
         left_ref[n * size : (n + 1) * size, :] = jnp.concatenate([rows, tail], axis=0).T
         vector_ref[:, n * size : (n + 1) * size] = line_ref[n, 80:112, :]
 
     def step(turn, state):
         columns = pl.ds(pl.multiple_of(turn * WIDE, WIDE), WIDE)
-        for n in range(per):
-            block = turn * per + n
-            right_ref[0:64, n * size : (n + 1) * size] = plane_ref[block, 0:64, :]
-            right_ref[64:128, n * size : (n + 1) * size] = tail_rows(
-                plane_ref[block, 64:80, :], False, gains
-            )
-        right = right_ref[...]
+        right = right_ref[:, columns]
         for n in range(blocks):
             power = jnp.dot(
                 left_ref[n * size : (n + 1) * size, :], right, preferred_element_type=F32
@@ -118,72 +140,82 @@
         )
         for n in range(per):
             block = turn * per + n
-            value = carried_ref[block] + product[:, n * size : (n + 1) * size]
+            value = product[:, n * size : (n + 1) * size]
+            if not first:
+                value = value + carried_ref[block]
+            if last:
+                block = block ^ me_ref[0]
             out_ref[block] = value.astype(out_ref.dtype)
         return state
 
-    lax.fori_loop(0, plane_ref.shape[0] // per, step, 0)
-
-
-def start_body(scale, gains, line_ref, plane_ref, tile_ref, out_ref, *scratch):
-    out_ref[...] = jnp.zeros_like(out_ref)
-    build_body(scale, gains, line_ref, plane_ref, out_ref, tile_ref, out_ref, *scratch)
-
-
-def build(line, plane, carried, scale, gains, out_dtype):
+    lax.fori_loop(0, right_ref.shape[1] // WIDE, step, 0)
+
+
+def build(line, right, carried, me, scale, last=False):
     blocks, rows, size = line.shape
-    columns = plane.shape[0]
+    total = right.shape[1]
     vectors = rows - HEAD
     points = blocks * size
-    body = start_body if carried is None else build_body
-    operands = [line, plane] + ([] if carried is None else [carried])
+    first = carried is None
+    operands, in_specs = [me, line, right], [SMEM, VMEM, VMEM]
+    if not first:
+        operands.append(carried)
+        in_specs.append(VMEM)
     return pl.pallas_call(
-        functools.partial(body, scale, gains),
-        in_specs=[VMEM] * len(operands),
+        functools.partial(build_body, scale, first=first, last=last),
+        in_specs=in_specs,
         out_specs=[VMEM] * 2,
         out_shape=[
-            pltpu.VMEM((points, columns * size), BF16),
-            pltpu.VMEM((columns, vectors, size), out_dtype),
+            pltpu.VMEM((points, total), BF16),
+            pltpu.VMEM((total // size, vectors, size), BF16 if last else F32),
         ],
-        scratch_shapes=[
-            pltpu.VMEM((points, DEPTH), BF16),
-            pltpu.VMEM((vectors, points), BF16),
-            pltpu.VMEM((DEPTH, WIDE), BF16),
-        ],
-        compiler_params=pltpu.CompilerParams(vmem_limit_bytes=16 << 20),
+        scratch_shapes=[pltpu.VMEM((points, DEPTH), BF16), pltpu.VMEM((vectors, points), BF16)],
+        compiler_params=pltpu.CompilerParams(vmem_limit_bytes=6 << 20),
         cost_estimate=pl.CostEstimate(
-            flops=2 * points * columns * size * 512,
-            bytes_accessed=2 * points * columns * size,
-            transcendentals=points * columns * size,
+            flops=2 * points * total * 512,
+            bytes_accessed=2 * points * total,
+            transcendentals=points * total,
         ),
         name="build",
     )(*operands)
 
 
-def apply_body(vector_ref, tile_ref, *refs):
-    out_ref, flat_ref = refs[-2:]
+def apply_body(vector_ref, tile_ref, *refs, first, last):
+    if not first:
+        carried_ref, refs = refs[0], refs[1:]
+    if last:
+        me_ref, refs = refs[0], refs[1:]
+    out_ref, flat_ref = refs
     blocks, _, size = vector_ref.shape
     for n in range(blocks):
         flat_ref[:, n * size : (n + 1) * size] = vector_ref[n]
     product = jnp.dot(flat_ref[...], tile_ref[...], preferred_element_type=F32)
     for n in range(out_ref.shape[0]):
         value = product[:, n * size : (n + 1) * size]
-        if len(refs) == 3:
-            value = value + refs[0][n]
-        out_ref[n] = value.astype(out_ref.dtype)
-
-
-def apply(vector, tile, carried, out_dtype):
+        if not first:
+            value = value + carried_ref[n]
+        block = n ^ me_ref[0] if last else n
+        out_ref[block] = value.astype(out_ref.dtype)
+
+
+def apply(vector, tile, carried, me):
     blocks, vectors, size = vector.shape
     points, total = tile.shape
-    operands = [vector, tile] + ([] if carried is None else [carried])
+    first, last = carried is None, me is not None
+    operands, in_specs = [vector, tile], [VMEM, VMEM]
+    if not first:
+        operands.append(carried)
+        in_specs.append(VMEM)
+    if last:
+        operands.append(me)
+        in_specs.append(SMEM)
     return pl.pallas_call(
-        apply_body,
-        in_specs=[VMEM] * len(operands),
+        functools.partial(apply_body, first=first, last=last),
+        in_specs=in_specs,
         out_specs=VMEM,
-        out_shape=pltpu.VMEM((total // size, vectors, size), out_dtype),
+        out_shape=pltpu.VMEM((total // size, vectors, size), BF16 if last else F32),
         scratch_shapes=[pltpu.VMEM((vectors, points), BF16)],
-        compiler_params=pltpu.CompilerParams(vmem_limit_bytes=8 << 20),
+        compiler_params=pltpu.CompilerParams(vmem_limit_bytes=4 << 20),
         cost_estimate=pl.CostEstimate(
             flops=2 * points * total * 256,
             bytes_accessed=2 * points * total,
@@ -263,26 +295,48 @@
     gains = constant_pieces(gain)
     shift = 0.5 * (math.log2(amplitude) / scale - gain)
 
-    def across(value, axis):
-        return lax.ppermute(value, axis, [(0, 1), (1, 0)])
-
-    plane, line = small(
+    me = lax.axis_index(ROW).astype(jnp.int32).reshape(1)
+
+    def across(value, axis, step=1):
+        count = lax.axis_size(axis)
+        return lax.ppermute(value, axis, [(n, n ^ step) for n in range(count)])
+
+    own, line = pl.pallas_call(
         functools.partial(pack_body, shift=shift),
-        "pack",
-        [pltpu.VMEM((rows, HEAD, size), BF16), pltpu.VMEM((lines, HEAD + vectors, size), BF16)],
-        [features, groups.reshape(1, size), start],
-    )
+        in_specs=[HBM] * 3,
+        out_specs=[VMEM] * 2,
+        out_shape=[
+            pltpu.VMEM((1, HEAD, size), BF16),
+            pltpu.VMEM((lines, HEAD + vectors, size), BF16),
+        ],
+        scratch_shapes=[
+            pltpu.VMEM((width, size), BF16),
+            pltpu.VMEM((1, size), jnp.int32),
+            pltpu.VMEM((vectors, size), F32),
+            pltpu.SemaphoreType.DMA((3,)),
+        ],
+        compiler_params=pltpu.CompilerParams(vmem_limit_bytes=4 << 20),
+        name="pack",
+    )(features, groups.reshape(1, size), start)
     line = lax.all_to_all(line, LINE, 0, 0)
+    pair = jnp.concatenate([own, across(own, "yl")], axis=0)
+    parts = [pair] + [across(pair, "x", step) for step in (1, 2, 3)]
+    (right,) = small(
+        functools.partial(right_body, gains),
+        "right",
+        [pltpu.VMEM((DEPTH, rows * size), BF16)],
+        parts,
+    )
+    line, right = lax.optimization_barrier((line, right))
     far = across(line, "yh")
     near = across(line, "core")
-    plane = lax.all_to_all(plane, ROW, 0, 0)
     tiles = [None] * 4
-    tiles[0], carried = build(line, plane, None, scale, gains, F32)
-    tiles[1], carried = build(near, plane, carried, scale, gains, F32)
+    tiles[0], carried = build(line, right, None, me, scale)
+    tiles[1], carried = build(near, right, carried, me, scale)
     far, carried = lax.optimization_barrier((far, carried))
     last = across(far, "core")
-    tiles[2], carried = build(far, plane, carried, scale, gains, F32)
-    tiles[3], partial_value = build(last, plane, carried, scale, gains, BF16)
+    tiles[2], carried = build(far, right, carried, me, scale)
+    tiles[3], partial_value = build(last, right, carried, me, scale, last=True)
     received = lax.all_to_all(partial_value, ROW, 0, 0)
 
     residual0, vector = small(
@@ -294,12 +348,12 @@
     vector = lax.all_to_all(vector, LINE, 0, 0)
     far = across(vector, "yh")
     near = across(vector, "core")
-    carried = apply(vector, tiles[0], None, F32)
-    carried = apply(near, tiles[1], carried, F32)
+    carried = apply(vector, tiles[0], None, None)
+    carried = apply(near, tiles[1], carried, None)
     far, carried = lax.optimization_barrier((far, carried))
     last = across(far, "core")
-    carried = apply(far, tiles[2], carried, F32)
-    partial_value = apply(last, tiles[3], carried, BF16)
+    carried = apply(far, tiles[2], carried, None)
+    partial_value = apply(last, tiles[3], carried, me)
     received = lax.all_to_all(partial_value, ROW, 0, 0)
 
     product, sums = small(

time: 126 us -> 121 us (0.960)
  blocking collectives: 74.5 us -> 53.2 us
  waiting for transfers between devices: 7.14 us -> 15.5 us
  starting transfers between devices: 16.2 us -> 24.3 us
    all_to_all x1 -> x0, blocking collectives: 23.3 us -> none  [per_device(): line = lax.all_to_all(line, LINE, 0, 0)]
    all_to_all x1, waiting for transfers between devices: 1.08 us -> 5.97 us  [per_device(): line = lax.all_to_all(line, LINE, 0, 0)]
    ppermute x6 -> x10, starting transfers between devices: 11.2 us -> 15.2 us  [across(): return lax.ppermute(value, axis, [(n, n ^ step) for n in range(count)])]
    all_to_all x1, starting transfers between devices: 5.03 us -> 9.03 us  [per_device(): line = lax.all_to_all(line, LINE, 0, 0)]
    ppermute x6 -> x10, waiting for transfers between devices: 6.06 us -> 9.54 us  [across(): return lax.ppermute(value, axis, [(n, n ^ step) for n in range(count)])]
    pallas_call x8 -> x9, Pallas kernels: 23 us -> 23.1 us  [the longest x4 16 us: build(): pl.pallas_call(functools.partial(build_body, scale, first=first, last=las...]
  transfers between devices with their start and end apart: 7 -> 11, of which waited for: 3 -> 6; matrix products, arithmetic and copies ran while one was open for 0% -> 0% of each run, Pallas kernels for 14% -> 14%
where the time goes in v3:
time: 121 us; the launch traced here: 120 us
  blocking collectives  53.2 us (44%)
  Pallas kernels  24.3 us (20%)
  starting transfers between devices  24.3 us (20%)
  waiting for transfers between devices  15.5 us (13%)
  local copies, waits for them, and re-layouts  2.21 us (2%)
    all_to_all x2, blocking collectives, per_device(): received = lax.all_to_all(partial_value, ROW, 0, 0)  17.7 us
    all_to_all x1, blocking collectives, per_device(): sums = lax.all_to_all(sums, COL, 0, 0)  17.1 us
    pallas_call x4, Pallas kernels, build(): pl.pallas_call(functools.partial(build_body, scale, first=first, last=las...  16 us
    ppermute x10, starting transfers between devices, across(): return lax.ppermute(value, axis, [(n, n ^ step) for n in range(count)])  15.2 us
    all_to_all x1, blocking collectives, per_device(): vector = lax.all_to_all(vector, LINE, 0, 0)  10.5 us
    ppermute x10, waiting for transfers between devices, across(): return lax.ppermute(value, axis, [(n, n ^ step) for n in range(count)])  9.54 us
    all_to_all x1, starting transfers between devices, per_device(): line = lax.all_to_all(line, LINE, 0, 0)  9.03 us
    all_to_all x1, blocking collectives, per_device(): sums = lax.all_to_all(sums, ROW, 0, 0)  7.91 us
  transfers between devices with their start and end apart: 11, of which 6 were waited for; matrix products, arithmetic and copies ran while one was open for 0% of the time, Pallas kernels for 14%

profile of v3, /device:TPU:1, one launch (start us, length us, event | category | flops | bytes accessed | tf_op | source)
XLA Modules:
  0.0 120.3 jit_solution(9249712949423116814)
XLA Ops:
  0.6 0.0 copy-start
  0.6 0.7 copy-done
  1.4 0.0 copy-start.2
  1.4 0.8 copy-done.2
  2.2 0.7 copy-done.4
  2.8 0.9 pack.1
  3.7 9.0 %all-to-all-start = ((bf16[8,112,256]{2,1,0:T(8,128)(2,1)}), bf16[8,112,256]{2,1,0:T(8,128)(2,1)S(1)}, u32[]{:S(2)}, u32[]{:S(2)}) async-start(bf16[8,112,256]{2,1,0:T(8,128)(2,1)} %get-tuple-element.23), calls=%async_computation | async-start | bytes 917504 | tf_op jit(solution)/shard_map/all_to_all | solution.py:321
  12.8 1.3 %collective-permute-start = (bf16[1,80,256]{2,1,0:T(8,128)(2,1)S(1)}, bf16[1,80,256]{2,1,0:T(8,128)(2,1)S(1)}, u32[]{:S(2)}, u32[]{:S(2)}) collective-permute-start(bf16[1,80,256]{2,1,0:T(8,128)(2,1)S(1)} %get-tuple-element.24), channel_id=1, source_target_pairs={{0,128},{128,0},{1,129},{129,1},{2,130},{130,2},{3,131},{131,3},{4... | collective-permute-start | bytes 122888 | tf_op jit(solution)/shard_map/ppermute | solution.py:302
  14.1 1.6 %collective-permute-done = bf16[1,80,256]{2,1,0:T(8,128)(2,1)S(1)} collective-permute-done((bf16[1,80,256]{2,1,0:T(8,128)(2,1)S(1)}, bf16[1,80,256]{2,1,0:T(8,128)(2,1)S(1)}, u32[]{:S(2)}, u32[]{:S(2)}) %collective-permute-start) | collective-permute-done | bytes 40992 | tf_op jit(solution)/shard_map/ppermute | solution.py:302
  15.6 2.5 %collective-permute-start.3 = (bf16[2,80,256]{2,1,0:T(8,128)(2,1)S(1)}, bf16[2,80,256]{2,1,0:T(8,128)(2,1)S(1)}, u32[]{:S(2)}, u32[]{:S(2)}) collective-permute-start(bf16[2,80,256]{2,1,0:T(8,128)(2,1)S(1)} %constant_dynamic-update-slice_fusion.refs_0_), channel_id=1, source_target_pairs={{0,96},{32,64},{64,32},{96,0},{1,97},{33,65},{65,33},{97,1},{2,98}... | collective-permute-start | bytes 245768 | tf_op jit(solution)/shard_map/ppermute | solution.py:302
  18.1 0.5 collective-permute-start.2
  18.6 0.3 collective-permute-start.1
  18.9 1.5 %collective-permute-done.3.refs_3_ = bf16[2,80,256]{2,1,0:T(8,128)(2,1)S(1)} collective-permute-done((bf16[2,80,256]{2,1,0:T(8,128)(2,1)S(1)}, bf16[2,80,256]{2,1,0:T(8,128)(2,1)S(1)}, u32[]{:S(2)}, u32[]{:S(2)}) %collective-permute-start.3) | collective-permute-done | bytes 81952 | tf_op jit(solution)/shard_map/ppermute | solution.py:302
  20.4 2.8 %collective-permute-done.2.refs_2_ = bf16[2,80,256]{2,1,0:T(8,128)(2,1)S(1)} collective-permute-done((bf16[2,80,256]{2,1,0:T(8,128)(2,1)S(1)}, bf16[2,80,256]{2,1,0:T(8,128)(2,1)S(1)}, u32[]{:S(2)}, u32[]{:S(2)}) %collective-permute-start.2) | collective-permute-done | bytes 81952 | tf_op jit(solution)/shard_map/ppermute | solution.py:302
  23.2 0.0 collective-permute-done.1.refs_1_
  23.2 0.1 right.1.right_ref
  23.2 6.0 %all-to-all-done.line_ref = bf16[8,112,256]{2,1,0:T(8,128)(2,1)S(1)} async-done(((bf16[8,112,256]{2,1,0:T(8,128)(2,1)}), bf16[8,112,256]{2,1,0:T(8,128)(2,1)S(1)}, u32[]{:S(2)}, u32[]{:S(2)}) %all-to-all-start) | async-done | bytes 458784 | tf_op jit(solution)/shard_map/all_to_all | solution.py:321
  29.2 0.6 collective-permute-start.5
  29.8 2.9 %collective-permute-start.4 = (bf16[8,112,256]{2,1,0:T(8,128)(2,1)S(1)}, bf16[8,112,256]{2,1,0:T(8,128)(2,1)S(1)}, u32[]{:S(2)}, u32[]{:S(2)}) collective-permute-start(bf16[8,112,256]{2,1,0:T(8,128)(2,1)S(1)} %all-to-all-done.line_ref), channel_id=1, source_target_pairs={{0,16},{16,0},{1,17},{17,1},{2,18},{18,2},{3,19},{19,3},{4,20},{20... | collective-permute-start | bytes 1376264 | tf_op jit(solution)/shard_map/ppermute | solution.py:302
  32.7 4.0 %build.4 = (bf16[2048,2048]{1,0:T(8,128)(2,1)S(1)}, f32[8,32,256]{2,1,0:T(8,128)S(1)}) custom-call(s32[1]{0:T(128)} %bitcast.me_ref.refs_1_, bf16[8,112,256]{2,1,0:T(8,128)(2,1)S(1)} %all-to-all-done.line_ref, bf16[128,2048]{1,0:T(8,128)(2,1)S(1)} %right.1.right_ref), custom_call_target="tpu_custom_call" | custom-call | flops 4294967296 | bytes 8388608 | tf_op jit(solution)/shard_map/build/pallas_call | solution.py:164
  36.7 0.0 collective-permute-done.5.line_ref
  36.7 4.0 %build.5 = (bf16[2048,2048]{1,0:T(8,128)(2,1)S(1)}, f32[8,32,256]{2,1,0:T(8,128)S(1)}) custom-call(s32[1]{0:T(128)} %bitcast.me_ref.refs_1_, bf16[8,112,256]{2,1,0:T(8,128)(2,1)S(1)} %collective-permute-done.5.line_ref, bf16[128,2048]{1,0:T(8,128)(2,1)S(1)} %right.1.right_ref, f32[8,32,256]{2,1,0:T(8,128)S(1)} %get-tuple-element.27.refs_0_), custom_call_target="tpu_custom_call" | custom-call | flops 4294967296 | bytes 8388608 | tf_op jit(solution)/shard_map/build/pallas_call | solution.py:164
  40.7 2.7 %collective-permute-done.4.line_ref = bf16[8,112,256]{2,1,0:T(8,128)(2,1)S(1)} collective-permute-done((bf16[8,112,256]{2,1,0:T(8,128)(2,1)S(1)}, bf16[8,112,256]{2,1,0:T(8,128)(2,1)S(1)}, u32[]{:S(2)}, u32[]{:S(2)}) %collective-permute-start.4) | collective-permute-done | bytes 458784 | tf_op jit(solution)/shard_map/ppermute | solution.py:302
  43.5 0.8 collective-permute-start.6
  44.2 4.0 %build.6 = (bf16[2048,2048]{1,0:T(8,128)(2,1)S(1)}, f32[8,32,256]{2,1,0:T(8,128)S(1)}) custom-call(s32[1]{0:T(128)} %bitcast.me_ref.refs_1_, bf16[8,112,256]{2,1,0:T(8,128)(2,1)S(1)} %collective-permute-done.4.line_ref, bf16[128,2048]{1,0:T(8,128)(2,1)S(1)} %right.1.right_ref, f32[8,32,256]{2,1,0:T(8,128)S(1)} %get-tuple-element.30.refs_0_), custom_call_target="tpu_custom_call" | custom-call | flops 4294967296 | bytes 8388608 | tf_op jit(solution)/shard_map/build/pallas_call | solution.py:164
  48.2 0.0 copy-start.1
  48.3 0.0 copy-start.3
  48.3 0.0 collective-permute-done.6.line_ref
  48.3 4.0 %build.7 = (bf16[2048,2048]{1,0:T(8,128)(2,1)S(1)}, bf16[8,32,256]{2,1,0:T(8,128)(2,1)S(1)}) custom-call(s32[1]{0:T(128)} %bitcast.me_ref.refs_1_, bf16[8,112,256]{2,1,0:T(8,128)(2,1)S(1)} %collective-permute-done.6.line_ref, bf16[128,2048]{1,0:T(8,128)(2,1)S(1)} %right.1.right_ref, f32[8,32,256]{2,1,0:T(8,128)S(1)} %get-tuple-element.31.refs_0_), custom_call_target="tpu_custom_call" | custom-call | flops 4294967296 | bytes 8388608 | tf_op jit(solution)/shard_map/build/pallas_call | solution.py:164
  52.3 10.1 %all_to_all.30.received_ref = bf16[8,32,256]{2,1,0:T(8,128)(2,1)S(1)} all-to-all(bf16[8,32,256]{2,1,0:T(8,128)(2,1)S(1)} %get-tuple-element.32), channel_id=1, replica_groups=mesh['yl'=2,'x'=4,'yh'=2,'z'=8,'core'=2] {'x','yl'}, dimensions={0} | all-to-all | bytes 262144 | tf_op jit(solution)/shard_map/all_to_all | solution.py:340
  62.4 0.0 copy-done.1
  62.4 0.0 copy-done.3
  62.4 10.5 %all_to_all.31.vector_ref = bf16[8,32,256]{2,1,0:T(8,128)(2,1)S(1)} all-to-all(bf16[8,32,256]{2,1,0:T(8,128)(2,1)S(1)} %get-tuple-element.33), channel_id=1, replica_groups=mesh['yl'=2,'x'=4,'yh'=2,'z'=8,'core'=2] {'z'}, dimensions={0} | all-to-all | bytes 262144 | tf_op jit(solution)/shard_map/all_to_all | solution.py:348
  72.9 3.0 %collective-permute-start.8 = (bf16[8,32,256]{2,1,0:T(8,128)(2,1)S(1)}, bf16[8,32,256]{2,1,0:T(8,128)(2,1)S(1)}, u32[]{:S(2)}, u32[]{:S(2)}) collective-permute-start(bf16[8,32,256]{2,1,0:T(8,128)(2,1)S(1)} %all_to_all.31.vector_ref), channel_id=1, source_target_pairs={{0,1},{1,0},{2,3},{3,2},{4,5},{5,4},{6,7},{7,6},{8,9},{9,8},{10,11... | collective-permute-start | bytes 393224 | tf_op jit(solution)/shard_map/ppermute | solution.py:302
  75.9 2.6 %collective-permute-start.7 = (bf16[8,32,256]{2,1,0:T(8,128)(2,1)S(1)}, bf16[8,32,256]{2,1,0:T(8,128)(2,1)S(1)}, u32[]{:S(2)}, u32[]{:S(2)}) collective-permute-start(bf16[8,32,256]{2,1,0:T(8,128)(2,1)S(1)} %all_to_all.31.vector_ref), channel_id=1, source_target_pairs={{0,16},{16,0},{1,17},{17,1},{2,18},{18,2},{3,19},{19,3},{4,20},{20... | collective-permute-start | bytes 393224 | tf_op jit(solution)/shard_map/ppermute | solution.py:302
  78.5 1.5 %apply.4.refs_0_ = f32[8,32,256]{2,1,0:T(8,128)S(1)} custom-call(bf16[8,32,256]{2,1,0:T(8,128)(2,1)S(1)} %all_to_all.31.vector_ref, bf16[2048,2048]{1,0:T(8,128)(2,1)S(1)} %get-tuple-element.35.tile_ref), custom_call_target="tpu_custom_call" | custom-call | flops 2147483648 | bytes 8388608 | tf_op jit(solution)/shard_map/apply/pallas_call | solution.py:212
  80.1 0.0 collective-permute-done.8.vector_ref
  80.1 1.5 %apply.5.refs_0_ = f32[8,32,256]{2,1,0:T(8,128)S(1)} custom-call(bf16[8,32,256]{2,1,0:T(8,128)(2,1)S(1)} %collective-permute-done.8.vector_ref, bf16[2048,2048]{1,0:T(8,128)(2,1)S(1)} %get-tuple-element.34.tile_ref, f32[8,32,256]{2,1,0:T(8,128)S(1)} %apply.4.refs_0_), custom_call_target="tpu_custom_call" | custom-call | flops 2147483648 | bytes 8388608 | tf_op jit(solution)/shard_map/apply/pallas_call | solution.py:212
  81.6 0.9 collective-permute-done.7.vector_ref
  82.6 0.8 collective-permute-start.9
  83.3 1.5 %apply.6.refs_0_ = f32[8,32,256]{2,1,0:T(8,128)S(1)} custom-call(bf16[8,32,256]{2,1,0:T(8,128)(2,1)S(1)} %collective-permute-done.7.vector_ref, bf16[2048,2048]{1,0:T(8,128)(2,1)S(1)} %get-tuple-element.38.tile_ref, f32[8,32,256]{2,1,0:T(8,128)S(1)} %apply.5.refs_0_), custom_call_target="tpu_custom_call" | custom-call | flops 2147483648 | bytes 8388608 | tf_op jit(solution)/shard_map/apply/pallas_call | solution.py:212
  84.9 0.0 collective-permute-done.9.vector_ref
  84.9 1.5 %apply.7 = bf16[8,32,256]{2,1,0:T(8,128)(2,1)S(1)} custom-call(bf16[8,32,256]{2,1,0:T(8,128)(2,1)S(1)} %collective-permute-done.9.vector_ref, bf16[2048,2048]{1,0:T(8,128)(2,1)S(1)} %get-tuple-element.37.tile_ref, f32[8,32,256]{2,1,0:T(8,128)S(1)} %apply.6.refs_0_, s32[1]{0:T(128)} %bitcast.me_ref.refs_1_), custom_call_target="tpu_custom_call" | custom-call | flops 2147483648 | bytes 8388608 | tf_op jit(solution)/shard_map/apply/pallas_call | solution.py:212
  86.4 7.7 %all_to_all.32.received_ref = bf16[8,32,256]{2,1,0:T(8,128)(2,1)S(1)} all-to-all(bf16[8,32,256]{2,1,0:T(8,128)(2,1)S(1)} %apply.7), channel_id=1, replica_groups=mesh['yl'=2,'x'=4,'yh'=2,'z'=8,'core'=2] {'x','yl'}, dimensions={0} | all-to-all | bytes 262144 | tf_op jit(solution)/shard_map/all_to_all | solution.py:357
  94.1 0.2 sums.1
  94.2 7.9 %all_to_all.33.received_ref = f32[8,8,128]{2,1,0:T(8,128)S(1)} all-to-all(f32[8,8,128]{2,1,0:T(8,128)S(1)} %get-tuple-element.41), channel_id=1, replica_groups=mesh['yl'=2,'x'=4,'yh'=2,'z'=8,'core'=2] {'x','yl'}, dimensions={0} | all-to-all | bytes 65536 | tf_op jit(solution)/shard_map/all_to_all | solution.py:365
  102.2 17.1 %all_to_all.34.received_ref = f32[32,8,128]{2,1,0:T(8,128)S(1)} all-to-all(f32[32,8,128]{2,1,0:T(8,128)S(1)} %spread.1), channel_id=1, replica_groups=mesh['yl'=2,'x'=4,'yh'=2,'z'=8,'core'=2] {'yh','z','core'}, dimensions={0} | all-to-all | bytes 262144 | tf_op jit(solution)/shard_map/all_to_all | solution.py:367
  119.3 1.0 last.1
  (5 shorter events, 0.1 us)
Async XLA Ops:
  0.6 0.8 copy-start
  1.4 0.8 copy-start.2
  2.1 0.7 copy-start.4
  3.7 25.5 %all-to-all-start = ((bf16[8,112,256]{2,1,0:T(8,128)(2,1)}), bf16[8,112,256]{2,1,0:T(8,128)(2,1)S(1)}, u32[]{:S(2)}, u32[]{:S(2)}) async-start(bf16[8,112,256]{2,1,0:T(8,128)(2,1)} %get-tuple-element.23), calls=%async_computation | async-start | bytes 917504 | tf_op jit(solution)/shard_map/all_to_all | solution.py:321
  12.8 2.9 %collective-permute-start = (bf16[1,80,256]{2,1,0:T(8,128)(2,1)S(1)}, bf16[1,80,256]{2,1,0:T(8,128)(2,1)S(1)}, u32[]{:S(2)}, u32[]{:S(2)}) collective-permute-start(bf16[1,80,256]{2,1,0:T(8,128)(2,1)S(1)} %get-tuple-element.24), channel_id=1, source_target_pairs={{0,128},{128,0},{1,129},{129,1},{2,130},{130,2},{3,131},{131,3},{4... | collective-permute-start | bytes 122888 | tf_op jit(solution)/shard_map/ppermute | solution.py:302
  15.6 4.8 %collective-permute-start.3 = (bf16[2,80,256]{2,1,0:T(8,128)(2,1)S(1)}, bf16[2,80,256]{2,1,0:T(8,128)(2,1)S(1)}, u32[]{:S(2)}, u32[]{:S(2)}) collective-permute-start(bf16[2,80,256]{2,1,0:T(8,128)(2,1)S(1)} %constant_dynamic-update-slice_fusion.refs_0_), channel_id=1, source_target_pairs={{0,96},{32,64},{64,32},{96,0},{1,97},{33,65},{65,33},{97,1},{2,98}... | collective-permute-start | bytes 245768 | tf_op jit(solution)/shard_map/ppermute | solution.py:302
  18.1 5.1 %collective-permute-start.2 = (bf16[2,80,256]{2,1,0:T(8,128)(2,1)S(1)}, bf16[2,80,256]{2,1,0:T(8,128)(2,1)S(1)}, u32[]{:S(2)}, u32[]{:S(2)}) collective-permute-start(bf16[2,80,256]{2,1,0:T(8,128)(2,1)S(1)} %constant_dynamic-update-slice_fusion.refs_0_), channel_id=1, source_target_pairs={{0,64},{32,96},{64,0},{96,32},{1,65},{33,97},{65,1},{97,33},{2,66}... | collective-permute-start | bytes 245768 | tf_op jit(solution)/shard_map/ppermute | solution.py:302
  18.6 4.6 %collective-permute-start.1 = (bf16[2,80,256]{2,1,0:T(8,128)(2,1)S(1)}, bf16[2,80,256]{2,1,0:T(8,128)(2,1)S(1)}, u32[]{:S(2)}, u32[]{:S(2)}) collective-permute-start(bf16[2,80,256]{2,1,0:T(8,128)(2,1)S(1)} %constant_dynamic-update-slice_fusion.refs_0_), channel_id=1, source_target_pairs={{0,32},{32,0},{64,96},{96,64},{1,33},{33,1},{65,97},{97,65},{2,34}... | collective-permute-start | bytes 245768 | tf_op jit(solution)/shard_map/ppermute | solution.py:302
  29.2 7.5 %collective-permute-start.5 = (bf16[8,112,256]{2,1,0:T(8,128)(2,1)S(1)}, bf16[8,112,256]{2,1,0:T(8,128)(2,1)S(1)}, u32[]{:S(2)}, u32[]{:S(2)}) collective-permute-start(bf16[8,112,256]{2,1,0:T(8,128)(2,1)S(1)} %all-to-all-done.line_ref), channel_id=1, source_target_pairs={{0,1},{1,0},{2,3},{3,2},{4,5},{5,4},{6,7},{7,6},{8,9},{9,8},{10,11... | collective-permute-start | bytes 1376264 | tf_op jit(solution)/shard_map/ppermute | solution.py:302
  29.8 13.7 %collective-permute-start.4 = (bf16[8,112,256]{2,1,0:T(8,128)(2,1)S(1)}, bf16[8,112,256]{2,1,0:T(8,128)(2,1)S(1)}, u32[]{:S(2)}, u32[]{:S(2)}) collective-permute-start(bf16[8,112,256]{2,1,0:T(8,128)(2,1)S(1)} %all-to-all-done.line_ref), channel_id=1, source_target_pairs={{0,16},{16,0},{1,17},{17,1},{2,18},{18,2},{3,19},{19,3},{4,20},{20... | collective-permute-start | bytes 1376264 | tf_op jit(solution)/shard_map/ppermute | solution.py:302
  43.5 4.8 %collective-permute-start.6 = (bf16[8,112,256]{2,1,0:T(8,128)(2,1)S(1)}, bf16[8,112,256]{2,1,0:T(8,128)(2,1)S(1)}, u32[]{:S(2)}, u32[]{:S(2)}) collective-permute-start(bf16[8,112,256]{2,1,0:T(8,128)(2,1)S(1)} %collective-permute-done.4.line_ref), channel_id=1, source_target_pairs={{0,1},{1,0},{2,3},{3,2},{4,5},{5,4},{6,7},{7,6},{8,9},{9,8},{10,11... | collective-permute-start | bytes 1376264 | tf_op jit(solution)/shard_map/ppermute | solution.py:302
  48.2 14.1 %copy-start.1 = (f32[32,256]{1,0:T(8,128)S(1)}, f32[32,256]{1,0:T(8,128)}, u32[]{:S(2)}) copy-start(f32[32,256]{1,0:T(8,128)} %start_ref.3) | copy-start | bytes 98308
  48.3 14.1 %copy-start.3 = (f32[32,256]{1,0:T(8,128)S(1)}, f32[32,256]{1,0:T(8,128)}, u32[]{:S(2)}) copy-start(f32[32,256]{1,0:T(8,128)} %targets_ref.1) | copy-start | bytes 98308
  72.9 7.2 %collective-permute-start.8 = (bf16[8,32,256]{2,1,0:T(8,128)(2,1)S(1)}, bf16[8,32,256]{2,1,0:T(8,128)(2,1)S(1)}, u32[]{:S(2)}, u32[]{:S(2)}) collective-permute-start(bf16[8,32,256]{2,1,0:T(8,128)(2,1)S(1)} %all_to_all.31.vector_ref), channel_id=1, source_target_pairs={{0,1},{1,0},{2,3},{3,2},{4,5},{5,4},{6,7},{7,6},{8,9},{9,8},{10,11... | collective-permute-start | bytes 393224 | tf_op jit(solution)/shard_map/ppermute | solution.py:302
  75.9 6.6 %collective-permute-start.7 = (bf16[8,32,256]{2,1,0:T(8,128)(2,1)S(1)}, bf16[8,32,256]{2,1,0:T(8,128)(2,1)S(1)}, u32[]{:S(2)}, u32[]{:S(2)}) collective-permute-start(bf16[8,32,256]{2,1,0:T(8,128)(2,1)S(1)} %all_to_all.31.vector_ref), channel_id=1, source_target_pairs={{0,16},{16,0},{1,17},{17,1},{2,18},{18,2},{3,19},{19,3},{4,20},{20... | collective-permute-start | bytes 393224 | tf_op jit(solution)/shard_map/ppermute | solution.py:302
  82.6 2.3 %collective-permute-start.9 = (bf16[8,32,256]{2,1,0:T(8,128)(2,1)S(1)}, bf16[8,32,256]{2,1,0:T(8,128)(2,1)S(1)}, u32[]{:S(2)}, u32[]{:S(2)}) collective-permute-start(bf16[8,32,256]{2,1,0:T(8,128)(2,1)S(1)} %collective-permute-done.7.vector_ref), channel_id=1, source_target_pairs={{0,1},{1,0},{2,3},{3,2},{4,5},{5,4},{6,7},{7,6},{8,9},{9,8},{10,11... | collective-permute-start | bytes 393224 | tf_op jit(solution)/shard_map/ppermute | solution.py:302

commit v4 on v3

--- a/solution.py
+++ b/solution.py
@@ -304,10 +304,9 @@
     own, line = pl.pallas_call(
         functools.partial(pack_body, shift=shift),
         in_specs=[HBM] * 3,
-        out_specs=[VMEM] * 2,
         out_shape=[
-            pltpu.VMEM((1, HEAD, size), BF16),
-            pltpu.VMEM((lines, HEAD + vectors, size), BF16),
+            jax.ShapeDtypeStruct((1, HEAD, size), BF16),
+            jax.ShapeDtypeStruct((lines, HEAD + vectors, size), BF16),
         ],
         scratch_shapes=[
             pltpu.VMEM((width, size), BF16),
@@ -315,7 +314,6 @@
             pltpu.VMEM((vectors, size), F32),
             pltpu.SemaphoreType.DMA((3,)),
         ],
-        compiler_params=pltpu.CompilerParams(vmem_limit_bytes=4 << 20),
         name="pack",
     )(features, groups.reshape(1, size), start)
     line = lax.all_to_all(line, LINE, 0, 0)
@@ -362,9 +360,9 @@
         [pltpu.VMEM((vectors, size), F32), pltpu.VMEM((rows, 8, 128), F32)],
         [received, residual0],
     )
-    sums = lax.all_to_all(sums, ROW, 0, 0)
+    sums = lax.all_to_all(sums, ('x', 'core'), 0, 0)
     (sums,) = small(spread_body, "spread", [pltpu.VMEM((columns, 8, 128), F32)], [sums])
-    sums = lax.all_to_all(sums, COL, 0, 0)
+    sums = lax.all_to_all(sums, ('yl', 'yh', 'z'), 0, 0)
     return tuple(
         small(
             last_body,

time: 121 us -> 117 us (0.967)
  blocking collectives: 53.2 us -> 50.5 us
  local copies, waits for them, and re-layouts: 2.21 us -> 0.83 us
    all_to_all x2, blocking collectives: 25 us -> 22.1 us  [the longest x1 13.5 us: per_device(): sums = lax.all_to_all(sums, ('yl', 'yh', 'z'), 0, 0)]
    unnamed x11 -> x5, local copies, waits for them, and re-layouts: 2.21 us -> 0.83 us
  transfers between devices with their start and end apart: 11 -> 11, of which waited for: 6 -> 6; matrix products, arithmetic and copies ran while one was open for 0% -> 1% of each run, Pallas kernels for 14% -> 14%
where the time goes in v4:
time: 117 us; the launch traced here: 116 us
  blocking collectives  50.5 us (43%)
  Pallas kernels  25 us (21%)
  starting transfers between devices  24.3 us (21%)
  waiting for transfers between devices  14.7 us (13%)
    all_to_all x2, blocking collectives, per_device(): received = lax.all_to_all(partial_value, ROW, 0, 0)  17.7 us
    pallas_call x4, Pallas kernels, build(): pl.pallas_call(functools.partial(build_body, scale, first=first, last=las...  16 us
    ppermute x10, starting transfers between devices, across(): return lax.ppermute(value, axis, [(n, n ^ step) for n in range(count)])  15.3 us
    all_to_all x1, blocking collectives, per_device(): sums = lax.all_to_all(sums, ('yl', 'yh', 'z'), 0, 0)  13.5 us
    all_to_all x1, blocking collectives, per_device(): vector = lax.all_to_all(vector, LINE, 0, 0)  10.7 us
    all_to_all x1, starting transfers between devices, per_device(): line = lax.all_to_all(line, LINE, 0, 0)  9.03 us
    ppermute x10, waiting for transfers between devices, across(): return lax.ppermute(value, axis, [(n, n ^ step) for n in range(count)])  8.97 us
    all_to_all x1, blocking collectives, per_device(): sums = lax.all_to_all(sums, ('x', 'core'), 0, 0)  8.64 us
  transfers between devices with their start and end apart: 11, of which 6 were waited for; matrix products, arithmetic and copies ran while one was open for 1% of the time, Pallas kernels for 14%

profile of v4, /device:TPU:1, one launch (start us, length us, event | category | flops | bytes accessed | tf_op | source)
XLA Modules:
  0.0 116.1 jit_solution(7704698654273111574)
XLA Ops:
  0.6 1.6 %pack.1 = (bf16[1,80,256]{2,1,0:T(8,128)(2,1)}, bf16[8,112,256]{2,1,0:T(8,128)(2,1)}) custom-call(bf16[64,256]{1,0:T(8,128)(2,1)} %features_hbm.1, s32[1,256]{1,0:T(1,128)} %bitcast.2, f32[32,256]{1,0:T(8,128)} %start_ref.3), custom_call_target="tpu_custom_call" | custom-call | tf_op jit(solution)/shard_map/pack/pallas_call | solution.py:304
  2.3 9.0 %all-to-all-start = ((bf16[8,112,256]{2,1,0:T(8,128)(2,1)}), bf16[8,112,256]{2,1,0:T(8,128)(2,1)S(1)}, u32[]{:S(2)}, u32[]{:S(2)}) async-start(bf16[8,112,256]{2,1,0:T(8,128)(2,1)} %get-tuple-element.23), calls=%async_computation | async-start | bytes 917504 | tf_op jit(solution)/shard_map/all_to_all | solution.py:319
  11.3 1.3 %collective-permute-start = (bf16[1,80,256]{2,1,0:T(8,128)(2,1)}, bf16[1,80,256]{2,1,0:T(8,128)(2,1)S(1)}, u32[]{:S(2)}, u32[]{:S(2)}) collective-permute-start(bf16[1,80,256]{2,1,0:T(8,128)(2,1)} %get-tuple-element.24), channel_id=1, source_target_pairs={{0,128},{128,0},{1,129},{129,1},{2,130},{130,2},{3,131},{131,3},{4... | collective-permute-start | bytes 122888 | tf_op jit(solution)/shard_map/ppermute | solution.py:302
  12.6 0.8 constant_dynamic-update-slice_fusion.1
  13.4 1.0 collective-permute-done
  14.4 2.5 %collective-permute-start.3 = (bf16[2,80,256]{2,1,0:T(8,128)(2,1)S(1)}, bf16[2,80,256]{2,1,0:T(8,128)(2,1)S(1)}, u32[]{:S(2)}, u32[]{:S(2)}) collective-permute-start(bf16[2,80,256]{2,1,0:T(8,128)(2,1)S(1)} %constant_dynamic-update-slice_fusion.refs_0_), channel_id=1, source_target_pairs={{0,96},{32,64},{64,32},{96,0},{1,97},{33,65},{65,33},{97,1},{2,98}... | collective-permute-start | bytes 245768 | tf_op jit(solution)/shard_map/ppermute | solution.py:302
  16.8 0.5 collective-permute-start.2
  17.4 0.3 collective-permute-start.1
  17.6 1.5 %collective-permute-done.3.refs_3_ = bf16[2,80,256]{2,1,0:T(8,128)(2,1)S(1)} collective-permute-done((bf16[2,80,256]{2,1,0:T(8,128)(2,1)S(1)}, bf16[2,80,256]{2,1,0:T(8,128)(2,1)S(1)}, u32[]{:S(2)}, u32[]{:S(2)}) %collective-permute-start.3) | collective-permute-done | bytes 81952 | tf_op jit(solution)/shard_map/ppermute | solution.py:302
  19.2 2.8 %collective-permute-done.2.refs_2_ = bf16[2,80,256]{2,1,0:T(8,128)(2,1)S(1)} collective-permute-done((bf16[2,80,256]{2,1,0:T(8,128)(2,1)S(1)}, bf16[2,80,256]{2,1,0:T(8,128)(2,1)S(1)}, u32[]{:S(2)}, u32[]{:S(2)}) %collective-permute-start.2) | collective-permute-done | bytes 81952 | tf_op jit(solution)/shard_map/ppermute | solution.py:302
  21.9 0.0 collective-permute-done.1.refs_1_
  21.9 0.1 right.1.right_ref
  22.0 5.8 %all-to-all-done.line_ref = bf16[8,112,256]{2,1,0:T(8,128)(2,1)S(1)} async-done(((bf16[8,112,256]{2,1,0:T(8,128)(2,1)}), bf16[8,112,256]{2,1,0:T(8,128)(2,1)S(1)}, u32[]{:S(2)}, u32[]{:S(2)}) %all-to-all-start) | async-done | bytes 458784 | tf_op jit(solution)/shard_map/all_to_all | solution.py:319
  27.8 0.6 collective-permute-start.5
  28.3 2.9 %collective-permute-start.4 = (bf16[8,112,256]{2,1,0:T(8,128)(2,1)S(1)}, bf16[8,112,256]{2,1,0:T(8,128)(2,1)S(1)}, u32[]{:S(2)}, u32[]{:S(2)}) collective-permute-start(bf16[8,112,256]{2,1,0:T(8,128)(2,1)S(1)} %all-to-all-done.line_ref), channel_id=1, source_target_pairs={{0,16},{16,0},{1,17},{17,1},{2,18},{18,2},{3,19},{19,3},{4,20},{20... | collective-permute-start | bytes 1376264 | tf_op jit(solution)/shard_map/ppermute | solution.py:302
  31.3 4.0 %build.4 = (bf16[2048,2048]{1,0:T(8,128)(2,1)S(1)}, f32[8,32,256]{2,1,0:T(8,128)S(1)}) custom-call(s32[1]{0:T(128)} %bitcast.me_ref.refs_1_, bf16[8,112,256]{2,1,0:T(8,128)(2,1)S(1)} %all-to-all-done.line_ref, bf16[128,2048]{1,0:T(8,128)(2,1)S(1)} %right.1.right_ref), custom_call_target="tpu_custom_call" | custom-call | flops 4294967296 | bytes 8388608 | tf_op jit(solution)/shard_map/build/pallas_call | solution.py:164
  35.3 0.0 collective-permute-done.5.line_ref
  35.3 4.0 %build.5 = (bf16[2048,2048]{1,0:T(8,128)(2,1)S(1)}, f32[8,32,256]{2,1,0:T(8,128)S(1)}) custom-call(s32[1]{0:T(128)} %bitcast.me_ref.refs_1_, bf16[8,112,256]{2,1,0:T(8,128)(2,1)S(1)} %collective-permute-done.5.line_ref, bf16[128,2048]{1,0:T(8,128)(2,1)S(1)} %right.1.right_ref, f32[8,32,256]{2,1,0:T(8,128)S(1)} %get-tuple-element.27.refs_0_), custom_call_target="tpu_custom_call" | custom-call | flops 4294967296 | bytes 8388608 | tf_op jit(solution)/shard_map/build/pallas_call | solution.py:164
  39.3 2.7 %collective-permute-done.4.line_ref = bf16[8,112,256]{2,1,0:T(8,128)(2,1)S(1)} collective-permute-done((bf16[8,112,256]{2,1,0:T(8,128)(2,1)S(1)}, bf16[8,112,256]{2,1,0:T(8,128)(2,1)S(1)}, u32[]{:S(2)}, u32[]{:S(2)}) %collective-permute-start.4) | collective-permute-done | bytes 458784 | tf_op jit(solution)/shard_map/ppermute | solution.py:302
  42.0 0.8 collective-permute-start.6
  42.8 4.0 %build.6 = (bf16[2048,2048]{1,0:T(8,128)(2,1)S(1)}, f32[8,32,256]{2,1,0:T(8,128)S(1)}) custom-call(s32[1]{0:T(128)} %bitcast.me_ref.refs_1_, bf16[8,112,256]{2,1,0:T(8,128)(2,1)S(1)} %collective-permute-done.4.line_ref, bf16[128,2048]{1,0:T(8,128)(2,1)S(1)} %right.1.right_ref, f32[8,32,256]{2,1,0:T(8,128)S(1)} %get-tuple-element.30.refs_0_), custom_call_target="tpu_custom_call" | custom-call | flops 4294967296 | bytes 8388608 | tf_op jit(solution)/shard_map/build/pallas_call | solution.py:164
  46.8 0.0 copy-start
  46.8 0.0 copy-start.1
  46.8 0.0 collective-permute-done.6.line_ref
  46.8 4.0 %build.7 = (bf16[2048,2048]{1,0:T(8,128)(2,1)S(1)}, bf16[8,32,256]{2,1,0:T(8,128)(2,1)S(1)}) custom-call(s32[1]{0:T(128)} %bitcast.me_ref.refs_1_, bf16[8,112,256]{2,1,0:T(8,128)(2,1)S(1)} %collective-permute-done.6.line_ref, bf16[128,2048]{1,0:T(8,128)(2,1)S(1)} %right.1.right_ref, f32[8,32,256]{2,1,0:T(8,128)S(1)} %get-tuple-element.31.refs_0_), custom_call_target="tpu_custom_call" | custom-call | flops 4294967296 | bytes 8388608 | tf_op jit(solution)/shard_map/build/pallas_call | solution.py:164
  50.8 10.1 %all_to_all.30.received_ref = bf16[8,32,256]{2,1,0:T(8,128)(2,1)S(1)} all-to-all(bf16[8,32,256]{2,1,0:T(8,128)(2,1)S(1)} %get-tuple-element.32), channel_id=1, replica_groups=mesh['yl'=2,'x'=4,'yh'=2,'z'=8,'core'=2] {'x','yl'}, dimensions={0} | all-to-all | bytes 262144 | tf_op jit(solution)/shard_map/all_to_all | solution.py:338
  60.9 0.0 copy-done
  60.9 0.0 copy-done.1
  60.9 10.7 %all_to_all.31.vector_ref = bf16[8,32,256]{2,1,0:T(8,128)(2,1)S(1)} all-to-all(bf16[8,32,256]{2,1,0:T(8,128)(2,1)S(1)} %get-tuple-element.33), channel_id=1, replica_groups=mesh['yl'=2,'x'=4,'yh'=2,'z'=8,'core'=2] {'z'}, dimensions={0} | all-to-all | bytes 262144 | tf_op jit(solution)/shard_map/all_to_all | solution.py:346
  71.6 3.0 %collective-permute-start.8 = (bf16[8,32,256]{2,1,0:T(8,128)(2,1)S(1)}, bf16[8,32,256]{2,1,0:T(8,128)(2,1)S(1)}, u32[]{:S(2)}, u32[]{:S(2)}) collective-permute-start(bf16[8,32,256]{2,1,0:T(8,128)(2,1)S(1)} %all_to_all.31.vector_ref), channel_id=1, source_target_pairs={{0,1},{1,0},{2,3},{3,2},{4,5},{5,4},{6,7},{7,6},{8,9},{9,8},{10,11... | collective-permute-start | bytes 393224 | tf_op jit(solution)/shard_map/ppermute | solution.py:302
  74.6 2.6 %collective-permute-start.7 = (bf16[8,32,256]{2,1,0:T(8,128)(2,1)S(1)}, bf16[8,32,256]{2,1,0:T(8,128)(2,1)S(1)}, u32[]{:S(2)}, u32[]{:S(2)}) collective-permute-start(bf16[8,32,256]{2,1,0:T(8,128)(2,1)S(1)} %all_to_all.31.vector_ref), channel_id=1, source_target_pairs={{0,16},{16,0},{1,17},{17,1},{2,18},{18,2},{3,19},{19,3},{4,20},{20... | collective-permute-start | bytes 393224 | tf_op jit(solution)/shard_map/ppermute | solution.py:302
  77.3 1.5 %apply.4.refs_0_ = f32[8,32,256]{2,1,0:T(8,128)S(1)} custom-call(bf16[8,32,256]{2,1,0:T(8,128)(2,1)S(1)} %all_to_all.31.vector_ref, bf16[2048,2048]{1,0:T(8,128)(2,1)S(1)} %get-tuple-element.35.tile_ref), custom_call_target="tpu_custom_call" | custom-call | flops 2147483648 | bytes 8388608 | tf_op jit(solution)/shard_map/apply/pallas_call | solution.py:212
  78.8 0.0 collective-permute-done.8.vector_ref
  78.8 1.5 %apply.5.refs_0_ = f32[8,32,256]{2,1,0:T(8,128)S(1)} custom-call(bf16[8,32,256]{2,1,0:T(8,128)(2,1)S(1)} %collective-permute-done.8.vector_ref, bf16[2048,2048]{1,0:T(8,128)(2,1)S(1)} %get-tuple-element.34.tile_ref, f32[8,32,256]{2,1,0:T(8,128)S(1)} %apply.4.refs_0_), custom_call_target="tpu_custom_call" | custom-call | flops 2147483648 | bytes 8388608 | tf_op jit(solution)/shard_map/apply/pallas_call | solution.py:212
  80.3 0.9 collective-permute-done.7.vector_ref
  81.3 0.8 collective-permute-start.9
  82.1 1.5 %apply.6.refs_0_ = f32[8,32,256]{2,1,0:T(8,128)S(1)} custom-call(bf16[8,32,256]{2,1,0:T(8,128)(2,1)S(1)} %collective-permute-done.7.vector_ref, bf16[2048,2048]{1,0:T(8,128)(2,1)S(1)} %get-tuple-element.38.tile_ref, f32[8,32,256]{2,1,0:T(8,128)S(1)} %apply.5.refs_0_), custom_call_target="tpu_custom_call" | custom-call | flops 2147483648 | bytes 8388608 | tf_op jit(solution)/shard_map/apply/pallas_call | solution.py:212
  83.6 0.0 collective-permute-done.9.vector_ref
  83.6 1.5 %apply.7 = bf16[8,32,256]{2,1,0:T(8,128)(2,1)S(1)} custom-call(bf16[8,32,256]{2,1,0:T(8,128)(2,1)S(1)} %collective-permute-done.9.vector_ref, bf16[2048,2048]{1,0:T(8,128)(2,1)S(1)} %get-tuple-element.37.tile_ref, f32[8,32,256]{2,1,0:T(8,128)S(1)} %apply.6.refs_0_, s32[1]{0:T(128)} %bitcast.me_ref.refs_1_), custom_call_target="tpu_custom_call" | custom-call | flops 2147483648 | bytes 8388608 | tf_op jit(solution)/shard_map/apply/pallas_call | solution.py:212
  85.1 7.7 %all_to_all.32.received_ref = bf16[8,32,256]{2,1,0:T(8,128)(2,1)S(1)} all-to-all(bf16[8,32,256]{2,1,0:T(8,128)(2,1)S(1)} %apply.7), channel_id=1, replica_groups=mesh['yl'=2,'x'=4,'yh'=2,'z'=8,'core'=2] {'x','yl'}, dimensions={0} | all-to-all | bytes 262144 | tf_op jit(solution)/shard_map/all_to_all | solution.py:355
  92.8 0.2 sums.1
  93.0 8.6 %all_to_all.33.received_ref = f32[8,8,128]{2,1,0:T(8,128)S(1)} all-to-all(f32[8,8,128]{2,1,0:T(8,128)S(1)} %get-tuple-element.41), channel_id=1, replica_groups=mesh['yl'=2,'x'=4,'yh'=2,'z'=8,'core'=2] {'x','core'}, dimensions={0} | all-to-all | bytes 65536 | tf_op jit(solution)/shard_map/all_to_all | solution.py:363
  101.6 13.5 %all_to_all.34.received_ref = f32[32,8,128]{2,1,0:T(8,128)S(1)} all-to-all(f32[32,8,128]{2,1,0:T(8,128)S(1)} %spread.1), channel_id=1, replica_groups=mesh['yl'=2,'x'=4,'yh'=2,'z'=8,'core'=2] {'yl','yh','z'}, dimensions={0} | all-to-all | bytes 262144 | tf_op jit(solution)/shard_map/all_to_all | solution.py:365
  115.1 1.0 last.1
  (3 shorter events, 0.0 us)
Async XLA Ops:
  2.3 25.5 %all-to-all-start = ((bf16[8,112,256]{2,1,0:T(8,128)(2,1)}), bf16[8,112,256]{2,1,0:T(8,128)(2,1)S(1)}, u32[]{:S(2)}, u32[]{:S(2)}) async-start(bf16[8,112,256]{2,1,0:T(8,128)(2,1)} %get-tuple-element.23), calls=%async_computation | async-start | bytes 917504 | tf_op jit(solution)/shard_map/all_to_all | solution.py:319
  11.3 3.1 %collective-permute-start = (bf16[1,80,256]{2,1,0:T(8,128)(2,1)}, bf16[1,80,256]{2,1,0:T(8,128)(2,1)S(1)}, u32[]{:S(2)}, u32[]{:S(2)}) collective-permute-start(bf16[1,80,256]{2,1,0:T(8,128)(2,1)} %get-tuple-element.24), channel_id=1, source_target_pairs={{0,128},{128,0},{1,129},{129,1},{2,130},{130,2},{3,131},{131,3},{4... | collective-permute-start | bytes 122888 | tf_op jit(solution)/shard_map/ppermute | solution.py:302
  14.4 4.8 %collective-permute-start.3 = (bf16[2,80,256]{2,1,0:T(8,128)(2,1)S(1)}, bf16[2,80,256]{2,1,0:T(8,128)(2,1)S(1)}, u32[]{:S(2)}, u32[]{:S(2)}) collective-permute-start(bf16[2,80,256]{2,1,0:T(8,128)(2,1)S(1)} %constant_dynamic-update-slice_fusion.refs_0_), channel_id=1, source_target_pairs={{0,96},{32,64},{64,32},{96,0},{1,97},{33,65},{65,33},{97,1},{2,98}... | collective-permute-start | bytes 245768 | tf_op jit(solution)/shard_map/ppermute | solution.py:302
  16.8 5.1 %collective-permute-start.2 = (bf16[2,80,256]{2,1,0:T(8,128)(2,1)S(1)}, bf16[2,80,256]{2,1,0:T(8,128)(2,1)S(1)}, u32[]{:S(2)}, u32[]{:S(2)}) collective-permute-start(bf16[2,80,256]{2,1,0:T(8,128)(2,1)S(1)} %constant_dynamic-update-slice_fusion.refs_0_), channel_id=1, source_target_pairs={{0,64},{32,96},{64,0},{96,32},{1,65},{33,97},{65,1},{97,33},{2,66}... | collective-permute-start | bytes 245768 | tf_op jit(solution)/shard_map/ppermute | solution.py:302
  17.4 4.6 %collective-permute-start.1 = (bf16[2,80,256]{2,1,0:T(8,128)(2,1)S(1)}, bf16[2,80,256]{2,1,0:T(8,128)(2,1)S(1)}, u32[]{:S(2)}, u32[]{:S(2)}) collective-permute-start(bf16[2,80,256]{2,1,0:T(8,128)(2,1)S(1)} %constant_dynamic-update-slice_fusion.refs_0_), channel_id=1, source_target_pairs={{0,32},{32,0},{64,96},{96,64},{1,33},{33,1},{65,97},{97,65},{2,34}... | collective-permute-start | bytes 245768 | tf_op jit(solution)/shard_map/ppermute | solution.py:302
  27.8 7.5 %collective-permute-start.5 = (bf16[8,112,256]{2,1,0:T(8,128)(2,1)S(1)}, bf16[8,112,256]{2,1,0:T(8,128)(2,1)S(1)}, u32[]{:S(2)}, u32[]{:S(2)}) collective-permute-start(bf16[8,112,256]{2,1,0:T(8,128)(2,1)S(1)} %all-to-all-done.line_ref), channel_id=1, source_target_pairs={{0,1},{1,0},{2,3},{3,2},{4,5},{5,4},{6,7},{7,6},{8,9},{9,8},{10,11... | collective-permute-start | bytes 1376264 | tf_op jit(solution)/shard_map/ppermute | solution.py:302
  28.3 13.7 %collective-permute-start.4 = (bf16[8,112,256]{2,1,0:T(8,128)(2,1)S(1)}, bf16[8,112,256]{2,1,0:T(8,128)(2,1)S(1)}, u32[]{:S(2)}, u32[]{:S(2)}) collective-permute-start(bf16[8,112,256]{2,1,0:T(8,128)(2,1)S(1)} %all-to-all-done.line_ref), channel_id=1, source_target_pairs={{0,16},{16,0},{1,17},{17,1},{2,18},{18,2},{3,19},{19,3},{4,20},{20... | collective-permute-start | bytes 1376264 | tf_op jit(solution)/shard_map/ppermute | solution.py:302
  42.0 4.8 %collective-permute-start.6 = (bf16[8,112,256]{2,1,0:T(8,128)(2,1)S(1)}, bf16[8,112,256]{2,1,0:T(8,128)(2,1)S(1)}, u32[]{:S(2)}, u32[]{:S(2)}) collective-permute-start(bf16[8,112,256]{2,1,0:T(8,128)(2,1)S(1)} %collective-permute-done.4.line_ref), channel_id=1, source_target_pairs={{0,1},{1,0},{2,3},{3,2},{4,5},{5,4},{6,7},{7,6},{8,9},{9,8},{10,11... | collective-permute-start | bytes 1376264 | tf_op jit(solution)/shard_map/ppermute | solution.py:302
  46.8 14.1 %copy-start = (f32[32,256]{1,0:T(8,128)S(1)}, f32[32,256]{1,0:T(8,128)}, u32[]{:S(2)}) copy-start(f32[32,256]{1,0:T(8,128)} %start_ref.3) | copy-start | bytes 98308
  46.8 14.1 %copy-start.1 = (f32[32,256]{1,0:T(8,128)S(1)}, f32[32,256]{1,0:T(8,128)}, u32[]{:S(2)}) copy-start(f32[32,256]{1,0:T(8,128)} %targets_ref.1) | copy-start | bytes 98308
  71.6 7.2 %collective-permute-start.8 = (bf16[8,32,256]{2,1,0:T(8,128)(2,1)S(1)}, bf16[8,32,256]{2,1,0:T(8,128)(2,1)S(1)}, u32[]{:S(2)}, u32[]{:S(2)}) collective-permute-start(bf16[8,32,256]{2,1,0:T(8,128)(2,1)S(1)} %all_to_all.31.vector_ref), channel_id=1, source_target_pairs={{0,1},{1,0},{2,3},{3,2},{4,5},{5,4},{6,7},{7,6},{8,9},{9,8},{10,11... | collective-permute-start | bytes 393224 | tf_op jit(solution)/shard_map/ppermute | solution.py:302
  74.6 6.6 %collective-permute-start.7 = (bf16[8,32,256]{2,1,0:T(8,128)(2,1)S(1)}, bf16[8,32,256]{2,1,0:T(8,128)(2,1)S(1)}, u32[]{:S(2)}, u32[]{:S(2)}) collective-permute-start(bf16[8,32,256]{2,1,0:T(8,128)(2,1)S(1)} %all_to_all.31.vector_ref), channel_id=1, source_target_pairs={{0,16},{16,0},{1,17},{17,1},{2,18},{18,2},{3,19},{19,3},{4,20},{20... | collective-permute-start | bytes 393224 | tf_op jit(solution)/shard_map/ppermute | solution.py:302
  81.3 2.3 %collective-permute-start.9 = (bf16[8,32,256]{2,1,0:T(8,128)(2,1)S(1)}, bf16[8,32,256]{2,1,0:T(8,128)(2,1)S(1)}, u32[]{:S(2)}, u32[]{:S(2)}) collective-permute-start(bf16[8,32,256]{2,1,0:T(8,128)(2,1)S(1)} %collective-permute-done.7.vector_ref), channel_id=1, source_target_pairs={{0,1},{1,0},{2,3},{3,2},{4,5},{5,4},{6,7},{7,6},{8,9},{9,8},{10,11... | collective-permute-start | bytes 393224 | tf_op jit(solution)/shard_map/ppermute | solution.py:302

commit v5 on v4

--- a/solution.py
+++ b/solution.py
@@ -12,8 +12,7 @@
 AMP_NUM = 16.0
 
 AXES = ("yl", "x", "yh", "z", "core")
-ROW = ("x", "yl")
-COL = ("yh", "z", "core")
+PLANE = ("x", "yl", "yh")
 LINE = ("z",)
 
 BF16 = jnp.bfloat16
@@ -24,7 +23,6 @@
 
 HEAD = 80
 DEPTH = 128
-WIDE = 1024
 
 
 def scale_of(width):
@@ -103,74 +101,65 @@
     return out.astype(BF16)
 
 
-def right_body(gains, *refs):
-    right_ref = refs[-1]
-    size = refs[0].shape[2]
-    place = 0
-    for ref in refs[:-1]:
-        for n in range(ref.shape[0]):
-            columns = slice(place * size, (place + 1) * size)
-            right_ref[0:64, columns] = ref[n, 0:64, :]
-            right_ref[64:128, columns] = tail_rows(ref[n, 64:80, :], False, gains)
-            place += 1
-
-
-def build_body(scale, me_ref, line_ref, right_ref, *refs, first, last):
-    if not first:
-        carried_ref, refs = refs[0], refs[1:]
-    tile_ref, out_ref, left_ref, vector_ref = refs
+def right_body(gains, block_ref, right_ref):
+    size = block_ref.shape[2]
+    for n in range(block_ref.shape[0]):
+        columns = slice(n * size, (n + 1) * size)
+        right_ref[0:64, columns] = block_ref[n, 0:64, :]
+        right_ref[64:128, columns] = tail_rows(block_ref[n, 64:80, :], False, gains)
+
+
+def left_body(me_ref, line_ref, left_ref, vector_ref):
     blocks, _, size = line_ref.shape
-    per = WIDE // size
     for n in range(blocks):
         rows = line_ref[n, 0:64, :]
         tail = tail_rows(line_ref[n, 64:80, :], True, None)
         left_ref[n * size : (n + 1) * size, :] = jnp.concatenate([rows, tail], axis=0).T
         vector_ref[:, n * size : (n + 1) * size] = line_ref[n, 80:112, :]
 
-    def step(turn, state):
-        columns = pl.ds(pl.multiple_of(turn * WIDE, WIDE), WIDE)
-        right = right_ref[:, columns]
-        for n in range(blocks):
-            power = jnp.dot(
-                left_ref[n * size : (n + 1) * size, :], right, preferred_element_type=F32
-            )
-            tile_ref[n * size : (n + 1) * size, columns] = jnp.exp2(power * scale).astype(BF16)
-        product = jnp.dot(
-            vector_ref[...], tile_ref[:, columns], preferred_element_type=F32
-        )
-        for n in range(per):
-            block = turn * per + n
+
+def build_body(scale, *refs, groups, last):
+    if last:
+        me_ref, refs = refs[0], refs[1:]
+    left_ref, vector_ref, right_refs, refs = refs[0], refs[1], refs[2 : 2 + groups], refs[2 + groups :]
+    carried_refs, tile_refs, out_ref = refs[: -groups - 1], refs[-groups - 1 : -1], refs[-1]
+    points = left_ref.shape[0]
+    size = out_ref.shape[2]
+    place = 0
+    for group in range(groups):
+        right = right_refs[group][...]
+        tile_ref = tile_refs[group]
+        for n in range(0, points, 256):
+            power = jnp.dot(left_ref[n : n + 256, :], right, preferred_element_type=F32)
+            tile_ref[n : n + 256, :] = jnp.exp2(power * scale).astype(BF16)
+        product = jnp.dot(vector_ref[...], tile_ref[...], preferred_element_type=F32)
+        for n in range(product.shape[1] // size):
             value = product[:, n * size : (n + 1) * size]
-            if not first:
-                value = value + carried_ref[block]
             if last:
-                block = block ^ me_ref[0]
-            out_ref[block] = value.astype(out_ref.dtype)
-        return state
-
-    lax.fori_loop(0, right_ref.shape[1] // WIDE, step, 0)
-
-
-def build(line, right, carried, me, scale, last=False):
-    blocks, rows, size = line.shape
-    total = right.shape[1]
-    vectors = rows - HEAD
-    points = blocks * size
-    first = carried is None
-    operands, in_specs = [me, line, right], [SMEM, VMEM, VMEM]
-    if not first:
-        operands.append(carried)
-        in_specs.append(VMEM)
-    return pl.pallas_call(
-        functools.partial(build_body, scale, first=first, last=last),
+                value = (value + carried_refs[group][n]).astype(out_ref.dtype)
+                out_ref[place ^ me_ref[0]] = value
+            else:
+                out_ref[place] = value
+            place += 1
+
+
+def build(left, vector, rights, carried, size, scale, me):
+    points, wide = left.shape[0], rights[0].shape[1]
+    vectors = vector.shape[0]
+    last = carried is not None
+    operands = [left, vector] + rights
+    in_specs = [VMEM] * len(operands)
+    if last:
+        operands = [me] + operands + carried
+        in_specs = [SMEM] + in_specs + [VMEM] * len(carried)
+    total = len(rights) * wide
+    outs = pl.pallas_call(
+        functools.partial(build_body, scale, groups=len(rights), last=last),
         in_specs=in_specs,
-        out_specs=[VMEM] * 2,
-        out_shape=[
-            pltpu.VMEM((points, total), BF16),
-            pltpu.VMEM((total // size, vectors, size), BF16 if last else F32),
-        ],
-        scratch_shapes=[pltpu.VMEM((points, DEPTH), BF16), pltpu.VMEM((vectors, points), BF16)],
-        compiler_params=pltpu.CompilerParams(vmem_limit_bytes=6 << 20),
+        out_specs=[VMEM] * (len(rights) + 1),
+        out_shape=[pltpu.VMEM((points, wide), BF16)] * len(rights)
+        + [pltpu.VMEM((total // size, vectors, size), BF16 if last else F32)],
+        compiler_params=pltpu.CompilerParams(vmem_limit_bytes=8 << 20),
         cost_estimate=pl.CostEstimate(
             flops=2 * points * total * 512,
             bytes_accessed=2 * points * total,
@@ -178,39 +167,41 @@
         ),
         name="build",
     )(*operands)
-
-
-def apply_body(vector_ref, tile_ref, *refs, first, last):
-    if not first:
-        carried_ref, refs = refs[0], refs[1:]
+    return list(outs[:-1]), outs[-1]
+
+
+def apply_body(*refs, tiles, last):
     if last:
         me_ref, refs = refs[0], refs[1:]
-    out_ref, flat_ref = refs
+    vector_ref, tile_refs, refs = refs[0], refs[1 : 1 + tiles], refs[1 + tiles :]
+    out_ref, flat_ref = refs[-2:]
     blocks, _, size = vector_ref.shape
     for n in range(blocks):
         flat_ref[:, n * size : (n + 1) * size] = vector_ref[n]
-    product = jnp.dot(flat_ref[...], tile_ref[...], preferred_element_type=F32)
-    for n in range(out_ref.shape[0]):
-        value = product[:, n * size : (n + 1) * size]
-        if not first:
-            value = value + carried_ref[n]
-        block = n ^ me_ref[0] if last else n
-        out_ref[block] = value.astype(out_ref.dtype)
-
-
-def apply(vector, tile, carried, me):
+    place = 0
+    for tile_ref in tile_refs:
+        product = jnp.dot(flat_ref[...], tile_ref[...], preferred_element_type=F32)
+        for n in range(product.shape[1] // size):
+            value = product[:, n * size : (n + 1) * size]
+            if last:
+                out_ref[place ^ me_ref[0]] = (value + refs[0][place]).astype(out_ref.dtype)
+            else:
+                out_ref[place] = value
+            place += 1
+
+
+def apply(vector, tiles, carried, me):
     blocks, vectors, size = vector.shape
-    points, total = tile.shape
-    first, last = carried is None, me is not None
-    operands, in_specs = [vector, tile], [VMEM, VMEM]
-    if not first:
-        operands.append(carried)
-        in_specs.append(VMEM)
+    points, wide = tiles[0].shape
+    last = carried is not None
+    operands = [vector] + tiles
+    in_specs = [VMEM] * len(operands)
     if last:
-        operands.append(me)
-        in_specs.append(SMEM)
+        operands = [me] + operands + [carried]
+        in_specs = [SMEM] + in_specs + [VMEM]
+    total = len(tiles) * wide
     return pl.pallas_call(
-        functools.partial(apply_body, first=first, last=last),
+        functools.partial(apply_body, tiles=len(tiles), last=last),
         in_specs=in_specs,
         out_specs=VMEM,
         out_shape=pltpu.VMEM((total // size, vectors, size), BF16 if last else F32),
@@ -275,7 +266,7 @@
 def small(body, name, outs, operands):
     return pl.pallas_call(
         body,
-        in_specs=[VMEM] * len(operands),
+        in_specs=[SMEM if operand.size == 1 else VMEM for operand in operands],
         out_specs=[VMEM] * len(outs),
         out_shape=outs,
         compiler_params=pltpu.CompilerParams(vmem_limit_bytes=4 << 20),
@@ -286,16 +277,15 @@
 def per_device(features, groups, targets, start):
     width, size = features.shape
     vectors = start.shape[0]
-    rows = lax.axis_size(ROW)
+    planes = lax.axis_size(PLANE)
     lines = lax.axis_size(LINE)
-    columns = lax.axis_size(COL)
     scale = scale_of(width)
-    amplitude = AMP_NUM / math.sqrt(size * rows * columns)
+    amplitude = AMP_NUM / math.sqrt(size * planes * lines * lax.axis_size("core"))
     gain = -math.log2(RHO) / scale
     gains = constant_pieces(gain)
     shift = 0.5 * (math.log2(amplitude) / scale - gain)
 
-    me = lax.axis_index(ROW).astype(jnp.int32).reshape(1)
+    me = lax.axis_index(PLANE).astype(jnp.int32).reshape(1)
 
     def across(value, axis, step=1):
         count = lax.axis_size(axis)
@@ -317,25 +307,43 @@
         name="pack",
     )(features, groups.reshape(1, size), start)
     line = lax.all_to_all(line, LINE, 0, 0)
-    pair = jnp.concatenate([own, across(own, "yl")], axis=0)
-    parts = [pair] + [across(pair, "x", step) for step in (1, 2, 3)]
-    (right,) = small(
-        functools.partial(right_body, gains),
-        "right",
-        [pltpu.VMEM((DEPTH, rows * size), BF16)],
-        parts,
-    )
-    line, right = lax.optimization_barrier((line, right))
-    far = across(line, "yh")
+    side = [own] + [across(own, ("yl", "yh"), step) for step in (1, 2, 3)]
+    side = jnp.concatenate(side, axis=0)
+    parts = [side] + [across(side, "x", step) for step in (1, 2, 3)]
+
+    def right_of(part):
+        (out,) = small(
+            functools.partial(right_body, gains),
+            "right",
+            [pltpu.VMEM((DEPTH, part.shape[0] * size), BF16)],
+            [part],
+        )
+        return out
+
+    def left_of(value):
+        points = value.shape[0] * size
+        return small(
+            left_body,
+            "left",
+            [pltpu.VMEM((points, DEPTH), BF16), pltpu.VMEM((vectors, points), BF16)],
+            [me, value],
+        )
+
+    rights = [right_of(parts[0])]
+    line, rights[0] = lax.optimization_barrier((line, rights[0]))
     near = across(line, "core")
-    tiles = [None] * 4
-    tiles[0], carried = build(line, right, None, me, scale)
-    tiles[1], carried = build(near, right, carried, me, scale)
-    far, carried = lax.optimization_barrier((far, carried))
-    last = across(far, "core")
-    tiles[2], carried = build(far, right, carried, me, scale)
-    tiles[3], partial_value = build(last, right, carried, me, scale, last=True)
-    received = lax.all_to_all(partial_value, ROW, 0, 0)
+    left, vector = left_of(line)
+    tiles, carried = [None] * 4, [None] * 4
+    for n in range(4):
+        if n > 0:
+            left, part = lax.optimization_barrier((left, parts[n]))
+            rights.append(right_of(part))
+        (tiles[n],), carried[n] = build(left, vector, [rights[n]], None, size, scale, me)
+        left, carried[n] = lax.optimization_barrier((left, carried[n]))
+    near, carried[3] = lax.optimization_barrier((near, carried[3]))
+    left, vector = left_of(near)
+    near_tiles, partial_value = build(left, vector, rights, carried, size, scale, me)
+    received = lax.all_to_all(partial_value, PLANE, 0, 0)
 
     residual0, vector = small(
         first_body,
@@ -344,24 +352,19 @@
         [received, targets, start],
     )
     vector = lax.all_to_all(vector, LINE, 0, 0)
-    far = across(vector, "yh")
     near = across(vector, "core")
-    carried = apply(vector, tiles[0], None, None)
-    carried = apply(near, tiles[1], carried, None)
-    far, carried = lax.optimization_barrier((far, carried))
-    last = across(far, "core")
-    carried = apply(far, tiles[2], carried, None)
-    partial_value = apply(last, tiles[3], carried, me)
-    received = lax.all_to_all(partial_value, ROW, 0, 0)
+    total = apply(vector, tiles, None, me)
+    partial_value = apply(near, near_tiles, total, me)
+    received = lax.all_to_all(partial_value, PLANE, 0, 0)
 
     product, sums = small(
         sums_body,
         "sums",
-        [pltpu.VMEM((vectors, size), F32), pltpu.VMEM((rows, 8, 128), F32)],
+        [pltpu.VMEM((vectors, size), F32), pltpu.VMEM((8, 8, 128), F32)],
         [received, residual0],
     )
     sums = lax.all_to_all(sums, ('x', 'core'), 0, 0)
-    (sums,) = small(spread_body, "spread", [pltpu.VMEM((columns, 8, 128), F32)], [sums])
+    (sums,) = small(spread_body, "spread", [pltpu.VMEM((32, 8, 128), F32)], [sums])
     sums = lax.all_to_all(sums, ('yl', 'yh', 'z'), 0, 0)
     return tuple(
         small(

time: 117 us -> 114 us (0.974)
  blocking collectives: 50.5 us -> 57 us
  waiting for transfers between devices: 14.7 us -> 8.24 us
  starting transfers between devices: 24.3 us -> 22.4 us
    all_to_all x2, blocking collectives: 17.7 us -> 25.8 us  [per_device(): received = lax.all_to_all(partial_value, PLANE, 0, 0)]
    ppermute x10 -> x8, waiting for transfers between devices: 8.97 us -> 3.08 us  [across(): return lax.ppermute(value, axis, [(n, n ^ step) for n in range(count)])]
    ppermute x10 -> x8, starting transfers between devices: 15.3 us -> 13.4 us  [across(): return lax.ppermute(value, axis, [(n, n ^ step) for n in range(count)])]
    all_to_all x1, blocking collectives: 13.5 us -> 12.3 us  [per_device(): sums = lax.all_to_all(sums, ('yl', 'yh', 'z'), 0, 0)]
    pallas_call x13 -> x17, Pallas kernels: 23.4 us -> 22.8 us  [the longest x5 15.1 us: build(): pl.pallas_call(functools.partial(build_body, scale, groups=len(rights), l...]
  transfers between devices with their start and end apart: 11 -> 9, of which waited for: 6 -> 2; matrix products, arithmetic and copies ran while one was open for 1% -> 1% of each run, Pallas kernels for 14% -> 10%
where the time goes in v5:
time: 114 us
  blocking collectives  57 us (50%)
  Pallas kernels  24.4 us (21%)
  starting transfers between devices  22.4 us (20%)
  waiting for transfers between devices  8.24 us (7%)
    all_to_all x2, blocking collectives, per_device(): received = lax.all_to_all(partial_value, PLANE, 0, 0)  25.8 us
    pallas_call x5, Pallas kernels, build(): pl.pallas_call(functools.partial(build_body, scale, groups=len(rights), l...  15.1 us
    ppermute x8, starting transfers between devices, across(): return lax.ppermute(value, axis, [(n, n ^ step) for n in range(count)])  13.4 us
    all_to_all x1, blocking collectives, per_device(): sums = lax.all_to_all(sums, ('yl', 'yh', 'z'), 0, 0)  12.3 us
    all_to_all x1, blocking collectives, per_device(): vector = lax.all_to_all(vector, LINE, 0, 0)  10.3 us
    all_to_all x1, starting transfers between devices, per_device(): line = lax.all_to_all(line, LINE, 0, 0)  9.03 us
    all_to_all x1, blocking collectives, per_device(): sums = lax.all_to_all(sums, ('x', 'core'), 0, 0)  8.66 us
    pallas_call x2, Pallas kernels, apply(): pl.pallas_call(functools.partial(apply_body, tiles=len(tiles), last=last)...  5.92 us
  transfers between devices with their start and end apart: 9, of which 2 were waited for; matrix products, arithmetic and copies ran while one was open for 1% of the time, Pallas kernels for 10%

profile of v5, /device:TPU:1, one launch (start us, length us, event | category | flops | bytes accessed | tf_op | source)
XLA Modules:
  0.0 113.6 jit_solution(2470906439967835840)
XLA Ops:
  0.6 1.6 %pack.1 = (bf16[1,80,256]{2,1,0:T(8,128)(2,1)}, bf16[8,112,256]{2,1,0:T(8,128)(2,1)}) custom-call(bf16[64,256]{1,0:T(8,128)(2,1)} %features_hbm.1, s32[1,256]{1,0:T(1,128)} %bitcast.2, f32[32,256]{1,0:T(8,128)} %start_ref.3), custom_call_target="tpu_custom_call" | custom-call | tf_op jit(solution)/shard_map/pack/pallas_call | solution.py:294
  2.3 9.0 %all-to-all-start = ((bf16[8,112,256]{2,1,0:T(8,128)(2,1)}), bf16[8,112,256]{2,1,0:T(8,128)(2,1)S(1)}, u32[]{:S(2)}, u32[]{:S(2)}) async-start(bf16[8,112,256]{2,1,0:T(8,128)(2,1)} %get-tuple-element.43), calls=%async_computation | async-start | bytes 917504 | tf_op jit(solution)/shard_map/all_to_all | solution.py:309
  11.3 2.7 %collective-permute-start.2 = (bf16[1,80,256]{2,1,0:T(8,128)(2,1)}, bf16[1,80,256]{2,1,0:T(8,128)(2,1)S(1)}, u32[]{:S(2)}, u32[]{:S(2)}) collective-permute-start(bf16[1,80,256]{2,1,0:T(8,128)(2,1)} %get-tuple-element.44), channel_id=1, source_target_pairs={{0,144},{16,128},{128,16},{144,0},{1,145},{17,129},{129,17},{145,1... | collective-permute-start | bytes 122888 | tf_op jit(solution)/shard_map/ppermute | solution.py:292
  14.0 0.0 collective-permute-start.1
  14.0 1.3 %collective-permute-start = (bf16[1,80,256]{2,1,0:T(8,128)(2,1)}, bf16[1,80,256]{2,1,0:T(8,128)(2,1)S(1)}, u32[]{:S(2)}, u32[]{:S(2)}) collective-permute-start(bf16[1,80,256]{2,1,0:T(8,128)(2,1)} %get-tuple-element.44), channel_id=1, source_target_pairs={{0,16},{16,0},{128,144},{144,128},{1,17},{17,1},{129,145},{145,129... | collective-permute-start | bytes 122888 | tf_op jit(solution)/shard_map/ppermute | solution.py:292
  15.3 0.8 constant_dynamic-update-slice_fusion.3
  16.1 3.1 %collective-permute-done = bf16[1,80,256]{2,1,0:T(8,128)(2,1)S(1)} collective-permute-done((bf16[1,80,256]{2,1,0:T(8,128)(2,1)}, bf16[1,80,256]{2,1,0:T(8,128)(2,1)S(1)}, u32[]{:S(2)}, u32[]{:S(2)}) %collective-permute-start) | collective-permute-done | bytes 40992 | tf_op jit(solution)/shard_map/ppermute | solution.py:292
  19.2 0.0 collective-permute-done.1
  19.2 0.0 collective-permute-done.2
  19.2 2.6 %collective-permute-start.6 = (bf16[4,80,256]{2,1,0:T(8,128)(2,1)S(1)}, bf16[4,80,256]{2,1,0:T(8,128)(2,1)S(1)}, u32[]{:S(2)}, u32[]{:S(2)}) collective-permute-start(bf16[4,80,256]{2,1,0:T(8,128)(2,1)S(1)} %constant_dynamic-update-slice_fusion.block_ref), channel_id=1, source_target_pairs={{0,96},{32,64},{64,32},{96,0},{1,97},{33,65},{65,33},{97,1},{2,98}... | collective-permute-start | bytes 491528 | tf_op jit(solution)/shard_map/ppermute | solution.py:292
  21.8 0.5 collective-permute-start.5
  22.3 0.3 collective-permute-start.4
  22.6 5.2 %all-to-all-done.line_ref = bf16[8,112,256]{2,1,0:T(8,128)(2,1)S(1)} async-done(((bf16[8,112,256]{2,1,0:T(8,128)(2,1)}), bf16[8,112,256]{2,1,0:T(8,128)(2,1)S(1)}, u32[]{:S(2)}, u32[]{:S(2)}) %all-to-all-start) | async-done | bytes 458784 | tf_op jit(solution)/shard_map/all_to_all | solution.py:309
  27.8 0.6 collective-permute-start.3
  28.3 0.2 left.2
  28.5 1.9 %build.5 = (bf16[2048,1024]{1,0:T(8,128)(2,1)S(1)}, f32[4,32,256]{2,1,0:T(8,128)S(1)}) custom-call(bf16[2048,128]{1,0:T(8,128)(2,1)S(1)} %get-tuple-element.59.refs_0_, bf16[32,2048]{1,0:T(8,128)(2,1)S(1)} %get-tuple-element.47.refs_1_, bf16[128,1024]{1,0:T(8,128)(2,1)S(1)} %right.4.refs_2_.refs_3_), custom_call_target="tpu_custom_call" | custom-call | flops 2147483648 | bytes 4194304 | tf_op jit(solution)/shard_map/build/pallas_call | solution.py:156
  30.4 0.0 collective-permute-done.4.block_ref
  30.5 1.9 %build.6 = (bf16[2048,1024]{1,0:T(8,128)(2,1)S(1)}, f32[4,32,256]{2,1,0:T(8,128)S(1)}) custom-call(bf16[2048,128]{1,0:T(8,128)(2,1)S(1)} %get-tuple-element.59.refs_0_, bf16[32,2048]{1,0:T(8,128)(2,1)S(1)} %get-tuple-element.47.refs_1_, bf16[128,1024]{1,0:T(8,128)(2,1)S(1)} %right.5.refs_2_.refs_4_), custom_call_target="tpu_custom_call" | custom-call | flops 2147483648 | bytes 4194304 | tf_op jit(solution)/shard_map/build/pallas_call | solution.py:156
  32.4 0.0 collective-permute-done.5.block_ref
  32.4 1.9 %build.7 = (bf16[2048,1024]{1,0:T(8,128)(2,1)S(1)}, f32[4,32,256]{2,1,0:T(8,128)S(1)}) custom-call(bf16[2048,128]{1,0:T(8,128)(2,1)S(1)} %get-tuple-element.59.refs_0_, bf16[32,2048]{1,0:T(8,128)(2,1)S(1)} %get-tuple-element.47.refs_1_, bf16[128,1024]{1,0:T(8,128)(2,1)S(1)} %right.6.refs_2_.refs_5_), custom_call_target="tpu_custom_call" | custom-call | flops 2147483648 | bytes 4194304 | tf_op jit(solution)/shard_map/build/pallas_call | solution.py:156
  34.3 0.0 collective-permute-done.6.block_ref
  34.4 1.9 %build.8 = (bf16[2048,1024]{1,0:T(8,128)(2,1)S(1)}, f32[4,32,256]{2,1,0:T(8,128)S(1)}) custom-call(bf16[2048,128]{1,0:T(8,128)(2,1)S(1)} %get-tuple-element.59.refs_0_, bf16[32,2048]{1,0:T(8,128)(2,1)S(1)} %get-tuple-element.47.refs_1_, bf16[128,1024]{1,0:T(8,128)(2,1)S(1)} %right.7.refs_2_.refs_6_), custom_call_target="tpu_custom_call" | custom-call | flops 2147483648 | bytes 4194304 | tf_op jit(solution)/shard_map/build/pallas_call | solution.py:156
  36.3 0.0 collective-permute-done.3.line_ref
  36.3 0.2 left.3
  36.5 0.0 copy-start
  36.5 0.0 copy-start.1
  36.5 7.5 %build.9 = (bf16[2048,1024]{1,0:T(8,128)(2,1)S(1)}, bf16[2048,1024]{1,0:T(8,128)(2,1)S(1)}, bf16[2048,1024]{1,0:T(8,128)(2,1)S(1)}, bf16[2048,1024]{1,0:T(8,128)(2,1)S(1)}, bf16[16,32,256]{2,1,0:T(8,128)(2,1)S(1)}) custom-call(s32[1]{0:T(128)} %bitcast.me_ref.refs_0_, bf16[2048,128]{1,0:T(8,128)(2,1)S(1)} %get-tuple-element.64.refs_1_, ...), custom_call_target="tpu_custom_call" | custom-call | flops 8589934592 | bytes 16777216 | tf_op jit(solution)/shard_map/build/pallas_call | solution.py:156
  44.0 14.7 %all_to_all.30.received_ref = bf16[16,32,256]{2,1,0:T(8,128)(2,1)S(1)} all-to-all(bf16[16,32,256]{2,1,0:T(8,128)(2,1)S(1)} %get-tuple-element.70), channel_id=1, replica_groups=mesh['yl'=2,'x'=4,'yh'=2,'z'=8,'core'=2] {'x','yl','yh'}, dimensions={0} | all-to-all | bytes 524288 | tf_op jit(solution)/shard_map/all_to_all | solution.py:346
  58.7 0.0 copy-done
  58.7 0.0 copy-done.1
  58.8 10.3 %all_to_all.31.refs_0_ = bf16[8,32,256]{2,1,0:T(8,128)(2,1)S(1)} all-to-all(bf16[8,32,256]{2,1,0:T(8,128)(2,1)S(1)} %get-tuple-element.71), channel_id=1, replica_groups=mesh['yl'=2,'x'=4,'yh'=2,'z'=8,'core'=2] {'z'}, dimensions={0} | all-to-all | bytes 262144 | tf_op jit(solution)/shard_map/all_to_all | solution.py:354
  69.1 5.4 %collective-permute-start.7 = (bf16[8,32,256]{2,1,0:T(8,128)(2,1)S(1)}, bf16[8,32,256]{2,1,0:T(8,128)(2,1)S(1)}, u32[]{:S(2)}, u32[]{:S(2)}) collective-permute-start(bf16[8,32,256]{2,1,0:T(8,128)(2,1)S(1)} %all_to_all.31.refs_0_), channel_id=1, source_target_pairs={{0,1},{1,0},{2,3},{3,2},{4,5},{5,4},{6,7},{7,6},{8,9},{9,8},{10,11... | collective-permute-start | bytes 393224 | tf_op jit(solution)/shard_map/ppermute | solution.py:292
  74.5 2.9 %apply.2.refs_6_ = f32[16,32,256]{2,1,0:T(8,128)S(1)} custom-call(bf16[8,32,256]{2,1,0:T(8,128)(2,1)S(1)} %all_to_all.31.refs_0_, bf16[2048,1024]{1,0:T(8,128)(2,1)S(1)} %get-tuple-element.76.refs_1_, bf16[2048,1024]{1,0:T(8,128)(2,1)S(1)} %get-tuple-element.77.refs_2_, bf16[2048,1024]{1,0:T(8,128)(2,1)S(1)} %get-tuple-element.78.refs_3_, ...), custom_call_target="tpu_custom_call" | custom-call | flops 4294967296 | bytes 16777216 | tf_op jit(solution)/shard_map/apply/pallas_call | solution.py:203
  77.5 0.0 collective-permute-done.7.refs_1_
  77.5 3.0 %apply.3 = bf16[16,32,256]{2,1,0:T(8,128)(2,1)S(1)} custom-call(s32[1]{0:T(128)} %bitcast.me_ref.refs_0_, bf16[8,32,256]{2,1,0:T(8,128)(2,1)S(1)} %collective-permute-done.7.refs_1_, bf16[2048,1024]{1,0:T(8,128)(2,1)S(1)} %get-tuple-element.72.refs_2_, bf16[2048,1024]{1,0:T(8,128)(2,1)S(1)} %get-tuple-element.73.refs_3_, ...), custom_call_target="tpu_custom_call" | custom-call | flops 4294967296 | bytes 16777216 | tf_op jit(solution)/shard_map/apply/pallas_call | solution.py:203
  80.5 11.0 %all_to_all.32.received_ref = bf16[16,32,256]{2,1,0:T(8,128)(2,1)S(1)} all-to-all(bf16[16,32,256]{2,1,0:T(8,128)(2,1)S(1)} %apply.3), channel_id=1, replica_groups=mesh['yl'=2,'x'=4,'yh'=2,'z'=8,'core'=2] {'x','yl','yh'}, dimensions={0} | all-to-all | bytes 524288 | tf_op jit(solution)/shard_map/all_to_all | solution.py:358
  91.5 0.2 sums.1
  91.7 8.7 %all_to_all.33.received_ref = f32[8,8,128]{2,1,0:T(8,128)S(1)} all-to-all(f32[8,8,128]{2,1,0:T(8,128)S(1)} %get-tuple-element.81), channel_id=1, replica_groups=mesh['yl'=2,'x'=4,'yh'=2,'z'=8,'core'=2] {'x','core'}, dimensions={0} | all-to-all | bytes 65536 | tf_op jit(solution)/shard_map/all_to_all | solution.py:366
  100.3 12.3 %all_to_all.34.received_ref = f32[32,8,128]{2,1,0:T(8,128)S(1)} all-to-all(f32[32,8,128]{2,1,0:T(8,128)S(1)} %spread.1), channel_id=1, replica_groups=mesh['yl'=2,'x'=4,'yh'=2,'z'=8,'core'=2] {'yl','yh','z'}, dimensions={0} | all-to-all | bytes 262144 | tf_op jit(solution)/shard_map/all_to_all | solution.py:368
  112.6 1.0 last.1
  (9 shorter events, 0.2 us)
Async XLA Ops:
  2.3 25.5 %all-to-all-start = ((bf16[8,112,256]{2,1,0:T(8,128)(2,1)}), bf16[8,112,256]{2,1,0:T(8,128)(2,1)S(1)}, u32[]{:S(2)}, u32[]{:S(2)}) async-start(bf16[8,112,256]{2,1,0:T(8,128)(2,1)} %get-tuple-element.43), calls=%async_computation | async-start | bytes 917504 | tf_op jit(solution)/shard_map/all_to_all | solution.py:309
  11.3 7.9 %collective-permute-start.2 = (bf16[1,80,256]{2,1,0:T(8,128)(2,1)}, bf16[1,80,256]{2,1,0:T(8,128)(2,1)S(1)}, u32[]{:S(2)}, u32[]{:S(2)}) collective-permute-start(bf16[1,80,256]{2,1,0:T(8,128)(2,1)} %get-tuple-element.44), channel_id=1, source_target_pairs={{0,144},{16,128},{128,16},{144,0},{1,145},{17,129},{129,17},{145,1... | collective-permute-start | bytes 122888 | tf_op jit(solution)/shard_map/ppermute | solution.py:292
  14.0 5.2 %collective-permute-start.1 = (bf16[1,80,256]{2,1,0:T(8,128)(2,1)}, bf16[1,80,256]{2,1,0:T(8,128)(2,1)S(1)}, u32[]{:S(2)}, u32[]{:S(2)}) collective-permute-start(bf16[1,80,256]{2,1,0:T(8,128)(2,1)} %get-tuple-element.44), channel_id=1, source_target_pairs={{0,128},{16,144},{128,0},{144,16},{1,129},{17,145},{129,1},{145,17... | collective-permute-start | bytes 122888 | tf_op jit(solution)/shard_map/ppermute | solution.py:292
  14.0 5.1 %collective-permute-start = (bf16[1,80,256]{2,1,0:T(8,128)(2,1)}, bf16[1,80,256]{2,1,0:T(8,128)(2,1)S(1)}, u32[]{:S(2)}, u32[]{:S(2)}) collective-permute-start(bf16[1,80,256]{2,1,0:T(8,128)(2,1)} %get-tuple-element.44), channel_id=1, source_target_pairs={{0,16},{16,0},{128,144},{144,128},{1,17},{17,1},{129,145},{145,129... | collective-permute-start | bytes 122888 | tf_op jit(solution)/shard_map/ppermute | solution.py:292
  19.2 15.1 %collective-permute-start.6 = (bf16[4,80,256]{2,1,0:T(8,128)(2,1)S(1)}, bf16[4,80,256]{2,1,0:T(8,128)(2,1)S(1)}, u32[]{:S(2)}, u32[]{:S(2)}) collective-permute-start(bf16[4,80,256]{2,1,0:T(8,128)(2,1)S(1)} %constant_dynamic-update-slice_fusion.block_ref), channel_id=1, source_target_pairs={{0,96},{32,64},{64,32},{96,0},{1,97},{33,65},{65,33},{97,1},{2,98}... | collective-permute-start | bytes 491528 | tf_op jit(solution)/shard_map/ppermute | solution.py:292
  21.8 10.6 %collective-permute-start.5 = (bf16[4,80,256]{2,1,0:T(8,128)(2,1)S(1)}, bf16[4,80,256]{2,1,0:T(8,128)(2,1)S(1)}, u32[]{:S(2)}, u32[]{:S(2)}) collective-permute-start(bf16[4,80,256]{2,1,0:T(8,128)(2,1)S(1)} %constant_dynamic-update-slice_fusion.block_ref), channel_id=1, source_target_pairs={{0,64},{32,96},{64,0},{96,32},{1,65},{33,97},{65,1},{97,33},{2,66}... | collective-permute-start | bytes 491528 | tf_op jit(solution)/shard_map/ppermute | solution.py:292
  22.3 8.1 %collective-permute-start.4 = (bf16[4,80,256]{2,1,0:T(8,128)(2,1)S(1)}, bf16[4,80,256]{2,1,0:T(8,128)(2,1)S(1)}, u32[]{:S(2)}, u32[]{:S(2)}) collective-permute-start(bf16[4,80,256]{2,1,0:T(8,128)(2,1)S(1)} %constant_dynamic-update-slice_fusion.block_ref), channel_id=1, source_target_pairs={{0,32},{32,0},{64,96},{96,64},{1,33},{33,1},{65,97},{97,65},{2,34}... | collective-permute-start | bytes 491528 | tf_op jit(solution)/shard_map/ppermute | solution.py:292
  27.8 8.5 %collective-permute-start.3 = (bf16[8,112,256]{2,1,0:T(8,128)(2,1)S(1)}, bf16[8,112,256]{2,1,0:T(8,128)(2,1)S(1)}, u32[]{:S(2)}, u32[]{:S(2)}) collective-permute-start(bf16[8,112,256]{2,1,0:T(8,128)(2,1)S(1)} %all-to-all-done.line_ref), channel_id=1, source_target_pairs={{0,1},{1,0},{2,3},{3,2},{4,5},{5,4},{6,7},{7,6},{8,9},{9,8},{10,11... | collective-permute-start | bytes 1376264 | tf_op jit(solution)/shard_map/ppermute | solution.py:292
  36.5 22.3 %copy-start = (f32[32,256]{1,0:T(8,128)S(1)}, f32[32,256]{1,0:T(8,128)}, u32[]{:S(2)}) copy-start(f32[32,256]{1,0:T(8,128)} %start_ref.3) | copy-start | bytes 98308
  36.5 22.2 %copy-start.1 = (f32[32,256]{1,0:T(8,128)S(1)}, f32[32,256]{1,0:T(8,128)}, u32[]{:S(2)}) copy-start(f32[32,256]{1,0:T(8,128)} %targets_ref.1) | copy-start | bytes 98308
  69.1 8.4 %collective-permute-start.7 = (bf16[8,32,256]{2,1,0:T(8,128)(2,1)S(1)}, bf16[8,32,256]{2,1,0:T(8,128)(2,1)S(1)}, u32[]{:S(2)}, u32[]{:S(2)}) collective-permute-start(bf16[8,32,256]{2,1,0:T(8,128)(2,1)S(1)} %all_to_all.31.refs_0_), channel_id=1, source_target_pairs={{0,1},{1,0},{2,3},{3,2},{4,5},{5,4},{6,7},{7,6},{8,9},{9,8},{10,11... | collective-permute-start | bytes 393224 | tf_op jit(solution)/shard_map/ppermute | solution.py:292

commit v6 on v5

--- a/solution.py
+++ b/solution.py
@@ -126,6 +126,18 @@
     points = left_ref.shape[0]
     size = out_ref.shape[2]
     place = 0
+
+    def put(value):
+        if last:
+            out_ref[place ^ me_ref[0]] = value.astype(out_ref.dtype)
+        else:
+            out_ref[place] = value
+
+    if last:
+        for n in range(carried_refs[0].shape[0]):
+            put(carried_refs[0][n])
+            place += 1
+        carried_refs = carried_refs[1:]
     for group in range(groups):
         right = right_refs[group][...]
         tile_ref = tile_refs[group]
@@ -135,30 +147,28 @@
         product = jnp.dot(vector_ref[...], tile_ref[...], preferred_element_type=F32)
         for n in range(product.shape[1] // size):
             value = product[:, n * size : (n + 1) * size]
-            if last:
-                value = (value + carried_refs[group][n]).astype(out_ref.dtype)
-                out_ref[place ^ me_ref[0]] = value
-            else:
-                out_ref[place] = value
+            if carried_refs:
+                value = value + carried_refs[group][n]
+            put(value)
             place += 1
 
 
-def build(left, vector, rights, carried, size, scale, me):
+def build(left, vector, rights, carried, size, scale, me, last=False):
     points, wide = left.shape[0], rights[0].shape[1]
     vectors = vector.shape[0]
-    last = carried is not None
-    operands = [left, vector] + rights
+    operands = [left, vector] + rights + carried
     in_specs = [VMEM] * len(operands)
     if last:
-        operands = [me] + operands + carried
-        in_specs = [SMEM] + in_specs + [VMEM] * len(carried)
+        operands = [me] + operands
+        in_specs = [SMEM] + in_specs
     total = len(rights) * wide
+    blocks = total // size + (carried[0].shape[0] if last else 0)
     outs = pl.pallas_call(
         functools.partial(build_body, scale, groups=len(rights), last=last),
         in_specs=in_specs,
         out_specs=[VMEM] * (len(rights) + 1),
         out_shape=[pltpu.VMEM((points, wide), BF16)] * len(rights)
-        + [pltpu.VMEM((total // size, vectors, size), BF16 if last else F32)],
+        + [pltpu.VMEM((blocks, vectors, size), BF16 if last else F32)],
         compiler_params=pltpu.CompilerParams(vmem_limit_bytes=8 << 20),
         cost_estimate=pl.CostEstimate(
             flops=2 * points * total * 512,
@@ -309,7 +319,7 @@
     line = lax.all_to_all(line, LINE, 0, 0)
     side = [own] + [across(own, ("yl", "yh"), step) for step in (1, 2, 3)]
     side = jnp.concatenate(side, axis=0)
-    parts = [side] + [across(side, "x", step) for step in (1, 2, 3)]
+    parts = [side, across(side, "x", 1)]
 
     def right_of(part):
         (out,) = small(
@@ -330,19 +340,30 @@
         )
 
     rights = [right_of(parts[0])]
+    side, rights[0] = lax.optimization_barrier((side, rights[0]))
+    parts.append(across(side, "x", 2))
     line, rights[0] = lax.optimization_barrier((line, rights[0]))
     near = across(line, "core")
     left, vector = left_of(line)
     tiles, carried = [None] * 4, [None] * 4
-    for n in range(4):
+    for n in range(3):
         if n > 0:
             left, part = lax.optimization_barrier((left, parts[n]))
             rights.append(right_of(part))
-        (tiles[n],), carried[n] = build(left, vector, [rights[n]], None, size, scale, me)
+        if n == 2:
+            parts.append(across(part, "x", 1))
+        (tiles[n],), carried[n] = build(left, vector, rights[n:], [], size, scale, me)
         left, carried[n] = lax.optimization_barrier((left, carried[n]))
-    near, carried[3] = lax.optimization_barrier((near, carried[3]))
-    left, vector = left_of(near)
-    near_tiles, partial_value = build(left, vector, rights, carried, size, scale, me)
+    near, carried[2] = lax.optimization_barrier((near, carried[2]))
+    near_left, near_vector = left_of(near)
+    near_tiles, done = build(near_left, near_vector, rights, carried[:3], size, scale, me)
+    left, part, done = lax.optimization_barrier((left, parts[3], done))
+    rights.append(right_of(part))
+    tiles[3:], carried[3] = build(left, vector, rights[3:], [], size, scale, me)
+    last_tile, partial_value = build(
+        near_left, near_vector, rights[3:], [done, carried[3]], size, scale, me, last=True
+    )
+    near_tiles = near_tiles + last_tile
     received = lax.all_to_all(partial_value, PLANE, 0, 0)
 
     residual0, vector = small(

time: 114 us -> 112 us (0.982)
    pallas_call x5 -> x6, Pallas kernels: 15.1 us -> 15 us  [build(): pl.pallas_call(functools.partial(build_body, scale, groups=len(rights), l...]
  transfers between devices with their start and end apart: 9 -> 9, of which waited for: 2 -> 2; matrix products, arithmetic and copies ran while one was open for 1% -> 1% of each run, Pallas kernels for 10% -> 13%
where the time goes in v6:
time: 112 us
  blocking collectives  56.6 us (51%)
  Pallas kernels  24.3 us (22%)
  starting transfers between devices  21.8 us (19%)
  waiting for transfers between devices  7.75 us (7%)
    all_to_all x2, blocking collectives, per_device(): received = lax.all_to_all(partial_value, PLANE, 0, 0)  25.4 us
    pallas_call x6, Pallas kernels, build(): pl.pallas_call(functools.partial(build_body, scale, groups=len(rights), l...  15 us
    ppermute x8, starting transfers between devices, across(): return lax.ppermute(value, axis, [(n, n ^ step) for n in range(count)])  12.8 us
    all_to_all x1, blocking collectives, per_device(): sums = lax.all_to_all(sums, ('yl', 'yh', 'z'), 0, 0)  12.3 us
    all_to_all x1, blocking collectives, per_device(): vector = lax.all_to_all(vector, LINE, 0, 0)  10.3 us
    all_to_all x1, starting transfers between devices, per_device(): line = lax.all_to_all(line, LINE, 0, 0)  9.03 us
    all_to_all x1, blocking collectives, per_device(): sums = lax.all_to_all(sums, ('x', 'core'), 0, 0)  8.66 us
    pallas_call x2, Pallas kernels, apply(): pl.pallas_call(functools.partial(apply_body, tiles=len(tiles), last=last)...  5.92 us
  transfers between devices with their start and end apart: 9, of which 2 were waited for; matrix products, arithmetic and copies ran while one was open for 1% of the time, Pallas kernels for 13%

profile of v6, /device:TPU:1, one launch (start us, length us, event | category | flops | bytes accessed | tf_op | source)
XLA Modules:
  0.0 112.0 jit_solution(4754061454542455719)
XLA Ops:
  0.6 1.6 %pack.1 = (bf16[1,80,256]{2,1,0:T(8,128)(2,1)}, bf16[8,112,256]{2,1,0:T(8,128)(2,1)}) custom-call(bf16[64,256]{1,0:T(8,128)(2,1)} %features_hbm.1, s32[1,256]{1,0:T(1,128)} %bitcast.2, f32[32,256]{1,0:T(8,128)} %start_ref.3), custom_call_target="tpu_custom_call" | custom-call | tf_op jit(solution)/shard_map/pack/pallas_call | solution.py:304
  2.3 9.0 %all-to-all-start = ((bf16[8,112,256]{2,1,0:T(8,128)(2,1)}), bf16[8,112,256]{2,1,0:T(8,128)(2,1)S(1)}, u32[]{:S(2)}, u32[]{:S(2)}) async-start(bf16[8,112,256]{2,1,0:T(8,128)(2,1)} %get-tuple-element.46), calls=%async_computation | async-start | bytes 917504 | tf_op jit(solution)/shard_map/all_to_all | solution.py:319
  11.3 2.7 %collective-permute-start.2 = (bf16[1,80,256]{2,1,0:T(8,128)(2,1)}, bf16[1,80,256]{2,1,0:T(8,128)(2,1)S(1)}, u32[]{:S(2)}, u32[]{:S(2)}) collective-permute-start(bf16[1,80,256]{2,1,0:T(8,128)(2,1)} %get-tuple-element.47), channel_id=1, source_target_pairs={{0,144},{16,128},{128,16},{144,0},{1,145},{17,129},{129,17},{145,1... | collective-permute-start | bytes 122888 | tf_op jit(solution)/shard_map/ppermute | solution.py:302
  14.0 0.0 collective-permute-start.1
  14.0 1.3 %collective-permute-start = (bf16[1,80,256]{2,1,0:T(8,128)(2,1)}, bf16[1,80,256]{2,1,0:T(8,128)(2,1)S(1)}, u32[]{:S(2)}, u32[]{:S(2)}) collective-permute-start(bf16[1,80,256]{2,1,0:T(8,128)(2,1)} %get-tuple-element.47), channel_id=1, source_target_pairs={{0,16},{16,0},{128,144},{144,128},{1,17},{17,1},{129,145},{145,129... | collective-permute-start | bytes 122888 | tf_op jit(solution)/shard_map/ppermute | solution.py:302
  15.3 0.8 constant_dynamic-update-slice_fusion.3
  16.1 3.1 %collective-permute-done = bf16[1,80,256]{2,1,0:T(8,128)(2,1)S(1)} collective-permute-done((bf16[1,80,256]{2,1,0:T(8,128)(2,1)}, bf16[1,80,256]{2,1,0:T(8,128)(2,1)S(1)}, u32[]{:S(2)}, u32[]{:S(2)}) %collective-permute-start) | collective-permute-done | bytes 40992 | tf_op jit(solution)/shard_map/ppermute | solution.py:302
  19.2 0.0 collective-permute-done.1
  19.2 0.0 collective-permute-done.2
  19.2 1.3 %collective-permute-start.4 = (bf16[4,80,256]{2,1,0:T(8,128)(2,1)S(1)}, bf16[4,80,256]{2,1,0:T(8,128)(2,1)S(1)}, u32[]{:S(2)}, u32[]{:S(2)}) collective-permute-start(bf16[4,80,256]{2,1,0:T(8,128)(2,1)S(1)} %constant_dynamic-update-slice_fusion.block_ref), channel_id=1, source_target_pairs={{0,32},{32,0},{64,96},{96,64},{1,33},{33,1},{65,97},{97,65},{2,34}... | collective-permute-start | bytes 491528 | tf_op jit(solution)/shard_map/ppermute | solution.py:302
  20.6 2.5 %collective-permute-start.5 = (bf16[4,80,256]{2,1,0:T(8,128)(2,1)S(1)}, bf16[4,80,256]{2,1,0:T(8,128)(2,1)S(1)}, u32[]{:S(2)}, u32[]{:S(2)}) collective-permute-start(bf16[4,80,256]{2,1,0:T(8,128)(2,1)S(1)} %constant_dynamic-update-slice_fusion.block_ref), channel_id=1, source_target_pairs={{0,64},{32,96},{64,0},{96,32},{1,65},{33,97},{65,1},{97,33},{2,66}... | collective-permute-start | bytes 491528 | tf_op jit(solution)/shard_map/ppermute | solution.py:302
  23.1 4.7 %all-to-all-done.line_ref = bf16[8,112,256]{2,1,0:T(8,128)(2,1)S(1)} async-done(((bf16[8,112,256]{2,1,0:T(8,128)(2,1)}), bf16[8,112,256]{2,1,0:T(8,128)(2,1)S(1)}, u32[]{:S(2)}, u32[]{:S(2)}) %all-to-all-start) | async-done | bytes 458784 | tf_op jit(solution)/shard_map/all_to_all | solution.py:319
  27.8 0.6 collective-permute-start.3
  28.3 0.2 left.2
  28.5 1.9 %build.6 = (bf16[2048,1024]{1,0:T(8,128)(2,1)S(1)}, f32[4,32,256]{2,1,0:T(8,128)S(1)}) custom-call(bf16[2048,128]{1,0:T(8,128)(2,1)S(1)} %get-tuple-element.74.refs_0_, bf16[32,2048]{1,0:T(8,128)(2,1)S(1)} %get-tuple-element.51.refs_1_, bf16[128,1024]{1,0:T(8,128)(2,1)S(1)} %right.4.refs_2_), custom_call_target="tpu_custom_call" | custom-call | flops 2147483648 | bytes 4194304 | tf_op jit(solution)/shard_map/build/pallas_call | solution.py:166
  30.4 0.0 collective-permute-done.4.block_ref
  30.5 1.9 %build.7 = (bf16[2048,1024]{1,0:T(8,128)(2,1)S(1)}, f32[4,32,256]{2,1,0:T(8,128)S(1)}) custom-call(bf16[2048,128]{1,0:T(8,128)(2,1)S(1)} %get-tuple-element.74.refs_0_, bf16[32,2048]{1,0:T(8,128)(2,1)S(1)} %get-tuple-element.51.refs_1_, bf16[128,1024]{1,0:T(8,128)(2,1)S(1)} %right.5.refs_2_.refs_3_), custom_call_target="tpu_custom_call" | custom-call | flops 2147483648 | bytes 4194304 | tf_op jit(solution)/shard_map/build/pallas_call | solution.py:166
  32.4 0.0 collective-permute-done.5.block_ref
  32.4 1.5 %collective-permute-start.6 = (bf16[4,80,256]{2,1,0:T(8,128)(2,1)S(1)}, bf16[4,80,256]{2,1,0:T(8,128)(2,1)S(1)}, u32[]{:S(2)}, u32[]{:S(2)}) collective-permute-start(bf16[4,80,256]{2,1,0:T(8,128)(2,1)S(1)} %collective-permute-done.5.block_ref), channel_id=1, source_target_pairs={{0,32},{32,0},{64,96},{96,64},{1,33},{33,1},{65,97},{97,65},{2,34}... | collective-permute-start | bytes 491528 | tf_op jit(solution)/shard_map/ppermute | solution.py:302
  33.9 1.9 %build.8 = (bf16[2048,1024]{1,0:T(8,128)(2,1)S(1)}, f32[4,32,256]{2,1,0:T(8,128)S(1)}) custom-call(bf16[2048,128]{1,0:T(8,128)(2,1)S(1)} %get-tuple-element.74.refs_0_, bf16[32,2048]{1,0:T(8,128)(2,1)S(1)} %get-tuple-element.51.refs_1_, bf16[128,1024]{1,0:T(8,128)(2,1)S(1)} %right.6.refs_2_.refs_4_), custom_call_target="tpu_custom_call" | custom-call | flops 2147483648 | bytes 4194304 | tf_op jit(solution)/shard_map/build/pallas_call | solution.py:166
  35.8 0.0 collective-permute-done.3.line_ref
  35.8 0.2 left.3
  36.0 5.5 %build.9 = (bf16[2048,1024]{1,0:T(8,128)(2,1)S(1)}, bf16[2048,1024]{1,0:T(8,128)(2,1)S(1)}, bf16[2048,1024]{1,0:T(8,128)(2,1)S(1)}, f32[12,32,256]{2,1,0:T(8,128)S(1)}) custom-call(bf16[2048,128]{1,0:T(8,128)(2,1)S(1)} %get-tuple-element.65.refs_0_.refs_1_, bf16[32,2048]{1,0:T(8,128)(2,1)S(1)} %get-tuple-element.66.refs_1_.refs_2_, ...), custom_call_target="tpu_custom_call" | custom-call | flops 6442450944 | bytes 12582912 | tf_op jit(solution)/shard_map/build/pallas_call | solution.py:166
  41.5 0.0 collective-permute-done.6.block_ref
  41.6 1.9 %build.10 = (bf16[2048,1024]{1,0:T(8,128)(2,1)S(1)}, f32[4,32,256]{2,1,0:T(8,128)S(1)}) custom-call(bf16[2048,128]{1,0:T(8,128)(2,1)S(1)} %get-tuple-element.74.refs_0_, bf16[32,2048]{1,0:T(8,128)(2,1)S(1)} %get-tuple-element.51.refs_1_, bf16[128,1024]{1,0:T(8,128)(2,1)S(1)} %right.7.refs_2_.refs_3_), custom_call_target="tpu_custom_call" | custom-call | flops 2147483648 | bytes 4194304 | tf_op jit(solution)/shard_map/build/pallas_call | solution.py:166
  43.5 0.0 copy-start
  43.5 0.0 copy-start.1
  43.5 1.9 %build.11 = (bf16[2048,1024]{1,0:T(8,128)(2,1)S(1)}, bf16[16,32,256]{2,1,0:T(8,128)(2,1)S(1)}) custom-call(s32[1]{0:T(128)} %bitcast.me_ref.refs_0_, bf16[2048,128]{1,0:T(8,128)(2,1)S(1)} %get-tuple-element.65.refs_0_.refs_1_, bf16[32,2048]{1,0:T(8,128)(2,1)S(1)} %get-tuple-element.66.refs_1_.refs_2_, bf16[128,1024]{1,0:T(8,128)(2,1)S(1)} %right.7.refs_2_.refs_3_, ...), custom_call_target="tpu_custom_call" | custom-call | flops 2147483648 | bytes 4194304 | tf_op jit(solution)/shard_map/build/pallas_call | solution.py:166
  45.4 14.3 %all_to_all.30.received_ref = bf16[16,32,256]{2,1,0:T(8,128)(2,1)S(1)} all-to-all(bf16[16,32,256]{2,1,0:T(8,128)(2,1)S(1)} %get-tuple-element.76), channel_id=1, replica_groups=mesh['yl'=2,'x'=4,'yh'=2,'z'=8,'core'=2] {'x','yl','yh'}, dimensions={0} | all-to-all | bytes 524288 | tf_op jit(solution)/shard_map/all_to_all | solution.py:367
  59.7 0.0 copy-done
  59.7 0.0 copy-done.1
  59.8 10.3 %all_to_all.31.refs_0_ = bf16[8,32,256]{2,1,0:T(8,128)(2,1)S(1)} all-to-all(bf16[8,32,256]{2,1,0:T(8,128)(2,1)S(1)} %get-tuple-element.77), channel_id=1, replica_groups=mesh['yl'=2,'x'=4,'yh'=2,'z'=8,'core'=2] {'z'}, dimensions={0} | all-to-all | bytes 262144 | tf_op jit(solution)/shard_map/all_to_all | solution.py:375
  70.1 2.8 %collective-permute-start.7 = (bf16[8,32,256]{2,1,0:T(8,128)(2,1)S(1)}, bf16[8,32,256]{2,1,0:T(8,128)(2,1)S(1)}, u32[]{:S(2)}, u32[]{:S(2)}) collective-permute-start(bf16[8,32,256]{2,1,0:T(8,128)(2,1)S(1)} %all_to_all.31.refs_0_), channel_id=1, source_target_pairs={{0,1},{1,0},{2,3},{3,2},{4,5},{5,4},{6,7},{7,6},{8,9},{9,8},{10,11... | collective-permute-start | bytes 393224 | tf_op jit(solution)/shard_map/ppermute | solution.py:302
  72.9 2.9 %apply.2.refs_6_ = f32[16,32,256]{2,1,0:T(8,128)S(1)} custom-call(bf16[8,32,256]{2,1,0:T(8,128)(2,1)S(1)} %all_to_all.31.refs_0_, bf16[2048,1024]{1,0:T(8,128)(2,1)S(1)} %get-tuple-element.82.refs_1_, bf16[2048,1024]{1,0:T(8,128)(2,1)S(1)} %get-tuple-element.83.refs_2_, bf16[2048,1024]{1,0:T(8,128)(2,1)S(1)} %get-tuple-element.84.refs_3_, ...), custom_call_target="tpu_custom_call" | custom-call | flops 4294967296 | bytes 16777216 | tf_op jit(solution)/shard_map/apply/pallas_call | solution.py:213
  75.9 0.0 collective-permute-done.7.refs_1_
  75.9 3.0 %apply.3 = bf16[16,32,256]{2,1,0:T(8,128)(2,1)S(1)} custom-call(s32[1]{0:T(128)} %bitcast.me_ref.refs_0_, bf16[8,32,256]{2,1,0:T(8,128)(2,1)S(1)} %collective-permute-done.7.refs_1_, bf16[2048,1024]{1,0:T(8,128)(2,1)S(1)} %get-tuple-element.78.refs_2_, bf16[2048,1024]{1,0:T(8,128)(2,1)S(1)} %get-tuple-element.79.refs_3_, ...), custom_call_target="tpu_custom_call" | custom-call | flops 4294967296 | bytes 16777216 | tf_op jit(solution)/shard_map/apply/pallas_call | solution.py:213
  78.8 11.0 %all_to_all.32.received_ref = bf16[16,32,256]{2,1,0:T(8,128)(2,1)S(1)} all-to-all(bf16[16,32,256]{2,1,0:T(8,128)(2,1)S(1)} %apply.3), channel_id=1, replica_groups=mesh['yl'=2,'x'=4,'yh'=2,'z'=8,'core'=2] {'x','yl','yh'}, dimensions={0} | all-to-all | bytes 524288 | tf_op jit(solution)/shard_map/all_to_all | solution.py:379
  89.9 0.2 sums.1
  90.0 8.7 %all_to_all.33.received_ref = f32[8,8,128]{2,1,0:T(8,128)S(1)} all-to-all(f32[8,8,128]{2,1,0:T(8,128)S(1)} %get-tuple-element.87), channel_id=1, replica_groups=mesh['yl'=2,'x'=4,'yh'=2,'z'=8,'core'=2] {'x','core'}, dimensions={0} | all-to-all | bytes 65536 | tf_op jit(solution)/shard_map/all_to_all | solution.py:387
  98.7 12.3 %all_to_all.34.received_ref = f32[32,8,128]{2,1,0:T(8,128)S(1)} all-to-all(f32[32,8,128]{2,1,0:T(8,128)S(1)} %spread.1), channel_id=1, replica_groups=mesh['yl'=2,'x'=4,'yh'=2,'z'=8,'core'=2] {'yl','yh','z'}, dimensions={0} | all-to-all | bytes 262144 | tf_op jit(solution)/shard_map/all_to_all | solution.py:389
  111.0 1.0 last.1
  (9 shorter events, 0.2 us)
Async XLA Ops:
  2.3 25.5 %all-to-all-start = ((bf16[8,112,256]{2,1,0:T(8,128)(2,1)}), bf16[8,112,256]{2,1,0:T(8,128)(2,1)S(1)}, u32[]{:S(2)}, u32[]{:S(2)}) async-start(bf16[8,112,256]{2,1,0:T(8,128)(2,1)} %get-tuple-element.46), calls=%async_computation | async-start | bytes 917504 | tf_op jit(solution)/shard_map/all_to_all | solution.py:319
  11.3 7.9 %collective-permute-start.2 = (bf16[1,80,256]{2,1,0:T(8,128)(2,1)}, bf16[1,80,256]{2,1,0:T(8,128)(2,1)S(1)}, u32[]{:S(2)}, u32[]{:S(2)}) collective-permute-start(bf16[1,80,256]{2,1,0:T(8,128)(2,1)} %get-tuple-element.47), channel_id=1, source_target_pairs={{0,144},{16,128},{128,16},{144,0},{1,145},{17,129},{129,17},{145,1... | collective-permute-start | bytes 122888 | tf_op jit(solution)/shard_map/ppermute | solution.py:302
  14.0 5.2 %collective-permute-start.1 = (bf16[1,80,256]{2,1,0:T(8,128)(2,1)}, bf16[1,80,256]{2,1,0:T(8,128)(2,1)S(1)}, u32[]{:S(2)}, u32[]{:S(2)}) collective-permute-start(bf16[1,80,256]{2,1,0:T(8,128)(2,1)} %get-tuple-element.47), channel_id=1, source_target_pairs={{0,128},{16,144},{128,0},{144,16},{1,129},{17,145},{129,1},{145,17... | collective-permute-start | bytes 122888 | tf_op jit(solution)/shard_map/ppermute | solution.py:302
  14.0 5.1 %collective-permute-start = (bf16[1,80,256]{2,1,0:T(8,128)(2,1)}, bf16[1,80,256]{2,1,0:T(8,128)(2,1)S(1)}, u32[]{:S(2)}, u32[]{:S(2)}) collective-permute-start(bf16[1,80,256]{2,1,0:T(8,128)(2,1)} %get-tuple-element.47), channel_id=1, source_target_pairs={{0,16},{16,0},{128,144},{144,128},{1,17},{17,1},{129,145},{145,129... | collective-permute-start | bytes 122888 | tf_op jit(solution)/shard_map/ppermute | solution.py:302
  19.2 11.2 %collective-permute-start.4 = (bf16[4,80,256]{2,1,0:T(8,128)(2,1)S(1)}, bf16[4,80,256]{2,1,0:T(8,128)(2,1)S(1)}, u32[]{:S(2)}, u32[]{:S(2)}) collective-permute-start(bf16[4,80,256]{2,1,0:T(8,128)(2,1)S(1)} %constant_dynamic-update-slice_fusion.block_ref), channel_id=1, source_target_pairs={{0,32},{32,0},{64,96},{96,64},{1,33},{33,1},{65,97},{97,65},{2,34}... | collective-permute-start | bytes 491528 | tf_op jit(solution)/shard_map/ppermute | solution.py:302
  20.6 11.8 %collective-permute-start.5 = (bf16[4,80,256]{2,1,0:T(8,128)(2,1)S(1)}, bf16[4,80,256]{2,1,0:T(8,128)(2,1)S(1)}, u32[]{:S(2)}, u32[]{:S(2)}) collective-permute-start(bf16[4,80,256]{2,1,0:T(8,128)(2,1)S(1)} %constant_dynamic-update-slice_fusion.block_ref), channel_id=1, source_target_pairs={{0,64},{32,96},{64,0},{96,32},{1,65},{33,97},{65,1},{97,33},{2,66}... | collective-permute-start | bytes 491528 | tf_op jit(solution)/shard_map/ppermute | solution.py:302
  27.8 8.1 %collective-permute-start.3 = (bf16[8,112,256]{2,1,0:T(8,128)(2,1)S(1)}, bf16[8,112,256]{2,1,0:T(8,128)(2,1)S(1)}, u32[]{:S(2)}, u32[]{:S(2)}) collective-permute-start(bf16[8,112,256]{2,1,0:T(8,128)(2,1)S(1)} %all-to-all-done.line_ref), channel_id=1, source_target_pairs={{0,1},{1,0},{2,3},{3,2},{4,5},{5,4},{6,7},{7,6},{8,9},{9,8},{10,11... | collective-permute-start | bytes 1376264 | tf_op jit(solution)/shard_map/ppermute | solution.py:302
  32.4 9.1 %collective-permute-start.6 = (bf16[4,80,256]{2,1,0:T(8,128)(2,1)S(1)}, bf16[4,80,256]{2,1,0:T(8,128)(2,1)S(1)}, u32[]{:S(2)}, u32[]{:S(2)}) collective-permute-start(bf16[4,80,256]{2,1,0:T(8,128)(2,1)S(1)} %collective-permute-done.5.block_ref), channel_id=1, source_target_pairs={{0,32},{32,0},{64,96},{96,64},{1,33},{33,1},{65,97},{97,65},{2,34}... | collective-permute-start | bytes 491528 | tf_op jit(solution)/shard_map/ppermute | solution.py:302
  43.5 16.2 %copy-start = (f32[32,256]{1,0:T(8,128)S(1)}, f32[32,256]{1,0:T(8,128)}, u32[]{:S(2)}) copy-start(f32[32,256]{1,0:T(8,128)} %start_ref.3) | copy-start | bytes 98308
  43.5 16.2 %copy-start.1 = (f32[32,256]{1,0:T(8,128)S(1)}, f32[32,256]{1,0:T(8,128)}, u32[]{:S(2)}) copy-start(f32[32,256]{1,0:T(8,128)} %targets_ref.1) | copy-start | bytes 98308
  70.1 5.8 %collective-permute-start.7 = (bf16[8,32,256]{2,1,0:T(8,128)(2,1)S(1)}, bf16[8,32,256]{2,1,0:T(8,128)(2,1)S(1)}, u32[]{:S(2)}, u32[]{:S(2)}) collective-permute-start(bf16[8,32,256]{2,1,0:T(8,128)(2,1)S(1)} %all_to_all.31.refs_0_), channel_id=1, source_target_pairs={{0,1},{1,0},{2,3},{3,2},{4,5},{5,4},{6,7},{7,6},{8,9},{9,8},{10,11... | collective-permute-start | bytes 393224 | tf_op jit(solution)/shard_map/ppermute | solution.py:302

commit v7 on v6

--- a/solution.py
+++ b/solution.py
@@ -12,7 +12,7 @@
 AMP_NUM = 16.0
 
 AXES = ("yl", "x", "yh", "z", "core")
-PLANE = ("x", "yl", "yh")
+PLANE = ("x", "yh", "yl")
 LINE = ("z",)
 
 BF16 = jnp.bfloat16
@@ -317,7 +317,7 @@
         name="pack",
     )(features, groups.reshape(1, size), start)
     line = lax.all_to_all(line, LINE, 0, 0)
-    side = [own] + [across(own, ("yl", "yh"), step) for step in (1, 2, 3)]
+    side = [own] + [across(own, ("yl", "yh"), step) for step in (2, 1, 3)]
     side = jnp.concatenate(side, axis=0)
     parts = [side, across(side, "x", 1)]
 
@@ -386,7 +386,7 @@
     )
     sums = lax.all_to_all(sums, ('x', 'core'), 0, 0)
     (sums,) = small(spread_body, "spread", [pltpu.VMEM((32, 8, 128), F32)], [sums])
-    sums = lax.all_to_all(sums, ('yl', 'yh', 'z'), 0, 0)
+    sums = lax.all_to_all(sums, ('yh', 'yl', 'z'), 0, 0)
     return tuple(
         small(
             last_body,

time: 112 us -> 112 us (level)
  transfers between devices with their start and end apart: 9 -> 9, of which waited for: 2 -> 3; matrix products, arithmetic and copies ran while one was open for 1% -> 1% of each run, Pallas kernels for 13% -> 13%
where the time goes in v7:
time: 112 us
  blocking collectives  56.1 us (50%)
  Pallas kernels  24.3 us (22%)
  starting transfers between devices  21.3 us (19%)
  waiting for transfers between devices  8.37 us (7%)
    all_to_all x2, blocking collectives, per_device(): received = lax.all_to_all(partial_value, PLANE, 0, 0)  24.9 us
    pallas_call x6, Pallas kernels, build(): pl.pallas_call(functools.partial(build_body, scale, groups=len(rights), l...  15 us
    ppermute x8, starting transfers between devices, across(): return lax.ppermute(value, axis, [(n, n ^ step) for n in range(count)])  12.3 us
    all_to_all x1, blocking collectives, per_device(): sums = lax.all_to_all(sums, ('yh', 'yl', 'z'), 0, 0)  12.1 us
    all_to_all x1, blocking collectives, per_device(): vector = lax.all_to_all(vector, LINE, 0, 0)  10.3 us
    all_to_all x1, starting transfers between devices, per_device(): line = lax.all_to_all(line, LINE, 0, 0)  9.03 us
    all_to_all x1, blocking collectives, per_device(): sums = lax.all_to_all(sums, ('x', 'core'), 0, 0)  8.72 us
    pallas_call x2, Pallas kernels, apply(): pl.pallas_call(functools.partial(apply_body, tiles=len(tiles), last=last)...  5.92 us
  transfers between devices with their start and end apart: 9, of which 3 were waited for; matrix products, arithmetic and copies ran while one was open for 1% of the time, Pallas kernels for 13%

profile of v7, /device:TPU:1, one launch (start us, length us, event | category | flops | bytes accessed | tf_op | source)
XLA Modules:
  0.0 111.6 jit_solution(18440130534213914353)
XLA Ops:
  0.6 1.6 %pack.1 = (bf16[1,80,256]{2,1,0:T(8,128)(2,1)}, bf16[8,112,256]{2,1,0:T(8,128)(2,1)}) custom-call(bf16[64,256]{1,0:T(8,128)(2,1)} %features_hbm.1, s32[1,256]{1,0:T(1,128)} %bitcast.2, f32[32,256]{1,0:T(8,128)} %start_ref.3), custom_call_target="tpu_custom_call" | custom-call | tf_op jit(solution)/shard_map/pack/pallas_call | solution.py:304
  2.3 9.0 %all-to-all-start = ((bf16[8,112,256]{2,1,0:T(8,128)(2,1)}), bf16[8,112,256]{2,1,0:T(8,128)(2,1)S(1)}, u32[]{:S(2)}, u32[]{:S(2)}) async-start(bf16[8,112,256]{2,1,0:T(8,128)(2,1)} %get-tuple-element.46), calls=%async_computation | async-start | bytes 917504 | tf_op jit(solution)/shard_map/all_to_all | solution.py:319
  11.3 2.7 %collective-permute-start.2 = (bf16[1,80,256]{2,1,0:T(8,128)(2,1)}, bf16[1,80,256]{2,1,0:T(8,128)(2,1)S(1)}, u32[]{:S(2)}, u32[]{:S(2)}) collective-permute-start(bf16[1,80,256]{2,1,0:T(8,128)(2,1)} %get-tuple-element.47), channel_id=1, source_target_pairs={{0,144},{16,128},{128,16},{144,0},{1,145},{17,129},{129,17},{145,1... | collective-permute-start | bytes 122888 | tf_op jit(solution)/shard_map/ppermute | solution.py:302
  14.0 0.3 collective-permute-start.1
  14.4 0.3 collective-permute-start
  14.7 0.8 constant_dynamic-update-slice_fusion.3
  15.5 2.3 %collective-permute-done = bf16[1,80,256]{2,1,0:T(8,128)(2,1)S(1)} collective-permute-done((bf16[1,80,256]{2,1,0:T(8,128)(2,1)}, bf16[1,80,256]{2,1,0:T(8,128)(2,1)S(1)}, u32[]{:S(2)}, u32[]{:S(2)}) %collective-permute-start) | collective-permute-done | bytes 40992 | tf_op jit(solution)/shard_map/ppermute | solution.py:302
  17.9 1.0 collective-permute-done.1
  18.9 0.0 collective-permute-done.2
  18.9 1.3 %collective-permute-start.4 = (bf16[4,80,256]{2,1,0:T(8,128)(2,1)S(1)}, bf16[4,80,256]{2,1,0:T(8,128)(2,1)S(1)}, u32[]{:S(2)}, u32[]{:S(2)}) collective-permute-start(bf16[4,80,256]{2,1,0:T(8,128)(2,1)S(1)} %constant_dynamic-update-slice_fusion.block_ref), channel_id=1, source_target_pairs={{0,32},{32,0},{64,96},{96,64},{1,33},{33,1},{65,97},{97,65},{2,34}... | collective-permute-start | bytes 491528 | tf_op jit(solution)/shard_map/ppermute | solution.py:302
  20.2 2.5 %collective-permute-start.5 = (bf16[4,80,256]{2,1,0:T(8,128)(2,1)S(1)}, bf16[4,80,256]{2,1,0:T(8,128)(2,1)S(1)}, u32[]{:S(2)}, u32[]{:S(2)}) collective-permute-start(bf16[4,80,256]{2,1,0:T(8,128)(2,1)S(1)} %constant_dynamic-update-slice_fusion.block_ref), channel_id=1, source_target_pairs={{0,64},{32,96},{64,0},{96,32},{1,65},{33,97},{65,1},{97,33},{2,66}... | collective-permute-start | bytes 491528 | tf_op jit(solution)/shard_map/ppermute | solution.py:302
  22.8 5.0 %all-to-all-done.line_ref = bf16[8,112,256]{2,1,0:T(8,128)(2,1)S(1)} async-done(((bf16[8,112,256]{2,1,0:T(8,128)(2,1)}), bf16[8,112,256]{2,1,0:T(8,128)(2,1)S(1)}, u32[]{:S(2)}, u32[]{:S(2)}) %all-to-all-start) | async-done | bytes 458784 | tf_op jit(solution)/shard_map/all_to_all | solution.py:319
  27.8 0.6 collective-permute-start.3
  28.3 0.2 left.2
  28.5 1.9 %build.6 = (bf16[2048,1024]{1,0:T(8,128)(2,1)S(1)}, f32[4,32,256]{2,1,0:T(8,128)S(1)}) custom-call(bf16[2048,128]{1,0:T(8,128)(2,1)S(1)} %get-tuple-element.74.refs_0_, bf16[32,2048]{1,0:T(8,128)(2,1)S(1)} %get-tuple-element.51.refs_1_, bf16[128,1024]{1,0:T(8,128)(2,1)S(1)} %right.4.refs_2_), custom_call_target="tpu_custom_call" | custom-call | flops 2147483648 | bytes 4194304 | tf_op jit(solution)/shard_map/build/pallas_call | solution.py:166
  30.4 0.0 collective-permute-done.4.block_ref
  30.5 1.9 %build.7 = (bf16[2048,1024]{1,0:T(8,128)(2,1)S(1)}, f32[4,32,256]{2,1,0:T(8,128)S(1)}) custom-call(bf16[2048,128]{1,0:T(8,128)(2,1)S(1)} %get-tuple-element.74.refs_0_, bf16[32,2048]{1,0:T(8,128)(2,1)S(1)} %get-tuple-element.51.refs_1_, bf16[128,1024]{1,0:T(8,128)(2,1)S(1)} %right.5.refs_2_.refs_3_), custom_call_target="tpu_custom_call" | custom-call | flops 2147483648 | bytes 4194304 | tf_op jit(solution)/shard_map/build/pallas_call | solution.py:166
  32.4 0.0 collective-permute-done.5.block_ref
  32.4 1.5 %collective-permute-start.6 = (bf16[4,80,256]{2,1,0:T(8,128)(2,1)S(1)}, bf16[4,80,256]{2,1,0:T(8,128)(2,1)S(1)}, u32[]{:S(2)}, u32[]{:S(2)}) collective-permute-start(bf16[4,80,256]{2,1,0:T(8,128)(2,1)S(1)} %collective-permute-done.5.block_ref), channel_id=1, source_target_pairs={{0,32},{32,0},{64,96},{96,64},{1,33},{33,1},{65,97},{97,65},{2,34}... | collective-permute-start | bytes 491528 | tf_op jit(solution)/shard_map/ppermute | solution.py:302
  33.9 1.9 %build.8 = (bf16[2048,1024]{1,0:T(8,128)(2,1)S(1)}, f32[4,32,256]{2,1,0:T(8,128)S(1)}) custom-call(bf16[2048,128]{1,0:T(8,128)(2,1)S(1)} %get-tuple-element.74.refs_0_, bf16[32,2048]{1,0:T(8,128)(2,1)S(1)} %get-tuple-element.51.refs_1_, bf16[128,1024]{1,0:T(8,128)(2,1)S(1)} %right.6.refs_2_.refs_4_), custom_call_target="tpu_custom_call" | custom-call | flops 2147483648 | bytes 4194304 | tf_op jit(solution)/shard_map/build/pallas_call | solution.py:166
  35.8 0.0 collective-permute-done.3.line_ref
  35.8 0.2 left.3
  36.0 5.5 %build.9 = (bf16[2048,1024]{1,0:T(8,128)(2,1)S(1)}, bf16[2048,1024]{1,0:T(8,128)(2,1)S(1)}, bf16[2048,1024]{1,0:T(8,128)(2,1)S(1)}, f32[12,32,256]{2,1,0:T(8,128)S(1)}) custom-call(bf16[2048,128]{1,0:T(8,128)(2,1)S(1)} %get-tuple-element.65.refs_0_.refs_1_, bf16[32,2048]{1,0:T(8,128)(2,1)S(1)} %get-tuple-element.66.refs_1_.refs_2_, ...), custom_call_target="tpu_custom_call" | custom-call | flops 6442450944 | bytes 12582912 | tf_op jit(solution)/shard_map/build/pallas_call | solution.py:166
  41.5 0.0 collective-permute-done.6.block_ref
  41.6 1.9 %build.10 = (bf16[2048,1024]{1,0:T(8,128)(2,1)S(1)}, f32[4,32,256]{2,1,0:T(8,128)S(1)}) custom-call(bf16[2048,128]{1,0:T(8,128)(2,1)S(1)} %get-tuple-element.74.refs_0_, bf16[32,2048]{1,0:T(8,128)(2,1)S(1)} %get-tuple-element.51.refs_1_, bf16[128,1024]{1,0:T(8,128)(2,1)S(1)} %right.7.refs_2_.refs_3_), custom_call_target="tpu_custom_call" | custom-call | flops 2147483648 | bytes 4194304 | tf_op jit(solution)/shard_map/build/pallas_call | solution.py:166
  43.5 0.0 copy-start
  43.5 0.0 copy-start.1
  43.5 1.9 %build.11 = (bf16[2048,1024]{1,0:T(8,128)(2,1)S(1)}, bf16[16,32,256]{2,1,0:T(8,128)(2,1)S(1)}) custom-call(s32[1]{0:T(128)} %bitcast.me_ref.refs_0_, bf16[2048,128]{1,0:T(8,128)(2,1)S(1)} %get-tuple-element.65.refs_0_.refs_1_, bf16[32,2048]{1,0:T(8,128)(2,1)S(1)} %get-tuple-element.66.refs_1_.refs_2_, bf16[128,1024]{1,0:T(8,128)(2,1)S(1)} %right.7.refs_2_.refs_3_, ...), custom_call_target="tpu_custom_call" | custom-call | flops 2147483648 | bytes 4194304 | tf_op jit(solution)/shard_map/build/pallas_call | solution.py:166
  45.4 13.9 %all_to_all.30.received_ref = bf16[16,32,256]{2,1,0:T(8,128)(2,1)S(1)} all-to-all(bf16[16,32,256]{2,1,0:T(8,128)(2,1)S(1)} %get-tuple-element.76), channel_id=1, replica_groups=mesh['yl'=2,'x'=4,'yh'=2,'z'=8,'core'=2] {'x','yh','yl'}, dimensions={0} | all-to-all | bytes 524288 | tf_op jit(solution)/shard_map/all_to_all | solution.py:367
  59.3 0.0 copy-done
  59.3 0.0 copy-done.1
  59.4 10.3 %all_to_all.31.refs_0_ = bf16[8,32,256]{2,1,0:T(8,128)(2,1)S(1)} all-to-all(bf16[8,32,256]{2,1,0:T(8,128)(2,1)S(1)} %get-tuple-element.77), channel_id=1, replica_groups=mesh['yl'=2,'x'=4,'yh'=2,'z'=8,'core'=2] {'z'}, dimensions={0} | all-to-all | bytes 262144 | tf_op jit(solution)/shard_map/all_to_all | solution.py:375
  69.7 3.0 %collective-permute-start.7 = (bf16[8,32,256]{2,1,0:T(8,128)(2,1)S(1)}, bf16[8,32,256]{2,1,0:T(8,128)(2,1)S(1)}, u32[]{:S(2)}, u32[]{:S(2)}) collective-permute-start(bf16[8,32,256]{2,1,0:T(8,128)(2,1)S(1)} %all_to_all.31.refs_0_), channel_id=1, source_target_pairs={{0,1},{1,0},{2,3},{3,2},{4,5},{5,4},{6,7},{7,6},{8,9},{9,8},{10,11... | collective-permute-start | bytes 393224 | tf_op jit(solution)/shard_map/ppermute | solution.py:302
  72.6 3.0 %apply.2.refs_6_ = f32[16,32,256]{2,1,0:T(8,128)S(1)} custom-call(bf16[8,32,256]{2,1,0:T(8,128)(2,1)S(1)} %all_to_all.31.refs_0_, bf16[2048,1024]{1,0:T(8,128)(2,1)S(1)} %get-tuple-element.82.refs_1_, bf16[2048,1024]{1,0:T(8,128)(2,1)S(1)} %get-tuple-element.83.refs_2_, bf16[2048,1024]{1,0:T(8,128)(2,1)S(1)} %get-tuple-element.84.refs_3_, ...), custom_call_target="tpu_custom_call" | custom-call | flops 4294967296 | bytes 16777216 | tf_op jit(solution)/shard_map/apply/pallas_call | solution.py:213
  75.6 0.0 collective-permute-done.7.refs_1_
  75.6 3.0 %apply.3 = bf16[16,32,256]{2,1,0:T(8,128)(2,1)S(1)} custom-call(s32[1]{0:T(128)} %bitcast.me_ref.refs_0_, bf16[8,32,256]{2,1,0:T(8,128)(2,1)S(1)} %collective-permute-done.7.refs_1_, bf16[2048,1024]{1,0:T(8,128)(2,1)S(1)} %get-tuple-element.78.refs_2_, bf16[2048,1024]{1,0:T(8,128)(2,1)S(1)} %get-tuple-element.79.refs_3_, ...), custom_call_target="tpu_custom_call" | custom-call | flops 4294967296 | bytes 16777216 | tf_op jit(solution)/shard_map/apply/pallas_call | solution.py:213
  78.5 11.0 %all_to_all.32.received_ref = bf16[16,32,256]{2,1,0:T(8,128)(2,1)S(1)} all-to-all(bf16[16,32,256]{2,1,0:T(8,128)(2,1)S(1)} %apply.3), channel_id=1, replica_groups=mesh['yl'=2,'x'=4,'yh'=2,'z'=8,'core'=2] {'x','yh','yl'}, dimensions={0} | all-to-all | bytes 524288 | tf_op jit(solution)/shard_map/all_to_all | solution.py:379
  89.5 0.2 sums.1
  89.7 8.7 %all_to_all.33.received_ref = f32[8,8,128]{2,1,0:T(8,128)S(1)} all-to-all(f32[8,8,128]{2,1,0:T(8,128)S(1)} %get-tuple-element.87), channel_id=1, replica_groups=mesh['yl'=2,'x'=4,'yh'=2,'z'=8,'core'=2] {'x','core'}, dimensions={0} | all-to-all | bytes 65536 | tf_op jit(solution)/shard_map/all_to_all | solution.py:387
  98.4 12.1 %all_to_all.34.received_ref = f32[32,8,128]{2,1,0:T(8,128)S(1)} all-to-all(f32[32,8,128]{2,1,0:T(8,128)S(1)} %spread.1), channel_id=1, replica_groups=mesh['yl'=2,'x'=4,'yh'=2,'z'=8,'core'=2] {'yh','yl','z'}, dimensions={0} | all-to-all | bytes 262144 | tf_op jit(solution)/shard_map/all_to_all | solution.py:389
  110.6 1.0 last.1
  (9 shorter events, 0.2 us)
Async XLA Ops:
  2.3 25.5 %all-to-all-start = ((bf16[8,112,256]{2,1,0:T(8,128)(2,1)}), bf16[8,112,256]{2,1,0:T(8,128)(2,1)S(1)}, u32[]{:S(2)}, u32[]{:S(2)}) async-start(bf16[8,112,256]{2,1,0:T(8,128)(2,1)} %get-tuple-element.46), calls=%async_computation | async-start | bytes 917504 | tf_op jit(solution)/shard_map/all_to_all | solution.py:319
  11.3 7.6 %collective-permute-start.2 = (bf16[1,80,256]{2,1,0:T(8,128)(2,1)}, bf16[1,80,256]{2,1,0:T(8,128)(2,1)S(1)}, u32[]{:S(2)}, u32[]{:S(2)}) collective-permute-start(bf16[1,80,256]{2,1,0:T(8,128)(2,1)} %get-tuple-element.47), channel_id=1, source_target_pairs={{0,144},{16,128},{128,16},{144,0},{1,145},{17,129},{129,17},{145,1... | collective-permute-start | bytes 122888 | tf_op jit(solution)/shard_map/ppermute | solution.py:302
  14.0 4.9 %collective-permute-start.1 = (bf16[1,80,256]{2,1,0:T(8,128)(2,1)}, bf16[1,80,256]{2,1,0:T(8,128)(2,1)S(1)}, u32[]{:S(2)}, u32[]{:S(2)}) collective-permute-start(bf16[1,80,256]{2,1,0:T(8,128)(2,1)} %get-tuple-element.47), channel_id=1, source_target_pairs={{0,16},{16,0},{128,144},{144,128},{1,17},{17,1},{129,145},{145,129... | collective-permute-start | bytes 122888 | tf_op jit(solution)/shard_map/ppermute | solution.py:302
  14.4 3.5 %collective-permute-start = (bf16[1,80,256]{2,1,0:T(8,128)(2,1)}, bf16[1,80,256]{2,1,0:T(8,128)(2,1)S(1)}, u32[]{:S(2)}, u32[]{:S(2)}) collective-permute-start(bf16[1,80,256]{2,1,0:T(8,128)(2,1)} %get-tuple-element.47), channel_id=1, source_target_pairs={{0,128},{16,144},{128,0},{144,16},{1,129},{17,145},{129,1},{145,17... | collective-permute-start | bytes 122888 | tf_op jit(solution)/shard_map/ppermute | solution.py:302
  18.9 11.5 %collective-permute-start.4 = (bf16[4,80,256]{2,1,0:T(8,128)(2,1)S(1)}, bf16[4,80,256]{2,1,0:T(8,128)(2,1)S(1)}, u32[]{:S(2)}, u32[]{:S(2)}) collective-permute-start(bf16[4,80,256]{2,1,0:T(8,128)(2,1)S(1)} %constant_dynamic-update-slice_fusion.block_ref), channel_id=1, source_target_pairs={{0,32},{32,0},{64,96},{96,64},{1,33},{33,1},{65,97},{97,65},{2,34}... | collective-permute-start | bytes 491528 | tf_op jit(solution)/shard_map/ppermute | solution.py:302
  20.2 12.1 %collective-permute-start.5 = (bf16[4,80,256]{2,1,0:T(8,128)(2,1)S(1)}, bf16[4,80,256]{2,1,0:T(8,128)(2,1)S(1)}, u32[]{:S(2)}, u32[]{:S(2)}) collective-permute-start(bf16[4,80,256]{2,1,0:T(8,128)(2,1)S(1)} %constant_dynamic-update-slice_fusion.block_ref), channel_id=1, source_target_pairs={{0,64},{32,96},{64,0},{96,32},{1,65},{33,97},{65,1},{97,33},{2,66}... | collective-permute-start | bytes 491528 | tf_op jit(solution)/shard_map/ppermute | solution.py:302
  27.8 8.1 %collective-permute-start.3 = (bf16[8,112,256]{2,1,0:T(8,128)(2,1)S(1)}, bf16[8,112,256]{2,1,0:T(8,128)(2,1)S(1)}, u32[]{:S(2)}, u32[]{:S(2)}) collective-permute-start(bf16[8,112,256]{2,1,0:T(8,128)(2,1)S(1)} %all-to-all-done.line_ref), channel_id=1, source_target_pairs={{0,1},{1,0},{2,3},{3,2},{4,5},{5,4},{6,7},{7,6},{8,9},{9,8},{10,11... | collective-permute-start | bytes 1376264 | tf_op jit(solution)/shard_map/ppermute | solution.py:302
  32.4 9.1 %collective-permute-start.6 = (bf16[4,80,256]{2,1,0:T(8,128)(2,1)S(1)}, bf16[4,80,256]{2,1,0:T(8,128)(2,1)S(1)}, u32[]{:S(2)}, u32[]{:S(2)}) collective-permute-start(bf16[4,80,256]{2,1,0:T(8,128)(2,1)S(1)} %collective-permute-done.5.block_ref), channel_id=1, source_target_pairs={{0,32},{32,0},{64,96},{96,64},{1,33},{33,1},{65,97},{97,65},{2,34}... | collective-permute-start | bytes 491528 | tf_op jit(solution)/shard_map/ppermute | solution.py:302
  43.5 15.8 %copy-start = (f32[32,256]{1,0:T(8,128)S(1)}, f32[32,256]{1,0:T(8,128)}, u32[]{:S(2)}) copy-start(f32[32,256]{1,0:T(8,128)} %start_ref.3) | copy-start | bytes 98308
  43.5 15.8 %copy-start.1 = (f32[32,256]{1,0:T(8,128)S(1)}, f32[32,256]{1,0:T(8,128)}, u32[]{:S(2)}) copy-start(f32[32,256]{1,0:T(8,128)} %targets_ref.1) | copy-start | bytes 98308
  69.7 5.9 %collective-permute-start.7 = (bf16[8,32,256]{2,1,0:T(8,128)(2,1)S(1)}, bf16[8,32,256]{2,1,0:T(8,128)(2,1)S(1)}, u32[]{:S(2)}, u32[]{:S(2)}) collective-permute-start(bf16[8,32,256]{2,1,0:T(8,128)(2,1)S(1)} %all_to_all.31.refs_0_), channel_id=1, source_target_pairs={{0,1},{1,0},{2,3},{3,2},{4,5},{5,4},{6,7},{7,6},{8,9},{9,8},{10,11... | collective-permute-start | bytes 393224 | tf_op jit(solution)/shard_map/ppermute | solution.py:302

commit v8 on v6

--- a/solution.py
+++ b/solution.py
@@ -381,12 +381,12 @@
     product, sums = small(
         sums_body,
         "sums",
-        [pltpu.VMEM((vectors, size), F32), pltpu.VMEM((8, 8, 128), F32)],
+        [pltpu.VMEM((vectors, size), F32), pltpu.VMEM((2 * planes, 8, 128), F32)],
         [received, residual0],
     )
-    sums = lax.all_to_all(sums, ('x', 'core'), 0, 0)
-    (sums,) = small(spread_body, "spread", [pltpu.VMEM((32, 8, 128), F32)], [sums])
-    sums = lax.all_to_all(sums, ('yl', 'yh', 'z'), 0, 0)
+    sums = lax.all_to_all(sums, ("yl", "x", "yh", "core"), 0, 0)
+    (sums,) = small(spread_body, "spread", [pltpu.VMEM((lines, 8, 128), F32)], [sums])
+    sums = lax.all_to_all(sums, LINE, 0, 0)
     return tuple(
         small(
             last_body,

time: 112 us -> 113 us (level)
  no operation moved by 1% of the time
where the time goes in v8:
time: 113 us
  blocking collectives  57.2 us (51%)
  Pallas kernels  24.3 us (22%)
  starting transfers between devices  21.8 us (19%)
  waiting for transfers between devices  7.75 us (7%)
    all_to_all x2, blocking collectives, per_device(): received = lax.all_to_all(partial_value, PLANE, 0, 0)  25.4 us
    pallas_call x6, Pallas kernels, build(): pl.pallas_call(functools.partial(build_body, scale, groups=len(rights), l...  15 us
    ppermute x8, starting transfers between devices, across(): return lax.ppermute(value, axis, [(n, n ^ step) for n in range(count)])  12.8 us
    all_to_all x1, blocking collectives, per_device(): sums = lax.all_to_all(sums, ('yl', 'x', 'yh', 'core'), 0, 0)  12.3 us
    all_to_all x1, blocking collectives, per_device(): vector = lax.all_to_all(vector, LINE, 0, 0)  10.3 us
    all_to_all x1, blocking collectives, per_device(): sums = lax.all_to_all(sums, LINE, 0, 0)  9.24 us
    all_to_all x1, starting transfers between devices, per_device(): line = lax.all_to_all(line, LINE, 0, 0)  9.03 us
    pallas_call x2, Pallas kernels, apply(): pl.pallas_call(functools.partial(apply_body, tiles=len(tiles), last=last)...  5.92 us
  transfers between devices with their start and end apart: 9, of which 2 were waited for; matrix products, arithmetic and copies ran while one was open for 1% of the time, Pallas kernels for 13%

profile of v8, /device:TPU:1, one launch (start us, length us, event | category | flops | bytes accessed | tf_op | source)
XLA Modules:
  0.0 112.6 jit_solution(8061002167004291010)
XLA Ops:
  0.6 1.6 %pack.1 = (bf16[1,80,256]{2,1,0:T(8,128)(2,1)}, bf16[8,112,256]{2,1,0:T(8,128)(2,1)}) custom-call(bf16[64,256]{1,0:T(8,128)(2,1)} %features_hbm.1, s32[1,256]{1,0:T(1,128)} %bitcast.2, f32[32,256]{1,0:T(8,128)} %start_ref.3), custom_call_target="tpu_custom_call" | custom-call | tf_op jit(solution)/shard_map/pack/pallas_call | solution.py:304
  2.3 9.0 %all-to-all-start = ((bf16[8,112,256]{2,1,0:T(8,128)(2,1)}), bf16[8,112,256]{2,1,0:T(8,128)(2,1)S(1)}, u32[]{:S(2)}, u32[]{:S(2)}) async-start(bf16[8,112,256]{2,1,0:T(8,128)(2,1)} %get-tuple-element.46), calls=%async_computation | async-start | bytes 917504 | tf_op jit(solution)/shard_map/all_to_all | solution.py:319
  11.3 2.7 %collective-permute-start.2 = (bf16[1,80,256]{2,1,0:T(8,128)(2,1)}, bf16[1,80,256]{2,1,0:T(8,128)(2,1)S(1)}, u32[]{:S(2)}, u32[]{:S(2)}) collective-permute-start(bf16[1,80,256]{2,1,0:T(8,128)(2,1)} %get-tuple-element.47), channel_id=1, source_target_pairs={{0,144},{16,128},{128,16},{144,0},{1,145},{17,129},{129,17},{145,1... | collective-permute-start | bytes 122888 | tf_op jit(solution)/shard_map/ppermute | solution.py:302
  14.0 0.0 collective-permute-start.1
  14.0 1.3 %collective-permute-start = (bf16[1,80,256]{2,1,0:T(8,128)(2,1)}, bf16[1,80,256]{2,1,0:T(8,128)(2,1)S(1)}, u32[]{:S(2)}, u32[]{:S(2)}) collective-permute-start(bf16[1,80,256]{2,1,0:T(8,128)(2,1)} %get-tuple-element.47), channel_id=1, source_target_pairs={{0,16},{16,0},{128,144},{144,128},{1,17},{17,1},{129,145},{145,129... | collective-permute-start | bytes 122888 | tf_op jit(solution)/shard_map/ppermute | solution.py:302
  15.3 0.8 constant_dynamic-update-slice_fusion.3
  16.1 3.1 %collective-permute-done = bf16[1,80,256]{2,1,0:T(8,128)(2,1)S(1)} collective-permute-done((bf16[1,80,256]{2,1,0:T(8,128)(2,1)}, bf16[1,80,256]{2,1,0:T(8,128)(2,1)S(1)}, u32[]{:S(2)}, u32[]{:S(2)}) %collective-permute-start) | collective-permute-done | bytes 40992 | tf_op jit(solution)/shard_map/ppermute | solution.py:302
  19.2 0.0 collective-permute-done.1
  19.2 0.0 collective-permute-done.2
  19.2 1.3 %collective-permute-start.4 = (bf16[4,80,256]{2,1,0:T(8,128)(2,1)S(1)}, bf16[4,80,256]{2,1,0:T(8,128)(2,1)S(1)}, u32[]{:S(2)}, u32[]{:S(2)}) collective-permute-start(bf16[4,80,256]{2,1,0:T(8,128)(2,1)S(1)} %constant_dynamic-update-slice_fusion.block_ref), channel_id=1, source_target_pairs={{0,32},{32,0},{64,96},{96,64},{1,33},{33,1},{65,97},{97,65},{2,34}... | collective-permute-start | bytes 491528 | tf_op jit(solution)/shard_map/ppermute | solution.py:302
  20.6 2.5 %collective-permute-start.5 = (bf16[4,80,256]{2,1,0:T(8,128)(2,1)S(1)}, bf16[4,80,256]{2,1,0:T(8,128)(2,1)S(1)}, u32[]{:S(2)}, u32[]{:S(2)}) collective-permute-start(bf16[4,80,256]{2,1,0:T(8,128)(2,1)S(1)} %constant_dynamic-update-slice_fusion.block_ref), channel_id=1, source_target_pairs={{0,64},{32,96},{64,0},{96,32},{1,65},{33,97},{65,1},{97,33},{2,66}... | collective-permute-start | bytes 491528 | tf_op jit(solution)/shard_map/ppermute | solution.py:302
  23.1 4.7 %all-to-all-done.line_ref = bf16[8,112,256]{2,1,0:T(8,128)(2,1)S(1)} async-done(((bf16[8,112,256]{2,1,0:T(8,128)(2,1)}), bf16[8,112,256]{2,1,0:T(8,128)(2,1)S(1)}, u32[]{:S(2)}, u32[]{:S(2)}) %all-to-all-start) | async-done | bytes 458784 | tf_op jit(solution)/shard_map/all_to_all | solution.py:319
  27.8 0.6 collective-permute-start.3
  28.3 0.2 left.2
  28.5 1.9 %build.6 = (bf16[2048,1024]{1,0:T(8,128)(2,1)S(1)}, f32[4,32,256]{2,1,0:T(8,128)S(1)}) custom-call(bf16[2048,128]{1,0:T(8,128)(2,1)S(1)} %get-tuple-element.74.refs_0_, bf16[32,2048]{1,0:T(8,128)(2,1)S(1)} %get-tuple-element.51.refs_1_, bf16[128,1024]{1,0:T(8,128)(2,1)S(1)} %right.4.refs_2_), custom_call_target="tpu_custom_call" | custom-call | flops 2147483648 | bytes 4194304 | tf_op jit(solution)/shard_map/build/pallas_call | solution.py:166
  30.4 0.0 collective-permute-done.4.block_ref
  30.5 1.9 %build.7 = (bf16[2048,1024]{1,0:T(8,128)(2,1)S(1)}, f32[4,32,256]{2,1,0:T(8,128)S(1)}) custom-call(bf16[2048,128]{1,0:T(8,128)(2,1)S(1)} %get-tuple-element.74.refs_0_, bf16[32,2048]{1,0:T(8,128)(2,1)S(1)} %get-tuple-element.51.refs_1_, bf16[128,1024]{1,0:T(8,128)(2,1)S(1)} %right.5.refs_2_.refs_3_), custom_call_target="tpu_custom_call" | custom-call | flops 2147483648 | bytes 4194304 | tf_op jit(solution)/shard_map/build/pallas_call | solution.py:166
  32.4 0.0 collective-permute-done.5.block_ref
  32.4 1.5 %collective-permute-start.6 = (bf16[4,80,256]{2,1,0:T(8,128)(2,1)S(1)}, bf16[4,80,256]{2,1,0:T(8,128)(2,1)S(1)}, u32[]{:S(2)}, u32[]{:S(2)}) collective-permute-start(bf16[4,80,256]{2,1,0:T(8,128)(2,1)S(1)} %collective-permute-done.5.block_ref), channel_id=1, source_target_pairs={{0,32},{32,0},{64,96},{96,64},{1,33},{33,1},{65,97},{97,65},{2,34}... | collective-permute-start | bytes 491528 | tf_op jit(solution)/shard_map/ppermute | solution.py:302
  33.9 1.9 %build.8 = (bf16[2048,1024]{1,0:T(8,128)(2,1)S(1)}, f32[4,32,256]{2,1,0:T(8,128)S(1)}) custom-call(bf16[2048,128]{1,0:T(8,128)(2,1)S(1)} %get-tuple-element.74.refs_0_, bf16[32,2048]{1,0:T(8,128)(2,1)S(1)} %get-tuple-element.51.refs_1_, bf16[128,1024]{1,0:T(8,128)(2,1)S(1)} %right.6.refs_2_.refs_4_), custom_call_target="tpu_custom_call" | custom-call | flops 2147483648 | bytes 4194304 | tf_op jit(solution)/shard_map/build/pallas_call | solution.py:166
  35.8 0.0 collective-permute-done.3.line_ref
  35.8 0.2 left.3
  36.0 5.5 %build.9 = (bf16[2048,1024]{1,0:T(8,128)(2,1)S(1)}, bf16[2048,1024]{1,0:T(8,128)(2,1)S(1)}, bf16[2048,1024]{1,0:T(8,128)(2,1)S(1)}, f32[12,32,256]{2,1,0:T(8,128)S(1)}) custom-call(bf16[2048,128]{1,0:T(8,128)(2,1)S(1)} %get-tuple-element.65.refs_0_.refs_1_, bf16[32,2048]{1,0:T(8,128)(2,1)S(1)} %get-tuple-element.66.refs_1_.refs_2_, ...), custom_call_target="tpu_custom_call" | custom-call | flops 6442450944 | bytes 12582912 | tf_op jit(solution)/shard_map/build/pallas_call | solution.py:166
  41.5 0.0 collective-permute-done.6.block_ref
  41.6 1.9 %build.10 = (bf16[2048,1024]{1,0:T(8,128)(2,1)S(1)}, f32[4,32,256]{2,1,0:T(8,128)S(1)}) custom-call(bf16[2048,128]{1,0:T(8,128)(2,1)S(1)} %get-tuple-element.74.refs_0_, bf16[32,2048]{1,0:T(8,128)(2,1)S(1)} %get-tuple-element.51.refs_1_, bf16[128,1024]{1,0:T(8,128)(2,1)S(1)} %right.7.refs_2_.refs_3_), custom_call_target="tpu_custom_call" | custom-call | flops 2147483648 | bytes 4194304 | tf_op jit(solution)/shard_map/build/pallas_call | solution.py:166
  43.5 0.0 copy-start
  43.5 0.0 copy-start.1
  43.5 1.9 %build.11 = (bf16[2048,1024]{1,0:T(8,128)(2,1)S(1)}, bf16[16,32,256]{2,1,0:T(8,128)(2,1)S(1)}) custom-call(s32[1]{0:T(128)} %bitcast.me_ref.refs_0_, bf16[2048,128]{1,0:T(8,128)(2,1)S(1)} %get-tuple-element.65.refs_0_.refs_1_, bf16[32,2048]{1,0:T(8,128)(2,1)S(1)} %get-tuple-element.66.refs_1_.refs_2_, bf16[128,1024]{1,0:T(8,128)(2,1)S(1)} %right.7.refs_2_.refs_3_, ...), custom_call_target="tpu_custom_call" | custom-call | flops 2147483648 | bytes 4194304 | tf_op jit(solution)/shard_map/build/pallas_call | solution.py:166
  45.4 14.3 %all_to_all.30.received_ref = bf16[16,32,256]{2,1,0:T(8,128)(2,1)S(1)} all-to-all(bf16[16,32,256]{2,1,0:T(8,128)(2,1)S(1)} %get-tuple-element.76), channel_id=1, replica_groups=mesh['yl'=2,'x'=4,'yh'=2,'z'=8,'core'=2] {'x','yl','yh'}, dimensions={0} | all-to-all | bytes 524288 | tf_op jit(solution)/shard_map/all_to_all | solution.py:367
  59.7 0.0 copy-done
  59.7 0.0 copy-done.1
  59.8 10.3 %all_to_all.31.refs_0_ = bf16[8,32,256]{2,1,0:T(8,128)(2,1)S(1)} all-to-all(bf16[8,32,256]{2,1,0:T(8,128)(2,1)S(1)} %get-tuple-element.77), channel_id=1, replica_groups=mesh['yl'=2,'x'=4,'yh'=2,'z'=8,'core'=2] {'z'}, dimensions={0} | all-to-all | bytes 262144 | tf_op jit(solution)/shard_map/all_to_all | solution.py:375
  70.1 2.8 %collective-permute-start.7 = (bf16[8,32,256]{2,1,0:T(8,128)(2,1)S(1)}, bf16[8,32,256]{2,1,0:T(8,128)(2,1)S(1)}, u32[]{:S(2)}, u32[]{:S(2)}) collective-permute-start(bf16[8,32,256]{2,1,0:T(8,128)(2,1)S(1)} %all_to_all.31.refs_0_), channel_id=1, source_target_pairs={{0,1},{1,0},{2,3},{3,2},{4,5},{5,4},{6,7},{7,6},{8,9},{9,8},{10,11... | collective-permute-start | bytes 393224 | tf_op jit(solution)/shard_map/ppermute | solution.py:302
  72.9 2.9 %apply.2.refs_6_ = f32[16,32,256]{2,1,0:T(8,128)S(1)} custom-call(bf16[8,32,256]{2,1,0:T(8,128)(2,1)S(1)} %all_to_all.31.refs_0_, bf16[2048,1024]{1,0:T(8,128)(2,1)S(1)} %get-tuple-element.82.refs_1_, bf16[2048,1024]{1,0:T(8,128)(2,1)S(1)} %get-tuple-element.83.refs_2_, bf16[2048,1024]{1,0:T(8,128)(2,1)S(1)} %get-tuple-element.84.refs_3_, ...), custom_call_target="tpu_custom_call" | custom-call | flops 4294967296 | bytes 16777216 | tf_op jit(solution)/shard_map/apply/pallas_call | solution.py:213
  75.9 0.0 collective-permute-done.7.refs_1_
  75.9 3.0 %apply.3 = bf16[16,32,256]{2,1,0:T(8,128)(2,1)S(1)} custom-call(s32[1]{0:T(128)} %bitcast.me_ref.refs_0_, bf16[8,32,256]{2,1,0:T(8,128)(2,1)S(1)} %collective-permute-done.7.refs_1_, bf16[2048,1024]{1,0:T(8,128)(2,1)S(1)} %get-tuple-element.78.refs_2_, bf16[2048,1024]{1,0:T(8,128)(2,1)S(1)} %get-tuple-element.79.refs_3_, ...), custom_call_target="tpu_custom_call" | custom-call | flops 4294967296 | bytes 16777216 | tf_op jit(solution)/shard_map/apply/pallas_call | solution.py:213
  78.8 11.0 %all_to_all.32.received_ref = bf16[16,32,256]{2,1,0:T(8,128)(2,1)S(1)} all-to-all(bf16[16,32,256]{2,1,0:T(8,128)(2,1)S(1)} %apply.3), channel_id=1, replica_groups=mesh['yl'=2,'x'=4,'yh'=2,'z'=8,'core'=2] {'x','yl','yh'}, dimensions={0} | all-to-all | bytes 524288 | tf_op jit(solution)/shard_map/all_to_all | solution.py:379
  89.9 0.2 sums.1
  90.1 12.3 %all_to_all.33.received_ref = f32[32,8,128]{2,1,0:T(8,128)S(1)} all-to-all(f32[32,8,128]{2,1,0:T(8,128)S(1)} %get-tuple-element.87), channel_id=1, replica_groups=mesh['yl'=2,'x'=4,'yh'=2,'z'=8,'core'=2] {'yl','x','yh','core'}, dimensions={0} | all-to-all | bytes 262144 | tf_op jit(solution)/shard_map/all_to_all | solution.py:387
  102.4 9.2 %all_to_all.34.received_ref = f32[8,8,128]{2,1,0:T(8,128)S(1)} all-to-all(f32[8,8,128]{2,1,0:T(8,128)S(1)} %spread.1), channel_id=1, replica_groups=mesh['yl'=2,'x'=4,'yh'=2,'z'=8,'core'=2] {'z'}, dimensions={0} | all-to-all | bytes 65536 | tf_op jit(solution)/shard_map/all_to_all | solution.py:389
  111.6 1.0 last.1
  (9 shorter events, 0.2 us)
Async XLA Ops:
  2.3 25.5 %all-to-all-start = ((bf16[8,112,256]{2,1,0:T(8,128)(2,1)}), bf16[8,112,256]{2,1,0:T(8,128)(2,1)S(1)}, u32[]{:S(2)}, u32[]{:S(2)}) async-start(bf16[8,112,256]{2,1,0:T(8,128)(2,1)} %get-tuple-element.46), calls=%async_computation | async-start | bytes 917504 | tf_op jit(solution)/shard_map/all_to_all | solution.py:319
  11.3 7.9 %collective-permute-start.2 = (bf16[1,80,256]{2,1,0:T(8,128)(2,1)}, bf16[1,80,256]{2,1,0:T(8,128)(2,1)S(1)}, u32[]{:S(2)}, u32[]{:S(2)}) collective-permute-start(bf16[1,80,256]{2,1,0:T(8,128)(2,1)} %get-tuple-element.47), channel_id=1, source_target_pairs={{0,144},{16,128},{128,16},{144,0},{1,145},{17,129},{129,17},{145,1... | collective-permute-start | bytes 122888 | tf_op jit(solution)/shard_map/ppermute | solution.py:302
  14.0 5.2 %collective-permute-start.1 = (bf16[1,80,256]{2,1,0:T(8,128)(2,1)}, bf16[1,80,256]{2,1,0:T(8,128)(2,1)S(1)}, u32[]{:S(2)}, u32[]{:S(2)}) collective-permute-start(bf16[1,80,256]{2,1,0:T(8,128)(2,1)} %get-tuple-element.47), channel_id=1, source_target_pairs={{0,128},{16,144},{128,0},{144,16},{1,129},{17,145},{129,1},{145,17... | collective-permute-start | bytes 122888 | tf_op jit(solution)/shard_map/ppermute | solution.py:302
  14.0 5.1 %collective-permute-start = (bf16[1,80,256]{2,1,0:T(8,128)(2,1)}, bf16[1,80,256]{2,1,0:T(8,128)(2,1)S(1)}, u32[]{:S(2)}, u32[]{:S(2)}) collective-permute-start(bf16[1,80,256]{2,1,0:T(8,128)(2,1)} %get-tuple-element.47), channel_id=1, source_target_pairs={{0,16},{16,0},{128,144},{144,128},{1,17},{17,1},{129,145},{145,129... | collective-permute-start | bytes 122888 | tf_op jit(solution)/shard_map/ppermute | solution.py:302
  19.2 11.2 %collective-permute-start.4 = (bf16[4,80,256]{2,1,0:T(8,128)(2,1)S(1)}, bf16[4,80,256]{2,1,0:T(8,128)(2,1)S(1)}, u32[]{:S(2)}, u32[]{:S(2)}) collective-permute-start(bf16[4,80,256]{2,1,0:T(8,128)(2,1)S(1)} %constant_dynamic-update-slice_fusion.block_ref), channel_id=1, source_target_pairs={{0,32},{32,0},{64,96},{96,64},{1,33},{33,1},{65,97},{97,65},{2,34}... | collective-permute-start | bytes 491528 | tf_op jit(solution)/shard_map/ppermute | solution.py:302
  20.6 11.8 %collective-permute-start.5 = (bf16[4,80,256]{2,1,0:T(8,128)(2,1)S(1)}, bf16[4,80,256]{2,1,0:T(8,128)(2,1)S(1)}, u32[]{:S(2)}, u32[]{:S(2)}) collective-permute-start(bf16[4,80,256]{2,1,0:T(8,128)(2,1)S(1)} %constant_dynamic-update-slice_fusion.block_ref), channel_id=1, source_target_pairs={{0,64},{32,96},{64,0},{96,32},{1,65},{33,97},{65,1},{97,33},{2,66}... | collective-permute-start | bytes 491528 | tf_op jit(solution)/shard_map/ppermute | solution.py:302
  27.8 8.1 %collective-permute-start.3 = (bf16[8,112,256]{2,1,0:T(8,128)(2,1)S(1)}, bf16[8,112,256]{2,1,0:T(8,128)(2,1)S(1)}, u32[]{:S(2)}, u32[]{:S(2)}) collective-permute-start(bf16[8,112,256]{2,1,0:T(8,128)(2,1)S(1)} %all-to-all-done.line_ref), channel_id=1, source_target_pairs={{0,1},{1,0},{2,3},{3,2},{4,5},{5,4},{6,7},{7,6},{8,9},{9,8},{10,11... | collective-permute-start | bytes 1376264 | tf_op jit(solution)/shard_map/ppermute | solution.py:302
  32.4 9.1 %collective-permute-start.6 = (bf16[4,80,256]{2,1,0:T(8,128)(2,1)S(1)}, bf16[4,80,256]{2,1,0:T(8,128)(2,1)S(1)}, u32[]{:S(2)}, u32[]{:S(2)}) collective-permute-start(bf16[4,80,256]{2,1,0:T(8,128)(2,1)S(1)} %collective-permute-done.5.block_ref), channel_id=1, source_target_pairs={{0,32},{32,0},{64,96},{96,64},{1,33},{33,1},{65,97},{97,65},{2,34}... | collective-permute-start | bytes 491528 | tf_op jit(solution)/shard_map/ppermute | solution.py:302
  43.5 16.2 %copy-start = (f32[32,256]{1,0:T(8,128)S(1)}, f32[32,256]{1,0:T(8,128)}, u32[]{:S(2)}) copy-start(f32[32,256]{1,0:T(8,128)} %start_ref.3) | copy-start | bytes 98308
  43.5 16.2 %copy-start.1 = (f32[32,256]{1,0:T(8,128)S(1)}, f32[32,256]{1,0:T(8,128)}, u32[]{:S(2)}) copy-start(f32[32,256]{1,0:T(8,128)} %targets_ref.1) | copy-start | bytes 98308
  70.1 5.8 %collective-permute-start.7 = (bf16[8,32,256]{2,1,0:T(8,128)(2,1)S(1)}, bf16[8,32,256]{2,1,0:T(8,128)(2,1)S(1)}, u32[]{:S(2)}, u32[]{:S(2)}) collective-permute-start(bf16[8,32,256]{2,1,0:T(8,128)(2,1)S(1)} %all_to_all.31.refs_0_), channel_id=1, source_target_pairs={{0,1},{1,0},{2,3},{3,2},{4,5},{5,4},{6,7},{7,6},{8,9},{9,8},{10,11... | collective-permute-start | bytes 393224 | tf_op jit(solution)/shard_map/ppermute | solution.py:302
